TPU v7x, 512 devices: a whole 4x8x8 slice. The times are simulated.
512 devices in a mesh: ctx: 64 (over z, y), kvh: 8 (over x, core).
Axes of the slice: x: 4, y: 8, z: 8, core: 2. Of those that a mesh axis runs over, the one named last changes fastest.
Arguments:
- queries: bfloat16 [1024, 128, 128], P(('ctx', 'kvh')), may hold values from -6 to 6
- new_keys: bfloat16 [1024, 8, 128], P('ctx', 'kvh'), may hold values from -6 to 6
- new_values: bfloat16 [1024, 8, 128], P('ctx', 'kvh'), may hold values from -6 to 6
- new_positions: int32 [1024], P('ctx'), may hold values from 0 to 1023, each once
- hist_keys: bfloat16 [192, 128, 8, 128], P('ctx', None, 'kvh'), may hold values from -6 to 6
- hist_values: bfloat16 [192, 128, 8, 128], P('ctx', None, 'kvh'), may hold values from -6 to 6
- page_slots: int32 [128], replicated, may hold values from 0 to 191, as said below
Outputs:
- attention: bfloat16 [1024, 128, 128], P(('ctx', 'kvh'))
Inputs may be any that keep to these rules, and one draw needn't show every extreme that they name: `page_slots`: entry p equals 3 * d + s: history page p is held in slot s of index d of ctx. Page p belongs to index p // 2, and d is that index or the one 64 // 2 away; an index holds at most one page that belongs to that other index and at most 3 pages in all; no slot holds two pages; slots that hold no page carry data that is not part of the history.
All inputs are finite; a program needn't handle non-finite values.
Results may differ from a plain program's by a relative error of at most 0.01.
Values may be sent and summed in bfloat16 or wider, within the bound.
No kernel may reach another device: no remote copies, remote signals or barrier semaphores. Data moves between devices by JAX's collectives and lax.ppermute only.
A program may use at most 64 MiB of HBM per device.

v0:
```python
import math

import jax
import jax.numpy as jnp
from jax import lax
from jax.sharding import PartitionSpec as P


def passed_along(block, axis, distance):
    devices = range(lax.axis_size(axis))
    route = [((i - distance) % len(devices), i) for i in devices]
    return lax.ppermute(block, axis, route)


def attend(running, kv_block, visible, grouped, scale):
    row_top, row_total, weighted = running
    scores = (
        jnp.einsum("tgqd,kgd->tgqk", grouped, kv_block[0], preferred_element_type=jnp.float32)
        * scale
    )
    masked_in = visible[:, None, None, :]
    scores = jnp.where(masked_in, scores, -1e30)
    new_top = jnp.maximum(row_top, jnp.max(scores, axis=-1))
    factor = jnp.exp(row_top - new_top)
    weights = jnp.where(masked_in, jnp.exp(scores - new_top[..., None]), 0.0)
    row_total = row_total * factor + jnp.sum(weights, axis=-1)
    rounded = weights.astype(jnp.bfloat16)
    update = jnp.einsum("tgqk,kgd->tgqd", rounded, kv_block[1], preferred_element_type=jnp.float32)
    weighted = weighted * factor[..., None] + update
    return (new_top, row_total, weighted)


def body(queries, new_keys, new_values, new_positions, hist_keys, hist_values, page_slots):
    cycle_size = lax.axis_size("ctx")
    own_index = lax.axis_index("ctx")
    local_queries = lax.all_to_all(queries, "kvh", split_axis=1, concat_axis=0, tiled=True)
    tokens_here, heads_here, width = local_queries.shape
    kv_groups = new_keys.shape[1]
    per_group = heads_here // kv_groups
    grouped = local_queries.reshape(tokens_here, kv_groups, per_group, width)
    scale = 1.0 / math.sqrt(width)
    all_positions = lax.all_gather(new_positions, "ctx", axis=0, tiled=True)
    slots_dev = hist_keys.shape[0]
    page_len = hist_keys.shape[1]
    slot_pool = jnp.stack([hist_keys, hist_values])
    fresh_kv = jnp.stack([new_keys, new_values])
    kv_block = slot_pool.reshape(2, slots_dev * page_len, kv_groups, width)
    slot_ids = jnp.arange(cycle_size * slots_dev, dtype=jnp.int32)
    live_slots = jnp.any(page_slots[None, :] == slot_ids[:, None], axis=1)

    def history_seen(source):
        live = lax.dynamic_slice_in_dim(live_slots, source * slots_dev, slots_dev)
        return jnp.repeat(live, page_len)

    history_len = kv_block.shape[1]
    running = (
        jnp.full((tokens_here, kv_groups, per_group), -1e30, jnp.float32),
        jnp.zeros((tokens_here, kv_groups, per_group), jnp.float32),
        jnp.zeros((tokens_here, kv_groups, per_group, width), jnp.float32),
    )
    carried = jnp.concatenate([kv_block, fresh_kv], axis=1)

    def visible_for(source):
        key_positions = lax.dynamic_slice_in_dim(all_positions, source * tokens_here, tokens_here)
        fresh_seen = key_positions[None, :] <= new_positions[:, None]
        seen_history = jnp.broadcast_to(history_seen(source)[None, :], (tokens_here, history_len))
        return jnp.concatenate([seen_history, fresh_seen], axis=1)

    running = attend(running, carried, visible_for(own_index), grouped, scale)

    def advance(step_index, loop_state):
        inner, moving = loop_state
        moving = passed_along(moving, "ctx", 1)
        source = (own_index - step_index) % cycle_size
        inner = attend(inner, moving, visible_for(source), grouped, scale)
        return (inner, moving)

    running, carried = lax.fori_loop(1, cycle_size, advance, (running, carried))
    row_top, row_total, weighted = running
    result = (weighted / row_total[..., None]).astype(jnp.bfloat16)
    result = result.reshape(tokens_here, heads_here, width)
    return lax.all_to_all(result, "kvh", split_axis=0, concat_axis=1, tiled=True)


def solution(mesh):
    in_specs = (
        P(("ctx", "kvh"), None, None),
        P("ctx", "kvh", None),
        P("ctx", "kvh", None),
        P("ctx"),
        P("ctx", None, "kvh", None),
        P("ctx", None, "kvh", None),
        P(),
    )
    out_specs = P(("ctx", "kvh"), None, None)
    return jax.shard_map(body, mesh=mesh, in_specs=in_specs, out_specs=out_specs, check_vma=False)
```

profile of v0, /device:TPU:1, one launch (start us, length us, event | category | flops | bytes accessed | tf_op | source)
XLA Modules:
  0.0 833.6 jit_solution(9844255314357360828)
XLA Ops:
  1.6 10.3 %all-to-all-start = ((bf16[2,128,128]{2,0,1:T(2,128)(2,1)}), bf16[2,128,128]{2,0,1:T(2,128)(2,1)S(1)}, u32[]{:S(2)}, u32[]{:S(2)}) async-start(bf16[2,128,128]{2,0,1:T(2,128)(2,1)} %copy.13), calls=%async_computation | async-start | bytes 131072 | tf_op jit(solution)/shard_map/all_to_all | solution.py:36
  13.9 22.2 %all-reduce = s32[1024]{0:T(1024)S(1)} all-reduce(s32[1024]{0:T(1024)S(1)} %dynamic-update-slice), channel_id=1, replica_groups=mesh['ctx'=64,'kvh'=8] {'ctx'}, use_global_device_ids=true, to_apply=%add | all-reduce | flops 1024 | bytes 8192
  38.2 710.7 %while.21 = (s32[]{:T(128)}, f32[16,1,16]{2,0,1:T(8,128)S(1)}, f32[16,1,16]{2,0,1:T(8,128)S(1)}, f32[16,1,16,128]{3,2,0,1:T(8,128)S(1)}, bf16[2,400,1,128]{3,1,2...) while((s32[]{:T(128)}, f32[16,1,16]{2,0,1:T(8,128)S(1)}, ...), condition=%wide.region_6.7_spmd, body=%wide.region_3.6_spmd.sunk | while | flops 53423380 | bytes 3167452 | solution.py:78
  51.3 7.5 collective-permute-done
  62.1 7.5 collective-permute-done
  72.9 7.5 collective-permute-done
  83.7 8.1 collective-permute-done
  95.0 9.2 %collective-permute-done = bf16[2,400,1,128]{3,1,2,0:T(8,128)(2,1)S(1)} collective-permute-done((bf16[2,400,1,128]{3,1,2,0:T(8,128)(2,1)S(1)}, bf16[2,400,1,128]{3,1,2,0:T(8,128)(2,1)S(1)}, u32[]{:S(2)}, u32[]{:S(2)}) %collective-permute-start) | collective-permute-done | bytes 204832 | tf_op jit(solution)/shard_map/while/body/eval_jaxpr/ppermute | solution.py:12
  107.4 9.4 %collective-permute-done = bf16[2,400,1,128]{3,1,2,0:T(8,128)(2,1)S(1)} collective-permute-done((bf16[2,400,1,128]{3,1,2,0:T(8,128)(2,1)S(1)}, bf16[2,400,1,128]{3,1,2,0:T(8,128)(2,1)S(1)}, u32[]{:S(2)}, u32[]{:S(2)}) %collective-permute-start) | collective-permute-done | bytes 204832 | tf_op jit(solution)/shard_map/while/body/eval_jaxpr/ppermute | solution.py:12
  120.1 8.5 %collective-permute-done = bf16[2,400,1,128]{3,1,2,0:T(8,128)(2,1)S(1)} collective-permute-done((bf16[2,400,1,128]{3,1,2,0:T(8,128)(2,1)S(1)}, bf16[2,400,1,128]{3,1,2,0:T(8,128)(2,1)S(1)}, u32[]{:S(2)}, u32[]{:S(2)}) %collective-permute-start) | collective-permute-done | bytes 204832 | tf_op jit(solution)/shard_map/while/body/eval_jaxpr/ppermute | solution.py:12
  131.8 7.5 collective-permute-done
  207.3 8.2 collective-permute-done
  218.7 9.3 %collective-permute-done = bf16[2,400,1,128]{3,1,2,0:T(8,128)(2,1)S(1)} collective-permute-done((bf16[2,400,1,128]{3,1,2,0:T(8,128)(2,1)S(1)}, bf16[2,400,1,128]{3,1,2,0:T(8,128)(2,1)S(1)}, u32[]{:S(2)}, u32[]{:S(2)}) %collective-permute-start) | collective-permute-done | bytes 204832 | tf_op jit(solution)/shard_map/while/body/eval_jaxpr/ppermute | solution.py:12
  231.2 9.3 %collective-permute-done = bf16[2,400,1,128]{3,1,2,0:T(8,128)(2,1)S(1)} collective-permute-done((bf16[2,400,1,128]{3,1,2,0:T(8,128)(2,1)S(1)}, bf16[2,400,1,128]{3,1,2,0:T(8,128)(2,1)S(1)}, u32[]{:S(2)}, u32[]{:S(2)}) %collective-permute-start) | collective-permute-done | bytes 204832 | tf_op jit(solution)/shard_map/while/body/eval_jaxpr/ppermute | solution.py:12
  243.8 8.4 %collective-permute-done = bf16[2,400,1,128]{3,1,2,0:T(8,128)(2,1)S(1)} collective-permute-done((bf16[2,400,1,128]{3,1,2,0:T(8,128)(2,1)S(1)}, bf16[2,400,1,128]{3,1,2,0:T(8,128)(2,1)S(1)}, u32[]{:S(2)}, u32[]{:S(2)}) %collective-permute-start) | collective-permute-done | bytes 204832 | tf_op jit(solution)/shard_map/while/body/eval_jaxpr/ppermute | solution.py:12
  330.8 8.4 %collective-permute-done = bf16[2,400,1,128]{3,1,2,0:T(8,128)(2,1)S(1)} collective-permute-done((bf16[2,400,1,128]{3,1,2,0:T(8,128)(2,1)S(1)}, bf16[2,400,1,128]{3,1,2,0:T(8,128)(2,1)S(1)}, u32[]{:S(2)}, u32[]{:S(2)}) %collective-permute-start) | collective-permute-done | bytes 204832 | tf_op jit(solution)/shard_map/while/body/eval_jaxpr/ppermute | solution.py:12
  342.4 9.5 %collective-permute-done = bf16[2,400,1,128]{3,1,2,0:T(8,128)(2,1)S(1)} collective-permute-done((bf16[2,400,1,128]{3,1,2,0:T(8,128)(2,1)S(1)}, bf16[2,400,1,128]{3,1,2,0:T(8,128)(2,1)S(1)}, u32[]{:S(2)}, u32[]{:S(2)}) %collective-permute-start) | collective-permute-done | bytes 204832 | tf_op jit(solution)/shard_map/while/body/eval_jaxpr/ppermute | solution.py:12
  355.2 9.2 %collective-permute-done = bf16[2,400,1,128]{3,1,2,0:T(8,128)(2,1)S(1)} collective-permute-done((bf16[2,400,1,128]{3,1,2,0:T(8,128)(2,1)S(1)}, bf16[2,400,1,128]{3,1,2,0:T(8,128)(2,1)S(1)}, u32[]{:S(2)}, u32[]{:S(2)}) %collective-permute-start) | collective-permute-done | bytes 204832 | tf_op jit(solution)/shard_map/while/body/eval_jaxpr/ppermute | solution.py:12
  367.6 8.3 collective-permute-done
  454.6 8.5 %collective-permute-done = bf16[2,400,1,128]{3,1,2,0:T(8,128)(2,1)S(1)} collective-permute-done((bf16[2,400,1,128]{3,1,2,0:T(8,128)(2,1)S(1)}, bf16[2,400,1,128]{3,1,2,0:T(8,128)(2,1)S(1)}, u32[]{:S(2)}, u32[]{:S(2)}) %collective-permute-start) | collective-permute-done | bytes 204832 | tf_op jit(solution)/shard_map/while/body/eval_jaxpr/ppermute | solution.py:12
  466.3 9.7 %collective-permute-done = bf16[2,400,1,128]{3,1,2,0:T(8,128)(2,1)S(1)} collective-permute-done((bf16[2,400,1,128]{3,1,2,0:T(8,128)(2,1)S(1)}, bf16[2,400,1,128]{3,1,2,0:T(8,128)(2,1)S(1)}, u32[]{:S(2)}, u32[]{:S(2)}) %collective-permute-start) | collective-permute-done | bytes 204832 | tf_op jit(solution)/shard_map/while/body/eval_jaxpr/ppermute | solution.py:12
  479.2 9.2 %collective-permute-done = bf16[2,400,1,128]{3,1,2,0:T(8,128)(2,1)S(1)} collective-permute-done((bf16[2,400,1,128]{3,1,2,0:T(8,128)(2,1)S(1)}, bf16[2,400,1,128]{3,1,2,0:T(8,128)(2,1)S(1)}, u32[]{:S(2)}, u32[]{:S(2)}) %collective-permute-start) | collective-permute-done | bytes 204832 | tf_op jit(solution)/shard_map/while/body/eval_jaxpr/ppermute | solution.py:12
  491.7 8.3 collective-permute-done
  578.6 8.5 %collective-permute-done = bf16[2,400,1,128]{3,1,2,0:T(8,128)(2,1)S(1)} collective-permute-done((bf16[2,400,1,128]{3,1,2,0:T(8,128)(2,1)S(1)}, bf16[2,400,1,128]{3,1,2,0:T(8,128)(2,1)S(1)}, u32[]{:S(2)}, u32[]{:S(2)}) %collective-permute-start) | collective-permute-done | bytes 204832 | tf_op jit(solution)/shard_map/while/body/eval_jaxpr/ppermute | solution.py:12
  590.3 9.7 %collective-permute-done = bf16[2,400,1,128]{3,1,2,0:T(8,128)(2,1)S(1)} collective-permute-done((bf16[2,400,1,128]{3,1,2,0:T(8,128)(2,1)S(1)}, bf16[2,400,1,128]{3,1,2,0:T(8,128)(2,1)S(1)}, u32[]{:S(2)}, u32[]{:S(2)}) %collective-permute-start) | collective-permute-done | bytes 204832 | tf_op jit(solution)/shard_map/while/body/eval_jaxpr/ppermute | solution.py:12
  603.3 9.2 %collective-permute-done = bf16[2,400,1,128]{3,1,2,0:T(8,128)(2,1)S(1)} collective-permute-done((bf16[2,400,1,128]{3,1,2,0:T(8,128)(2,1)S(1)}, bf16[2,400,1,128]{3,1,2,0:T(8,128)(2,1)S(1)}, u32[]{:S(2)}, u32[]{:S(2)}) %collective-permute-start) | collective-permute-done | bytes 204832 | tf_op jit(solution)/shard_map/while/body/eval_jaxpr/ppermute | solution.py:12
  615.7 8.3 collective-permute-done
  702.7 8.5 %collective-permute-done = bf16[2,400,1,128]{3,1,2,0:T(8,128)(2,1)S(1)} collective-permute-done((bf16[2,400,1,128]{3,1,2,0:T(8,128)(2,1)S(1)}, bf16[2,400,1,128]{3,1,2,0:T(8,128)(2,1)S(1)}, u32[]{:S(2)}, u32[]{:S(2)}) %collective-permute-start) | collective-permute-done | bytes 204832 | tf_op jit(solution)/shard_map/while/body/eval_jaxpr/ppermute | solution.py:12
  714.4 9.7 %collective-permute-done = bf16[2,400,1,128]{3,1,2,0:T(8,128)(2,1)S(1)} collective-permute-done((bf16[2,400,1,128]{3,1,2,0:T(8,128)(2,1)S(1)}, bf16[2,400,1,128]{3,1,2,0:T(8,128)(2,1)S(1)}, u32[]{:S(2)}, u32[]{:S(2)}) %collective-permute-start) | collective-permute-done | bytes 204832 | tf_op jit(solution)/shard_map/while/body/eval_jaxpr/ppermute | solution.py:12
  727.3 9.2 %collective-permute-done = bf16[2,400,1,128]{3,1,2,0:T(8,128)(2,1)S(1)} collective-permute-done((bf16[2,400,1,128]{3,1,2,0:T(8,128)(2,1)S(1)}, bf16[2,400,1,128]{3,1,2,0:T(8,128)(2,1)S(1)}, u32[]{:S(2)}, u32[]{:S(2)}) %collective-permute-start) | collective-permute-done | bytes 204832 | tf_op jit(solution)/shard_map/while/body/eval_jaxpr/ppermute | solution.py:12
  739.8 8.3 collective-permute-done
  749.1 83.9 %all_to_all.33 = bf16[16,16,128]{2,1,0:T(8,128)(2,1)S(1)} all-to-all(bf16[16,16,128]{2,1,0:T(8,128)(2,1)S(1)} %fusion.25), channel_id=1, replica_groups=mesh['ctx'=64,'kvh'=8] {'kvh'}, dimensions={0} | all-to-all | bytes 131072 | tf_op jit(solution)/shard_map/all_to_all | solution.py:82
  (950 shorter events, 467.3 us)
Async XLA Ops:
  1.6 35.8 %all-to-all-start = ((bf16[2,128,128]{2,0,1:T(2,128)(2,1)}), bf16[2,128,128]{2,0,1:T(2,128)(2,1)S(1)}, u32[]{:S(2)}, u32[]{:S(2)}) async-start(bf16[2,128,128]{2,0,1:T(2,128)(2,1)} %copy.13), calls=%async_computation | async-start | bytes 131072 | tf_op jit(solution)/shard_map/all_to_all | solution.py:36
  70.6 9.8 %collective-permute-start = (bf16[2,400,1,128]{3,1,2,0:T(8,128)(2,1)S(1)}, bf16[2,400,1,128]{3,1,2,0:T(8,128)(2,1)S(1)}, u32[]{:S(2)}, u32[]{:S(2)}) collective-permute-start(bf16[2,400,1,128]{3,1,2,0:T(8,128)(2,1)S(1)} %get-tuple-element.372), channel_id=1, source_target_pairs={{504,0},{0,8},{8,16},{16,24},{24,32},{32,40},{40,48},{48,56},{56,6... | collective-permute-start | bytes 614408 | tf_op jit(solution)/shard_map/while/body/eval_jaxpr/ppermute | solution.py:12
  81.4 10.4 %collective-permute-start = (bf16[2,400,1,128]{3,1,2,0:T(8,128)(2,1)S(1)}, bf16[2,400,1,128]{3,1,2,0:T(8,128)(2,1)S(1)}, u32[]{:S(2)}, u32[]{:S(2)}) collective-permute-start(bf16[2,400,1,128]{3,1,2,0:T(8,128)(2,1)S(1)} %get-tuple-element.372), channel_id=1, source_target_pairs={{504,0},{0,8},{8,16},{16,24},{24,32},{32,40},{40,48},{48,56},{56,6... | collective-permute-start | bytes 614408 | tf_op jit(solution)/shard_map/while/body/eval_jaxpr/ppermute | solution.py:12
  92.7 11.4 %collective-permute-start = (bf16[2,400,1,128]{3,1,2,0:T(8,128)(2,1)S(1)}, bf16[2,400,1,128]{3,1,2,0:T(8,128)(2,1)S(1)}, u32[]{:S(2)}, u32[]{:S(2)}) collective-permute-start(bf16[2,400,1,128]{3,1,2,0:T(8,128)(2,1)S(1)} %get-tuple-element.372), channel_id=1, source_target_pairs={{504,0},{0,8},{8,16},{16,24},{24,32},{32,40},{40,48},{48,56},{56,6... | collective-permute-start | bytes 614408 | tf_op jit(solution)/shard_map/while/body/eval_jaxpr/ppermute | solution.py:12
  105.1 11.7 %collective-permute-start = (bf16[2,400,1,128]{3,1,2,0:T(8,128)(2,1)S(1)}, bf16[2,400,1,128]{3,1,2,0:T(8,128)(2,1)S(1)}, u32[]{:S(2)}, u32[]{:S(2)}) collective-permute-start(bf16[2,400,1,128]{3,1,2,0:T(8,128)(2,1)S(1)} %get-tuple-element.372), channel_id=1, source_target_pairs={{504,0},{0,8},{8,16},{16,24},{24,32},{32,40},{40,48},{48,56},{56,6... | collective-permute-start | bytes 614408 | tf_op jit(solution)/shard_map/while/body/eval_jaxpr/ppermute | solution.py:12
  117.8 10.8 %collective-permute-start = (bf16[2,400,1,128]{3,1,2,0:T(8,128)(2,1)S(1)}, bf16[2,400,1,128]{3,1,2,0:T(8,128)(2,1)S(1)}, u32[]{:S(2)}, u32[]{:S(2)}) collective-permute-start(bf16[2,400,1,128]{3,1,2,0:T(8,128)(2,1)S(1)} %get-tuple-element.372), channel_id=1, source_target_pairs={{504,0},{0,8},{8,16},{16,24},{24,32},{32,40},{40,48},{48,56},{56,6... | collective-permute-start | bytes 614408 | tf_op jit(solution)/shard_map/while/body/eval_jaxpr/ppermute | solution.py:12
  129.5 9.8 %collective-permute-start = (bf16[2,400,1,128]{3,1,2,0:T(8,128)(2,1)S(1)}, bf16[2,400,1,128]{3,1,2,0:T(8,128)(2,1)S(1)}, u32[]{:S(2)}, u32[]{:S(2)}) collective-permute-start(bf16[2,400,1,128]{3,1,2,0:T(8,128)(2,1)S(1)} %get-tuple-element.372), channel_id=1, source_target_pairs={{504,0},{0,8},{8,16},{16,24},{24,32},{32,40},{40,48},{48,56},{56,6... | collective-permute-start | bytes 614408 | tf_op jit(solution)/shard_map/while/body/eval_jaxpr/ppermute | solution.py:12
  151.1 9.8 %collective-permute-start = (bf16[2,400,1,128]{3,1,2,0:T(8,128)(2,1)S(1)}, bf16[2,400,1,128]{3,1,2,0:T(8,128)(2,1)S(1)}, u32[]{:S(2)}, u32[]{:S(2)}) collective-permute-start(bf16[2,400,1,128]{3,1,2,0:T(8,128)(2,1)S(1)} %get-tuple-element.372), channel_id=1, source_target_pairs={{504,0},{0,8},{8,16},{16,24},{24,32},{32,40},{40,48},{48,56},{56,6... | collective-permute-start | bytes 614408 | tf_op jit(solution)/shard_map/while/body/eval_jaxpr/ppermute | solution.py:12
  183.4 9.8 %collective-permute-start = (bf16[2,400,1,128]{3,1,2,0:T(8,128)(2,1)S(1)}, bf16[2,400,1,128]{3,1,2,0:T(8,128)(2,1)S(1)}, u32[]{:S(2)}, u32[]{:S(2)}) collective-permute-start(bf16[2,400,1,128]{3,1,2,0:T(8,128)(2,1)S(1)} %get-tuple-element.372), channel_id=1, source_target_pairs={{504,0},{0,8},{8,16},{16,24},{24,32},{32,40},{40,48},{48,56},{56,6... | collective-permute-start | bytes 614408 | tf_op jit(solution)/shard_map/while/body/eval_jaxpr/ppermute | solution.py:12
  205.0 10.5 %collective-permute-start = (bf16[2,400,1,128]{3,1,2,0:T(8,128)(2,1)S(1)}, bf16[2,400,1,128]{3,1,2,0:T(8,128)(2,1)S(1)}, u32[]{:S(2)}, u32[]{:S(2)}) collective-permute-start(bf16[2,400,1,128]{3,1,2,0:T(8,128)(2,1)S(1)} %get-tuple-element.372), channel_id=1, source_target_pairs={{504,0},{0,8},{8,16},{16,24},{24,32},{32,40},{40,48},{48,56},{56,6... | collective-permute-start | bytes 614408 | tf_op jit(solution)/shard_map/while/body/eval_jaxpr/ppermute | solution.py:12
  216.4 11.6 %collective-permute-start = (bf16[2,400,1,128]{3,1,2,0:T(8,128)(2,1)S(1)}, bf16[2,400,1,128]{3,1,2,0:T(8,128)(2,1)S(1)}, u32[]{:S(2)}, u32[]{:S(2)}) collective-permute-start(bf16[2,400,1,128]{3,1,2,0:T(8,128)(2,1)S(1)} %get-tuple-element.372), channel_id=1, source_target_pairs={{504,0},{0,8},{8,16},{16,24},{24,32},{32,40},{40,48},{48,56},{56,6... | collective-permute-start | bytes 614408 | tf_op jit(solution)/shard_map/while/body/eval_jaxpr/ppermute | solution.py:12
  229.0 11.6 %collective-permute-start = (bf16[2,400,1,128]{3,1,2,0:T(8,128)(2,1)S(1)}, bf16[2,400,1,128]{3,1,2,0:T(8,128)(2,1)S(1)}, u32[]{:S(2)}, u32[]{:S(2)}) collective-permute-start(bf16[2,400,1,128]{3,1,2,0:T(8,128)(2,1)S(1)} %get-tuple-element.372), channel_id=1, source_target_pairs={{504,0},{0,8},{8,16},{16,24},{24,32},{32,40},{40,48},{48,56},{56,6... | collective-permute-start | bytes 614408 | tf_op jit(solution)/shard_map/while/body/eval_jaxpr/ppermute | solution.py:12
  241.5 10.6 %collective-permute-start = (bf16[2,400,1,128]{3,1,2,0:T(8,128)(2,1)S(1)}, bf16[2,400,1,128]{3,1,2,0:T(8,128)(2,1)S(1)}, u32[]{:S(2)}, u32[]{:S(2)}) collective-permute-start(bf16[2,400,1,128]{3,1,2,0:T(8,128)(2,1)S(1)} %get-tuple-element.372), channel_id=1, source_target_pairs={{504,0},{0,8},{8,16},{16,24},{24,32},{32,40},{40,48},{48,56},{56,6... | collective-permute-start | bytes 614408 | tf_op jit(solution)/shard_map/while/body/eval_jaxpr/ppermute | solution.py:12
  263.9 9.8 %collective-permute-start = (bf16[2,400,1,128]{3,1,2,0:T(8,128)(2,1)S(1)}, bf16[2,400,1,128]{3,1,2,0:T(8,128)(2,1)S(1)}, u32[]{:S(2)}, u32[]{:S(2)}) collective-permute-start(bf16[2,400,1,128]{3,1,2,0:T(8,128)(2,1)S(1)} %get-tuple-element.372), channel_id=1, source_target_pairs={{504,0},{0,8},{8,16},{16,24},{24,32},{32,40},{40,48},{48,56},{56,6... | collective-permute-start | bytes 614408 | tf_op jit(solution)/shard_map/while/body/eval_jaxpr/ppermute | solution.py:12
  274.6 9.8 %collective-permute-start = (bf16[2,400,1,128]{3,1,2,0:T(8,128)(2,1)S(1)}, bf16[2,400,1,128]{3,1,2,0:T(8,128)(2,1)S(1)}, u32[]{:S(2)}, u32[]{:S(2)}) collective-permute-start(bf16[2,400,1,128]{3,1,2,0:T(8,128)(2,1)S(1)} %get-tuple-element.372), channel_id=1, source_target_pairs={{504,0},{0,8},{8,16},{16,24},{24,32},{32,40},{40,48},{48,56},{56,6... | collective-permute-start | bytes 614408 | tf_op jit(solution)/shard_map/while/body/eval_jaxpr/ppermute | solution.py:12
  328.5 10.7 %collective-permute-start = (bf16[2,400,1,128]{3,1,2,0:T(8,128)(2,1)S(1)}, bf16[2,400,1,128]{3,1,2,0:T(8,128)(2,1)S(1)}, u32[]{:S(2)}, u32[]{:S(2)}) collective-permute-start(bf16[2,400,1,128]{3,1,2,0:T(8,128)(2,1)S(1)} %get-tuple-element.372), channel_id=1, source_target_pairs={{504,0},{0,8},{8,16},{16,24},{24,32},{32,40},{40,48},{48,56},{56,6... | collective-permute-start | bytes 614408 | tf_op jit(solution)/shard_map/while/body/eval_jaxpr/ppermute | solution.py:12
  340.1 11.8 %collective-permute-start = (bf16[2,400,1,128]{3,1,2,0:T(8,128)(2,1)S(1)}, bf16[2,400,1,128]{3,1,2,0:T(8,128)(2,1)S(1)}, u32[]{:S(2)}, u32[]{:S(2)}) collective-permute-start(bf16[2,400,1,128]{3,1,2,0:T(8,128)(2,1)S(1)} %get-tuple-element.372), channel_id=1, source_target_pairs={{504,0},{0,8},{8,16},{16,24},{24,32},{32,40},{40,48},{48,56},{56,6... | collective-permute-start | bytes 614408 | tf_op jit(solution)/shard_map/while/body/eval_jaxpr/ppermute | solution.py:12
  352.9 11.5 %collective-permute-start = (bf16[2,400,1,128]{3,1,2,0:T(8,128)(2,1)S(1)}, bf16[2,400,1,128]{3,1,2,0:T(8,128)(2,1)S(1)}, u32[]{:S(2)}, u32[]{:S(2)}) collective-permute-start(bf16[2,400,1,128]{3,1,2,0:T(8,128)(2,1)S(1)} %get-tuple-element.372), channel_id=1, source_target_pairs={{504,0},{0,8},{8,16},{16,24},{24,32},{32,40},{40,48},{48,56},{56,6... | collective-permute-start | bytes 614408 | tf_op jit(solution)/shard_map/while/body/eval_jaxpr/ppermute | solution.py:12
  365.3 10.6 %collective-permute-start = (bf16[2,400,1,128]{3,1,2,0:T(8,128)(2,1)S(1)}, bf16[2,400,1,128]{3,1,2,0:T(8,128)(2,1)S(1)}, u32[]{:S(2)}, u32[]{:S(2)}) collective-permute-start(bf16[2,400,1,128]{3,1,2,0:T(8,128)(2,1)S(1)} %get-tuple-element.372), channel_id=1, source_target_pairs={{504,0},{0,8},{8,16},{16,24},{24,32},{32,40},{40,48},{48,56},{56,6... | collective-permute-start | bytes 614408 | tf_op jit(solution)/shard_map/while/body/eval_jaxpr/ppermute | solution.py:12
  398.4 9.8 %collective-permute-start = (bf16[2,400,1,128]{3,1,2,0:T(8,128)(2,1)S(1)}, bf16[2,400,1,128]{3,1,2,0:T(8,128)(2,1)S(1)}, u32[]{:S(2)}, u32[]{:S(2)}) collective-permute-start(bf16[2,400,1,128]{3,1,2,0:T(8,128)(2,1)S(1)} %get-tuple-element.372), channel_id=1, source_target_pairs={{504,0},{0,8},{8,16},{16,24},{24,32},{32,40},{40,48},{48,56},{56,6... | collective-permute-start | bytes 614408 | tf_op jit(solution)/shard_map/while/body/eval_jaxpr/ppermute | solution.py:12
  452.3 10.7 %collective-permute-start = (bf16[2,400,1,128]{3,1,2,0:T(8,128)(2,1)S(1)}, bf16[2,400,1,128]{3,1,2,0:T(8,128)(2,1)S(1)}, u32[]{:S(2)}, u32[]{:S(2)}) collective-permute-start(bf16[2,400,1,128]{3,1,2,0:T(8,128)(2,1)S(1)} %get-tuple-element.372), channel_id=1, source_target_pairs={{504,0},{0,8},{8,16},{16,24},{24,32},{32,40},{40,48},{48,56},{56,6... | collective-permute-start | bytes 614408 | tf_op jit(solution)/shard_map/while/body/eval_jaxpr/ppermute | solution.py:12
  464.0 12.0 %collective-permute-start = (bf16[2,400,1,128]{3,1,2,0:T(8,128)(2,1)S(1)}, bf16[2,400,1,128]{3,1,2,0:T(8,128)(2,1)S(1)}, u32[]{:S(2)}, u32[]{:S(2)}) collective-permute-start(bf16[2,400,1,128]{3,1,2,0:T(8,128)(2,1)S(1)} %get-tuple-element.372), channel_id=1, source_target_pairs={{504,0},{0,8},{8,16},{16,24},{24,32},{32,40},{40,48},{48,56},{56,6... | collective-permute-start | bytes 614408 | tf_op jit(solution)/shard_map/while/body/eval_jaxpr/ppermute | solution.py:12
  476.9 11.5 %collective-permute-start = (bf16[2,400,1,128]{3,1,2,0:T(8,128)(2,1)S(1)}, bf16[2,400,1,128]{3,1,2,0:T(8,128)(2,1)S(1)}, u32[]{:S(2)}, u32[]{:S(2)}) collective-permute-start(bf16[2,400,1,128]{3,1,2,0:T(8,128)(2,1)S(1)} %get-tuple-element.372), channel_id=1, source_target_pairs={{504,0},{0,8},{8,16},{16,24},{24,32},{32,40},{40,48},{48,56},{56,6... | collective-permute-start | bytes 614408 | tf_op jit(solution)/shard_map/while/body/eval_jaxpr/ppermute | solution.py:12
  489.4 10.6 %collective-permute-start = (bf16[2,400,1,128]{3,1,2,0:T(8,128)(2,1)S(1)}, bf16[2,400,1,128]{3,1,2,0:T(8,128)(2,1)S(1)}, u32[]{:S(2)}, u32[]{:S(2)}) collective-permute-start(bf16[2,400,1,128]{3,1,2,0:T(8,128)(2,1)S(1)} %get-tuple-element.372), channel_id=1, source_target_pairs={{504,0},{0,8},{8,16},{16,24},{24,32},{32,40},{40,48},{48,56},{56,6... | collective-permute-start | bytes 614408 | tf_op jit(solution)/shard_map/while/body/eval_jaxpr/ppermute | solution.py:12
  576.3 10.8 %collective-permute-start = (bf16[2,400,1,128]{3,1,2,0:T(8,128)(2,1)S(1)}, bf16[2,400,1,128]{3,1,2,0:T(8,128)(2,1)S(1)}, u32[]{:S(2)}, u32[]{:S(2)}) collective-permute-start(bf16[2,400,1,128]{3,1,2,0:T(8,128)(2,1)S(1)} %get-tuple-element.372), channel_id=1, source_target_pairs={{504,0},{0,8},{8,16},{16,24},{24,32},{32,40},{40,48},{48,56},{56,6... | collective-permute-start | bytes 614408 | tf_op jit(solution)/shard_map/while/body/eval_jaxpr/ppermute | solution.py:12
  588.0 12.0 %collective-permute-start = (bf16[2,400,1,128]{3,1,2,0:T(8,128)(2,1)S(1)}, bf16[2,400,1,128]{3,1,2,0:T(8,128)(2,1)S(1)}, u32[]{:S(2)}, u32[]{:S(2)}) collective-permute-start(bf16[2,400,1,128]{3,1,2,0:T(8,128)(2,1)S(1)} %get-tuple-element.372), channel_id=1, source_target_pairs={{504,0},{0,8},{8,16},{16,24},{24,32},{32,40},{40,48},{48,56},{56,6... | collective-permute-start | bytes 614408 | tf_op jit(solution)/shard_map/while/body/eval_jaxpr/ppermute | solution.py:12
  601.0 11.5 %collective-permute-start = (bf16[2,400,1,128]{3,1,2,0:T(8,128)(2,1)S(1)}, bf16[2,400,1,128]{3,1,2,0:T(8,128)(2,1)S(1)}, u32[]{:S(2)}, u32[]{:S(2)}) collective-permute-start(bf16[2,400,1,128]{3,1,2,0:T(8,128)(2,1)S(1)} %get-tuple-element.372), channel_id=1, source_target_pairs={{504,0},{0,8},{8,16},{16,24},{24,32},{32,40},{40,48},{48,56},{56,6... | collective-permute-start | bytes 614408 | tf_op jit(solution)/shard_map/while/body/eval_jaxpr/ppermute | solution.py:12
  613.4 10.6 %collective-permute-start = (bf16[2,400,1,128]{3,1,2,0:T(8,128)(2,1)S(1)}, bf16[2,400,1,128]{3,1,2,0:T(8,128)(2,1)S(1)}, u32[]{:S(2)}, u32[]{:S(2)}) collective-permute-start(bf16[2,400,1,128]{3,1,2,0:T(8,128)(2,1)S(1)} %get-tuple-element.372), channel_id=1, source_target_pairs={{504,0},{0,8},{8,16},{16,24},{24,32},{32,40},{40,48},{48,56},{56,6... | collective-permute-start | bytes 614408 | tf_op jit(solution)/shard_map/while/body/eval_jaxpr/ppermute | solution.py:12
  700.4 10.7 %collective-permute-start = (bf16[2,400,1,128]{3,1,2,0:T(8,128)(2,1)S(1)}, bf16[2,400,1,128]{3,1,2,0:T(8,128)(2,1)S(1)}, u32[]{:S(2)}, u32[]{:S(2)}) collective-permute-start(bf16[2,400,1,128]{3,1,2,0:T(8,128)(2,1)S(1)} %get-tuple-element.372), channel_id=1, source_target_pairs={{504,0},{0,8},{8,16},{16,24},{24,32},{32,40},{40,48},{48,56},{56,6... | collective-permute-start | bytes 614408 | tf_op jit(solution)/shard_map/while/body/eval_jaxpr/ppermute | solution.py:12
  712.1 12.0 %collective-permute-start = (bf16[2,400,1,128]{3,1,2,0:T(8,128)(2,1)S(1)}, bf16[2,400,1,128]{3,1,2,0:T(8,128)(2,1)S(1)}, u32[]{:S(2)}, u32[]{:S(2)}) collective-permute-start(bf16[2,400,1,128]{3,1,2,0:T(8,128)(2,1)S(1)} %get-tuple-element.372), channel_id=1, source_target_pairs={{504,0},{0,8},{8,16},{16,24},{24,32},{32,40},{40,48},{48,56},{56,6... | collective-permute-start | bytes 614408 | tf_op jit(solution)/shard_map/while/body/eval_jaxpr/ppermute | solution.py:12
  725.1 11.5 %collective-permute-start = (bf16[2,400,1,128]{3,1,2,0:T(8,128)(2,1)S(1)}, bf16[2,400,1,128]{3,1,2,0:T(8,128)(2,1)S(1)}, u32[]{:S(2)}, u32[]{:S(2)}) collective-permute-start(bf16[2,400,1,128]{3,1,2,0:T(8,128)(2,1)S(1)} %get-tuple-element.372), channel_id=1, source_target_pairs={{504,0},{0,8},{8,16},{16,24},{24,32},{32,40},{40,48},{48,56},{56,6... | collective-permute-start | bytes 614408 | tf_op jit(solution)/shard_map/while/body/eval_jaxpr/ppermute | solution.py:12
  737.5 10.6 %collective-permute-start = (bf16[2,400,1,128]{3,1,2,0:T(8,128)(2,1)S(1)}, bf16[2,400,1,128]{3,1,2,0:T(8,128)(2,1)S(1)}, u32[]{:S(2)}, u32[]{:S(2)}) collective-permute-start(bf16[2,400,1,128]{3,1,2,0:T(8,128)(2,1)S(1)} %get-tuple-element.372), channel_id=1, source_target_pairs={{504,0},{0,8},{8,16},{16,24},{24,32},{32,40},{40,48},{48,56},{56,6... | collective-permute-start | bytes 614408 | tf_op jit(solution)/shard_map/while/body/eval_jaxpr/ppermute | solution.py:12
  (38 other events, 435.8 us)
where the time goes:
time: 837 us; the launch traced here: 834 us
  waiting for transfers between devices  506 us (60%)
  starting transfers between devices  132 us (16%)
  blocking collectives  106 us (13%)
  matrix products  39.4 us (5%)
  other arithmetic  22.7 us (3%)
  local copies, waits for them, and re-layouts  20.5 us (2%)
    ppermute x63, waiting for transfers between devices, passed_along(): return lax.ppermute(block, axis, route)  506 us
    ppermute x63, starting transfers between devices, passed_along(): return lax.ppermute(block, axis, route)  121 us
    all_to_all x1, blocking collectives, body(): lax.all_to_all(result, 'kvh', split_axis=0, concat_axis=1, tiled=True)  83.9 us
    unnamed x1, blocking collectives  22.2 us
    dot_general x64, matrix products, attend(): jnp.einsum('tgqd,kgd->tgqk', grouped, kv_block[0], preferred_element_type...  19.8 us
    dot_general x64, matrix products, attend(): jnp.einsum('tgqk,kgd->tgqd', rounded, kv_block[1], preferred_element_type...  19.6 us
  transfers between devices with their start and end apart: 64, of which 63 were waited for; matrix products, arithmetic and copies ran while one was open for 3% of the time, Pallas kernels for 0%

commit v1 on v0

v1 whole, which is shorter than its diff:
```python
import functools
import math

import jax
import jax.numpy as jnp
from jax import lax
from jax.experimental import pallas as pl
from jax.experimental.pallas import tpu as pltpu
from jax.sharding import Mesh, PartitionSpec as P

ZN, YN, XN, CN = 8, 8, 4, 2
KN = XN * CN
HEADS, GROUP, HD, PAGE, SLOTS, NEWT = 128, 16, 128, 128, 3, 16
HISTORY = SLOTS * PAGE
KV_ROWS = HISTORY + 2 * NEWT
PAGES = 2 * ZN
KEYS = PAGES * PAGE + ZN * NEWT
OWN = 2
BLOCK = OWN * GROUP
WIRE = BLOCK + 8
ALL_BLOCKS = YN * KN
STEP_BLOCKS = 16
ROWS = STEP_BLOCKS * BLOCK
CHUNKS = ((0, 512), (512, 512), (1024, 512), (1536, 512), (2048, 128))
TO_BITS = math.log2(math.e) / math.sqrt(HD)
LOWEST = -1e30


def attend_kernel(slots, kv, q, out, keys, values, key_positions, scores):
    @pl.when(pl.program_id(0) == 0)
    def _():
        for i in range(PAGES):
            slot = slots[i]
            source = slot // SLOTS
            first = pl.multiple_of((slot % SLOTS) * PAGE, PAGE)
            keys[i * PAGE : (i + 1) * PAGE, :] = kv[source, 0, pl.ds(first, PAGE), :]
            values[i * PAGE : (i + 1) * PAGE, :HD] = kv[source, 1, pl.ds(first, PAGE), :]
        base = PAGES * PAGE
        for z in range(ZN):
            here = slice(base + z * NEWT, base + (z + 1) * NEWT)
            keys[here, :] = kv[z, 0, HISTORY : HISTORY + NEWT, :]
            values[here, :HD] = kv[z, 1, HISTORY : HISTORY + NEWT, :]
        values[:, HD:] = jnp.ones((KEYS, HD), jnp.bfloat16)
        high = kv[:, 0, HISTORY + NEWT :, :].astype(jnp.float32)
        low = kv[:, 1, HISTORY + NEWT :, :].astype(jnp.float32)
        key_positions[...] = jnp.sum(high * 32.0 + low, axis=0)[:8]

    rows = q[:, :BLOCK, :].reshape(ROWS, HD)
    tags = q[:, BLOCK:, :].astype(jnp.float32)
    key_at = key_positions[0:1, :]
    bias = []
    for t in range(OWN):
        query_at = tags[:, 2 * t, :] * 32.0 + tags[:, 2 * t + 1, :]
        hidden = jnp.where(key_at <= query_at, 0.0, LOWEST)
        bias.append(jnp.broadcast_to(hidden[:, None, :], (STEP_BLOCKS, GROUP, HD)))
    bias = jnp.stack(bias, axis=1).reshape(ROWS, HD)
    top = None
    for start, size in CHUNKS:
        part = lax.dot_general(
            rows, keys[start : start + size, :], (((1,), (1,)), ((), ())), preferred_element_type=jnp.float32
        )
        if size == ZN * NEWT:
            part = part + bias
        scores[:, start : start + size] = part
        for j in range(size // HD):
            piece = part[:, j * HD : (j + 1) * HD]
            top = piece if top is None else jnp.maximum(top, piece)
    top = jnp.max(top, axis=1, keepdims=True) * TO_BITS
    summed = jnp.zeros((ROWS, 2 * HD), jnp.float32)
    for start, size in CHUNKS:
        weights = jnp.exp2(scores[:, start : start + size] * TO_BITS - top).astype(jnp.bfloat16)
        summed += jnp.dot(weights, values[start : start + size, :], preferred_element_type=jnp.float32)
    total = summed[:, HD:]
    out[:, :BLOCK, :] = (summed[:, :HD] / total).astype(jnp.bfloat16).reshape(STEP_BLOCKS, BLOCK, HD)
    level = (top + jnp.log2(total)).reshape(STEP_BLOCKS, BLOCK, HD)
    row = lax.broadcasted_iota(jnp.int32, (STEP_BLOCKS, BLOCK, HD), 1)
    lane = lax.broadcasted_iota(jnp.int32, (STEP_BLOCKS, BLOCK, HD), 2)
    level = jnp.sum(jnp.where(row == lane, level, 0.0), axis=1, keepdims=True)
    high = level.astype(jnp.bfloat16).astype(jnp.float32)
    rest = level - high
    middle = rest.astype(jnp.bfloat16).astype(jnp.float32)
    zeros = jnp.zeros((STEP_BLOCKS, 5, HD), jnp.float32)
    out[:, BLOCK:, :] = jnp.concatenate([high, middle, rest - middle, zeros], axis=1).astype(jnp.bfloat16)


def attend(slots, kv, q):
    return pl.pallas_call(
        attend_kernel,
        out_shape=jax.ShapeDtypeStruct((ALL_BLOCKS, WIRE, HD), jnp.bfloat16),
        grid_spec=pltpu.PrefetchScalarGridSpec(
            num_scalar_prefetch=1,
            grid=(ALL_BLOCKS // STEP_BLOCKS,),
            in_specs=[
                pl.BlockSpec((ZN, 2, KV_ROWS, HD), lambda i, s: (0, 0, 0, 0)),
                pl.BlockSpec((STEP_BLOCKS, WIRE, HD), lambda i, s: (i, 0, 0)),
            ],
            out_specs=pl.BlockSpec((STEP_BLOCKS, WIRE, HD), lambda i, s: (i, 0, 0)),
            scratch_shapes=[
                pltpu.VMEM((KEYS, HD), jnp.bfloat16),
                pltpu.VMEM((KEYS, 2 * HD), jnp.bfloat16),
                pltpu.VMEM((8, HD), jnp.float32),
                pltpu.VMEM((ROWS, KEYS), jnp.float32),
            ],
        ),
        compiler_params=pltpu.CompilerParams(vmem_limit_bytes=40 * 1024 * 1024),
        cost_estimate=pl.CostEstimate(flops=2300000000, bytes_accessed=4000000, transcendentals=4456448),
    )(slots, kv, q)


def combine_kernel(parts, out):
    tags = parts[:, BLOCK:, :].astype(jnp.float32)
    level = tags[:, 0:1, :] + tags[:, 1:2, :] + tags[:, 2:3, :]
    level = level.reshape(YN, KN, 1, HD)
    weight = jnp.exp2(level - jnp.max(level, axis=0, keepdims=True))
    weight = weight / jnp.sum(weight, axis=0, keepdims=True)
    row = lax.broadcasted_iota(jnp.int32, (BLOCK, HD), 0)
    lane = lax.broadcasted_iota(jnp.int32, (BLOCK, HD), 1)
    for k in range(KN):
        merged = jnp.zeros((BLOCK, HD), jnp.float32)
        for y in range(YN):
            column = jnp.sum(jnp.where(row == lane, weight[y, k], 0.0), axis=1, keepdims=True)
            merged += column * parts[y * KN + k, :BLOCK, :].astype(jnp.float32)
        merged = merged.astype(jnp.bfloat16)
        for t in range(OWN):
            out[t, k * GROUP : (k + 1) * GROUP, :] = merged[t * GROUP : (t + 1) * GROUP, :]


def combine(parts):
    return pl.pallas_call(
        combine_kernel,
        out_shape=jax.ShapeDtypeStruct((OWN, HEADS, HD), jnp.bfloat16),
        compiler_params=pltpu.CompilerParams(vmem_limit_bytes=16 * 1024 * 1024),
        cost_estimate=pl.CostEstimate(flops=1000000, bytes_accessed=800000, transcendentals=8192),
    )(parts)


def body(queries, new_keys, new_values, new_positions, hist_keys, hist_values, page_slots):
    z, y = lax.axis_index("z"), lax.axis_index("y")
    k = lax.axis_index(("x", "c"))
    high = (new_positions // 32).astype(jnp.bfloat16)
    low = (new_positions % 32).astype(jnp.bfloat16)

    def with_tag(history, fresh, tag):
        placed = lax.dynamic_update_slice(jnp.zeros((1, HD), jnp.bfloat16), tag[None, :], (0, z * NEWT))
        return jnp.concatenate(
            [history.reshape(HISTORY, HD), fresh.reshape(NEWT, HD), placed, jnp.zeros((NEWT - 1, HD), jnp.bfloat16)]
        )

    kv = jnp.stack([with_tag(hist_keys, new_keys, high), with_tag(hist_values, new_values, low)])
    kv = lax.all_gather(kv, "z", axis=0, tiled=False)
    held = lax.dynamic_index_in_dim(page_slots.reshape(ZN, YN, 2), y, 1, keepdims=False).reshape(PAGES)
    slots = (held // (SLOTS * YN)) * SLOTS + held % SLOTS

    own_high = lax.dynamic_slice_in_dim(high, k * OWN, OWN)
    own_low = lax.dynamic_slice_in_dim(low, k * OWN, OWN)
    tag = jnp.stack([own_high[0], own_low[0], own_high[1], own_low[1]] + [jnp.zeros((), jnp.bfloat16)] * 4)
    sent = queries.reshape(OWN, KN, GROUP, HD).transpose(1, 0, 2, 3).reshape(KN, BLOCK, HD)
    sent = jnp.concatenate([sent, jnp.broadcast_to(tag[None, :, None], (KN, 8, HD))], axis=1)
    sent = jnp.broadcast_to(sent[None], (YN, KN, WIRE, HD)).reshape(ALL_BLOCKS, WIRE, HD)
    q = lax.all_to_all(sent, ("y", "x", "c"), split_axis=0, concat_axis=0, tiled=True)
    parts = attend(slots, kv, q)
    parts = lax.all_to_all(parts, ("y", "x", "c"), split_axis=0, concat_axis=0, tiled=True)
    return combine(parts)


def solution(mesh):
    split = Mesh(mesh.devices.reshape(ZN, YN, XN, CN), ("z", "y", "x", "c"))
    ctx, kvh = ("z", "y"), ("x", "c")
    in_specs = (
        P(ctx + kvh, None, None),
        P(ctx, kvh, None),
        P(ctx, kvh, None),
        P(ctx),
        P(ctx, None, kvh, None),
        P(ctx, None, kvh, None),
        P(),
    )
    return jax.shard_map(body, mesh=split, in_specs=in_specs, out_specs=P(ctx + kvh, None, None), check_vma=False)
```

time: 837 us -> 111 us (0.13)
  waiting for transfers between devices: 506 us -> 27.9 us
  starting transfers between devices: 132 us -> 11.6 us
  blocking collectives: 106 us -> 34.5 us
  matrix products: 39.4 us -> 0 us
  other arithmetic: 22.7 us -> 2.6 us
  Pallas kernels: 0 us -> 12.9 us
  between operations: 0.69 us -> 13.5 us
  local copies, waits for them, and re-layouts: 20.5 us -> 7.74 us
    ppermute x63 -> x0, waiting for transfers between devices: 506 us -> none  [passed_along(): return lax.ppermute(block, axis, route)]
    ppermute x63 -> x0, starting transfers between devices: 121 us -> none  [passed_along(): return lax.ppermute(block, axis, route)]
    all_to_all x1, blocking collectives: 83.9 us -> 34.5 us  [body(): lax.all_to_all(parts, ('y', 'x', 'c'), split_axis=0, concat_axis=0, tiled...]
    dot_general x128 -> x0, matrix products: 39.4 us -> none  [the longest x64 19.8 us: attend(): jnp.einsum('tgqd,kgd->tgqk', grouped, kv_block[0], preferred_element_type...]
    unnamed x1 -> x0, blocking collectives: 22.2 us -> none
    all_to_all x1, waiting for transfers between devices: 0.01 us -> 19.6 us  [body(): lax.all_to_all(sent, ('y', 'x', 'c'), split_axis=0, concat_axis=0, tiled=...]
    reduce_sum x64 -> x0, other arithmetic: 15.8 us -> none  [attend(): row_total = row_total * factor + jnp.sum(weights, axis=-1)]
    pallas_call x0 -> x2, Pallas kernels: none -> 12.9 us  [the longest x1 11.8 us: attend(): pl.pallas_call(attend_kernel, out_shape=jax.ShapeDtypeStruct((ALL_BLOCKS,...]
  transfers between devices with their start and end apart: 64 -> 2, of which waited for: 63 -> 2; matrix products, arithmetic and copies ran while one was open for 3% -> 5% of each run, Pallas kernels for 0% -> 0%
where the time goes in v1:
time: 111 us
  blocking collectives  34.5 us (31%)
  waiting for transfers between devices  27.9 us (25%)
  between operations  13.5 us (12%)
  Pallas kernels  12.9 us (12%)
  starting transfers between devices  11.6 us (10%)
  local copies, waits for them, and re-layouts  7.74 us (7%)
  other arithmetic  2.6 us (2%)
    all_to_all x1, blocking collectives, body(): lax.all_to_all(parts, ('y', 'x', 'c'), split_axis=0, concat_axis=0, tiled...  34.5 us
    all_to_all x1, waiting for transfers between devices, body(): lax.all_to_all(sent, ('y', 'x', 'c'), split_axis=0, concat_axis=0, tiled=...  19.6 us
    pallas_call x1, Pallas kernels, attend(): pl.pallas_call(attend_kernel, out_shape=jax.ShapeDtypeStruct((ALL_BLOCKS,...  11.8 us
    all_to_all x1, starting transfers between devices, body(): lax.all_to_all(sent, ('y', 'x', 'c'), split_axis=0, concat_axis=0, tiled=...  11.6 us
    all_gather x1, waiting for transfers between devices, body(): kv = lax.all_gather(kv, 'z', axis=0, tiled=False)  8.31 us
    another operation x1, local copies, waits for them, and re-layouts, body(): jnp.stack([own_high[0], own_low[0], own_high[1], own_low[1]] + [jnp.zeros...  2.59 us
  transfers between devices with their start and end apart: 2, of which 2 were waited for; matrix products, arithmetic and copies ran while one was open for 5% of the time, Pallas kernels for 0%

profile of v1, /device:TPU:1, one launch (start us, length us, event | category | flops | bytes accessed | tf_op | source)
XLA Modules:
  0.0 110.7 jit_solution(15306564014609721285)
XLA Ops:
  6.5 0.0 all-gather.3.cloned.1.call-start
  6.5 0.7 fusion.3
  7.2 0.1 dynamic_update_slice.6
  7.4 0.1 dynamic_update_slice.7
  7.5 0.1 pad.11.clone
  7.6 1.1 maximum_bitcast_fusion
  8.7 0.7 pad_maximum_fusion
  9.4 0.0 all-gather.3.cloned.1.call-update
  9.5 0.1 dynamic_slice.11
  9.5 0.1 dynamic_slice.12
  9.6 0.6 fusion.4
  10.2 2.6 %stack.15 = bf16[8]{0:T(256)(128)(2,1)S(1)} concatenate(bf16[1]{0:T(256)(128)(2,1)} %get-tuple-element.15, bf16[1]{0:T(256)(128)(2,1)} %get-tuple-element.10, bf16[1]{0:T(256)(128)(2,1)} %get-tuple-element.16, bf16[1]{0:T(256)(128)(2,1)} %get-tuple-element.9, bf16[4]{0:T(256)(128)(2,1)S(1)} %broadcast.46), dimensions={0} | concatenate | bytes 32 | tf_op jit(solution)/shard_map/stack | solution.py:156
  12.8 0.1 pad.1.clone
  12.9 0.8 copy.14
  13.7 0.1 pad_maximum_fusion.1
  13.8 0.9 broadcast_in_dim.21
  14.7 11.6 %all-to-all-start = ((bf16[64,40,128]{2,1,0:T(8,128)(2,1)}), bf16[64,40,128]{2,1,0:T(8,128)(2,1)S(1)}, u32[]{:S(2)}, u32[]{:S(2)}) async-start(bf16[64,40,128]{2,1,0:T(8,128)(2,1)} %bitcast.12), calls=%async_computation | async-start | bytes 1310720 | tf_op jit(solution)/shard_map/all_to_all | solution.py:160
  26.4 0.0 copy-done.1
  26.4 0.1 reshape.40
  26.5 0.1 copy.15
  26.6 0.1 copy.12
  26.7 0.1 div.20
  26.8 0.1 copy.13
  26.9 0.1 rem.41
  27.0 0.1 copy.11
  27.1 0.1 and.24
  27.2 19.6 %all-to-all-done.q = bf16[64,40,128]{2,1,0:T(8,128)(2,1)S(1)} async-done(((bf16[64,40,128]{2,1,0:T(8,128)(2,1)}), bf16[64,40,128]{2,1,0:T(8,128)(2,1)S(1)}, u32[]{:S(2)}, u32[]{:S(2)}) %all-to-all-start) | async-done | bytes 655392 | tf_op jit(solution)/shard_map/all_to_all | solution.py:160
  46.7 8.3 %all-gather.3.cloned.1.call-done = bf16[16,416,128]{2,1,0:T(8,128)(2,1)} async-done(((bf16[2,416,128]{2,1,0:T(8,128)(2,1)}), bf16[16,416,128]{2,1,0:T(8,128)(2,1)}) %all-gather.3.cloned.1.call-update) | async-done | bytes 1703952 | tf_op jit(solution)/shard_map/all_gather | solution.py:150
  55.0 1.5 %copy-done = bf16[16,416,128]{2,1,0:T(8,128)(2,1)S(1)} copy-done((bf16[16,416,128]{2,1,0:T(8,128)(2,1)S(1)}, bf16[16,416,128]{2,1,0:T(8,128)(2,1)}, u32[]{:S(2)}) %copy-start) | copy-done | bytes 1703960
  56.5 11.8 %shard_map.73 = bf16[64,40,128]{2,1,0:T(8,128)(2,1)S(1)} custom-call(s32[16]{0:T(128)S(1)} %fusion.slots, bf16[8,2,416,128]{3,2,1,0:T(8,128)(2,1)S(1)} %bitcast.22, bf16[64,40,128]{2,1,0:T(8,128)(2,1)S(1)} %all-to-all-done.q), custom_call_target="tpu_custom_call" | custom-call | flops 2300000000 | bytes 4000000 | tf_op jit(solution)/shard_map/pallas_call | solution.py:87
  68.3 34.5 %all_to_all.10.parts = bf16[64,40,128]{2,1,0:T(8,128)(2,1)S(1)} all-to-all(bf16[64,40,128]{2,1,0:T(8,128)(2,1)S(1)} %shard_map.73), channel_id=1, replica_groups=mesh['z'=8,'y'=8,'x'=4,'c'=2] {'y','x','c'}, dimensions={0} | all-to-all | bytes 1310720 | tf_op jit(solution)/shard_map/all_to_all | solution.py:162
  102.9 1.0 shard_map.74
  (10 shorter events, 0.1 us)
Async XLA Ops:
  6.5 48.5 %all-gather.3.cloned.1.call-start = ((), (), s32[]{:S(2)}) async-start(), calls=%async_computation.2 | async-start | bytes 1916928 | tf_op jit(solution)/shard_map/all_gather | solution.py:150
  7.6 18.8 %copy-start.1 = (s32[128]{0:T(128)S(1)}, s32[128]{0:T(128)}, u32[]{:S(2)}) copy-start(s32[128]{0:T(128)} %param.13) | copy-start | bytes 1540
  14.7 32.0 %all-to-all-start = ((bf16[64,40,128]{2,1,0:T(8,128)(2,1)}), bf16[64,40,128]{2,1,0:T(8,128)(2,1)S(1)}, u32[]{:S(2)}, u32[]{:S(2)}) async-start(bf16[64,40,128]{2,1,0:T(8,128)(2,1)} %bitcast.12), calls=%async_computation | async-start | bytes 1310720 | tf_op jit(solution)/shard_map/all_to_all | solution.py:160
  55.0 1.5 %copy-start = (bf16[16,416,128]{2,1,0:T(8,128)(2,1)S(1)}, bf16[16,416,128]{2,1,0:T(8,128)(2,1)}, u32[]{:S(2)}) copy-start(bf16[16,416,128]{2,1,0:T(8,128)(2,1)} %all-gather.3.cloned.1.call-done) | copy-start | bytes 5111812
Sparse Core Ops, SparseCore 0:
  9.6 45.4 all-gather.2

commit v2 on v0

v2 whole, which is shorter than its diff:
```python
import functools
import math

import jax
import jax.numpy as jnp
import numpy as np
from jax import lax
from jax.experimental import pallas as pl
from jax.experimental.pallas import tpu as pltpu
from jax.sharding import Mesh, PartitionSpec as P

ZN, YN, XN, CN = 8, 8, 4, 2
LINE = 8
ALL = ("z", "y", "x", "c")
HEADS, GROUP, HD, PAGE, SLOTS, NEWT = 128, 16, 128, 128, 3, 16
HISTORY = SLOTS * PAGE
KV_ROWS = HISTORY + 2 * NEWT
FRESH = LINE * NEWT
MOST_PAGES = LINE * SLOTS
KEYS = FRESH + MOST_PAGES * PAGE
OWN = 2
TOKENS = OWN * CN
BLOCK = TOKENS * GROUP
WIRE = BLOCK + 8
BLOCKS = LINE * XN
STEP_BLOCKS = 8
ROWS = STEP_BLOCKS * BLOCK
OFFSETS = (0, -3, 3, -1, -4, 2, 1, -2)
TO_BITS = math.log2(math.e) / math.sqrt(HD)
LOWEST = -1e30

IDS = np.arange(ZN * YN * XN * CN).reshape(ZN, YN, XN, CN)
CROSS = [IDS[z, :, :, 0].ravel().tolist() for z in range(ZN)] + [IDS[:, y, :, 1].ravel().tolist() for y in range(YN)]


def along(distance):
    route = []
    for z in range(ZN):
        for y in range(YN):
            for x in range(XN):
                route.append((int(IDS[z, y, x, 0]), int(IDS[(z + distance) % ZN, y, x, 0])))
                route.append((int(IDS[z, y, x, 1]), int(IDS[z, (y + distance) % YN, x, 1])))
    return route


SWAP = [(int(i), int(i) ^ 1) for i in IDS.ravel()]


def call(kernel, out_shape, megabytes=16, flops=1000000, moved=800000, **options):
    return pl.pallas_call(
        kernel,
        out_shape=out_shape,
        compiler_params=pltpu.CompilerParams(vmem_limit_bytes=megabytes * 1024 * 1024),
        cost_estimate=pl.CostEstimate(flops=flops, bytes_accessed=moved, transcendentals=flops // 500),
        **options,
    )


def bf16(*shape):
    return jax.ShapeDtypeStruct(shape, jnp.bfloat16)


SMEM = pl.BlockSpec(memory_space=pltpu.SMEM)
VMEM = pl.BlockSpec(memory_space=pltpu.VMEM)


def pack_kernel(place, positions, queries, hist_keys, hist_values, new_keys, new_values, kv, kept, sent):
    core, line = place[0], place[1]
    for side, (history, fresh) in enumerate(((hist_keys, new_keys), (hist_values, new_values))):
        kv[side, :HISTORY, :] = history[...]
        kv[side, HISTORY : HISTORY + NEWT, :] = fresh[...]
        lane = lax.broadcasted_iota(jnp.int32, (NEWT, HD), 1)
        tag = jnp.zeros((NEWT, HD), jnp.int32)
        for i in range(NEWT):
            digit = positions[i] // 32 if side == 0 else positions[i] % 32
            tag = jnp.where(lane == line * NEWT + i, digit, tag)
        kv[side, HISTORY + NEWT :, :] = tag.astype(jnp.float32).astype(jnp.bfloat16)
    for target, parity in ((kept, core), (sent, 1 - core)):
        for t in range(OWN):
            for x in range(XN):
                first = pl.multiple_of((CN * x + parity) * GROUP, GROUP)
                target[t, x] = queries[t, pl.ds(first, GROUP), :]


def spread_kernel(place, positions, kept, received, out):
    core, x_here = place[0], place[2]
    row = lax.broadcasted_iota(jnp.int32, (8, HD), 0)
    tag = jnp.zeros((8, HD), jnp.int32)
    for i in range(TOKENS):
        position = positions[x_here * TOKENS + i]
        tag = jnp.where(row == 2 * i, position // 32, tag)
        tag = jnp.where(row == 2 * i + 1, position % 32, tag)
    tag = tag.astype(jnp.float32).astype(jnp.bfloat16)
    for x in range(XN):
        for other, array in ((0, kept), (1, received)):
            owner = core if other == 0 else 1 - core
            rows = array[:, x].reshape(OWN * GROUP, HD)
            first = pl.multiple_of(owner * OWN * GROUP, OWN * GROUP)
            for line in range(LINE):
                out[line * XN + x, pl.ds(first, OWN * GROUP), :] = rows
        for line in range(LINE):
            out[line * XN + x, BLOCK:, :] = tag


def join_kernel(own, lower, upper, three, two):
    for i, block in enumerate((own, lower, upper)):
        three[i] = block[...]
        if i < 2:
            two[i] = block[...]


def attend_kernel(
    place, page_slots, own, lower, upper, below, above, q, out, keys, values, key_positions, scores, found
):
    core, line, ctx = place[0], place[1], place[3]

    @pl.when(pl.program_id(0) == 0)
    def _():
        values[:, HD:] = jnp.ones((KEYS, HD), jnp.bfloat16)
        blocks = [own, lower, upper] + [below.at[i] for i in range(3)] + [above.at[i] for i in range(2)]
        stride = jnp.where(core == 0, YN, 1)
        high = jnp.zeros((NEWT, HD), jnp.float32)
        low = jnp.zeros((NEWT, HD), jnp.float32)
        count = jnp.int32(0)
        for block, offset in zip(blocks, OFFSETS, strict=True):
            source_line = lax.rem(line + offset + LINE, LINE)
            source = ctx + (source_line - line) * stride
            other = lax.rem(source + ZN * YN // 2, ZN * YN)
            first = pl.multiple_of(source_line * NEWT, NEWT)
            keys[pl.ds(first, NEWT), :] = block[0, HISTORY : HISTORY + NEWT, :]
            values[pl.ds(first, NEWT), :HD] = block[1, HISTORY : HISTORY + NEWT, :]
            high += block[0, HISTORY + NEWT :, :].astype(jnp.float32)
            low += block[1, HISTORY + NEWT :, :].astype(jnp.float32)
            candidates = [page_slots[2 * source], page_slots[2 * source + 1]]
            candidates += [page_slots[2 * other], page_slots[2 * other + 1]]
            for s in range(SLOTS):
                slot = source * SLOTS + s
                live = functools.reduce(jnp.logical_or, [candidate == slot for candidate in candidates])
                to = pl.multiple_of(FRESH + count * PAGE, PAGE)

                @pl.when(live)
                def _(block=block, s=s, to=to):
                    keys[pl.ds(to, PAGE), :] = block[0, s * PAGE : (s + 1) * PAGE, :]
                    values[pl.ds(to, PAGE), :HD] = block[1, s * PAGE : (s + 1) * PAGE, :]

                count += live.astype(jnp.int32)
        key_positions[...] = (high * 32.0 + low)[:8]
        found[0] = count
        for i in range(1, MOST_PAGES):

            @pl.when(i >= count)
            def _(i=i):
                here = slice(FRESH + i * PAGE, FRESH + (i + 1) * PAGE)
                keys[here, :] = keys[FRESH : FRESH + PAGE, :]
                values[here, :] = jnp.zeros((PAGE, 2 * HD), jnp.bfloat16)

    count = found[0]

    def attend_to(pages):
        chunks = [(0, FRESH + 3 * PAGE)]
        while sum(chunks[-1]) < FRESH + pages * PAGE:
            start = sum(chunks[-1])
            chunks.append((start, min(4 * PAGE, FRESH + pages * PAGE - start)))
        rows = q[:, :BLOCK, :].reshape(ROWS, HD)
        tags = q[:, BLOCK:, :].astype(jnp.float32)
        key_at = key_positions[0:1, :]
        bias = []
        for t in range(TOKENS):
            query_at = tags[:, 2 * t, :] * 32.0 + tags[:, 2 * t + 1, :]
            hidden = jnp.where(key_at <= query_at, 0.0, LOWEST)
            bias.append(jnp.broadcast_to(hidden[:, None, :], (STEP_BLOCKS, GROUP, HD)))
        bias = jnp.stack(bias, axis=1).reshape(ROWS, HD)
        top = None
        for start, size in chunks:
            part = lax.dot_general(
                rows, keys[start : start + size, :], (((1,), (1,)), ((), ())), preferred_element_type=jnp.float32
            )
            for j in range(size // HD):
                piece = part[:, j * HD : (j + 1) * HD]
                if start + j == 0:
                    piece = piece + bias
                scores[:, start + j * HD : start + (j + 1) * HD] = piece
                top = piece if top is None else jnp.maximum(top, piece)
        top = jnp.max(top, axis=1, keepdims=True) * TO_BITS
        summed = jnp.zeros((ROWS, 2 * HD), jnp.float32)
        for start, size in chunks:
            weights = jnp.exp2(scores[:, start : start + size] * TO_BITS - top).astype(jnp.bfloat16)
            summed += jnp.dot(weights, values[start : start + size, :], preferred_element_type=jnp.float32)
        total = summed[:, HD:]
        out[:, :BLOCK, :] = (summed[:, :HD] / total).astype(jnp.bfloat16).reshape(STEP_BLOCKS, BLOCK, HD)
        level = (top + jnp.log2(total)).reshape(STEP_BLOCKS, BLOCK, HD)
        row = lax.broadcasted_iota(jnp.int32, (STEP_BLOCKS, BLOCK, HD), 1)
        lane = lax.broadcasted_iota(jnp.int32, (STEP_BLOCKS, BLOCK, HD), 2)
        level = jnp.sum(jnp.where(row == lane, level, 0.0), axis=1, keepdims=True)
        high = level.astype(jnp.bfloat16).astype(jnp.float32)
        rest = level - high
        middle = rest.astype(jnp.bfloat16).astype(jnp.float32)
        zeros = jnp.zeros((STEP_BLOCKS, 5, HD), jnp.float32)
        out[:, BLOCK:, :] = jnp.concatenate([high, middle, rest - middle, zeros], axis=1).astype(jnp.bfloat16)

    usual, larger = 2 * LINE, 2 * LINE + LINE // 2
    pl.when(count <= usual)(lambda: attend_to(usual))
    pl.when((count > usual) & (count <= larger))(lambda: attend_to(larger))
    pl.when(count > larger)(lambda: attend_to(MOST_PAGES))


def attend(place, page_slots, pieces, q):
    def whole(array):
        return pl.BlockSpec(array.shape, lambda i, *_: (0,) * array.ndim)

    wire = pl.BlockSpec((STEP_BLOCKS, WIRE, HD), lambda i, *_: (i, 0, 0))
    return call(
        attend_kernel,
        bf16(BLOCKS, WIRE, HD),
        megabytes=40,
        flops=2300000000,
        moved=5000000,
        grid_spec=pltpu.PrefetchScalarGridSpec(
            num_scalar_prefetch=2,
            grid=(BLOCKS // STEP_BLOCKS,),
            in_specs=[whole(piece) for piece in pieces] + [wire],
            out_specs=wire,
            scratch_shapes=[
                pltpu.VMEM((KEYS, HD), jnp.bfloat16),
                pltpu.VMEM((KEYS, 2 * HD), jnp.bfloat16),
                pltpu.VMEM((8, HD), jnp.float32),
                pltpu.VMEM((ROWS, KEYS), jnp.float32),
                pltpu.SMEM((1,), jnp.int32),
            ],
        ),
    )(place, page_slots, *pieces, q)


def combine_kernel(place, parts, kept, sent, merged_rows):
    core = place[0]
    tags = parts[:, BLOCK:, :].astype(jnp.float32)
    level = tags[:, 0:1, :] + tags[:, 1:2, :] + tags[:, 2:3, :]
    level = level.reshape(LINE, XN, 1, HD)
    weight = jnp.exp2(level - jnp.max(level, axis=0, keepdims=True))
    weight = weight / jnp.sum(weight, axis=0, keepdims=True)
    row = lax.broadcasted_iota(jnp.int32, (BLOCK, HD), 0)
    lane = lax.broadcasted_iota(jnp.int32, (BLOCK, HD), 1)
    for x in range(XN):
        merged = jnp.zeros((BLOCK, HD), jnp.float32)
        for line in range(LINE):
            column = jnp.sum(jnp.where(row == lane, weight[line, x], 0.0), axis=1, keepdims=True)
            merged += column * parts[line * XN + x, :BLOCK, :].astype(jnp.float32)
        merged_rows[x] = merged.astype(jnp.bfloat16)
    for target, owner in ((kept, core), (sent, 1 - core)):
        for t in range(OWN):
            for x in range(XN):
                first = pl.multiple_of((owner * OWN + t) * GROUP, GROUP)
                target[t, x] = merged_rows[x, pl.ds(first, GROUP), :]


def finish_kernel(place, kept, received, out):
    core = place[0]
    for array, parity in ((kept, core), (received, 1 - core)):
        for t in range(OWN):
            for x in range(XN):
                first = pl.multiple_of((CN * x + parity) * GROUP, GROUP)
                out[t, pl.ds(first, GROUP), :] = array[t, x]


def body(queries, new_keys, new_values, new_positions, hist_keys, hist_values, page_slots):
    z, y, x, core = (lax.axis_index(name).astype(jnp.int32) for name in ALL)
    place = jnp.stack([core, jnp.where(core == 0, z, y), x, z * YN + y])
    half = bf16(OWN, XN, GROUP, HD)
    kv, q_kept, q_sent = call(
        pack_kernel, (bf16(2, KV_ROWS, HD), half, half), in_specs=[SMEM, SMEM] + [VMEM] * 5
    )(
        place,
        new_positions,
        queries,
        hist_keys.reshape(HISTORY, HD),
        hist_values.reshape(HISTORY, HD),
        new_keys.reshape(NEWT, HD),
        new_values.reshape(NEWT, HD),
    )
    lower = lax.ppermute(kv, ALL, along(3))
    upper = lax.ppermute(kv, ALL, along(-3))
    q_received = lax.ppermute(q_sent, ALL, SWAP)
    q = call(spread_kernel, bf16(BLOCKS, WIRE, HD), in_specs=[SMEM, SMEM, VMEM, VMEM])(
        place, new_positions, q_kept, q_received
    )
    q = lax.all_to_all(q, ALL, split_axis=0, concat_axis=0, axis_index_groups=CROSS, tiled=True)
    three, two = call(join_kernel, (bf16(3, 2, KV_ROWS, HD), bf16(2, 2, KV_ROWS, HD)))(kv, lower, upper)
    below = lax.ppermute(three, ALL, along(1))
    above = lax.ppermute(two, ALL, along(-1))
    parts = attend(place, page_slots, (kv, lower, upper, below, above), q)
    parts = lax.all_to_all(parts, ALL, split_axis=0, concat_axis=0, axis_index_groups=CROSS, tiled=True)
    kept, sent = call(
        combine_kernel,
        (half, half),
        in_specs=[SMEM, VMEM],
        scratch_shapes=[pltpu.VMEM((XN, BLOCK, HD), jnp.bfloat16)],
    )(place, parts)
    received = lax.ppermute(sent, ALL, SWAP)
    return call(finish_kernel, bf16(OWN, HEADS, HD), in_specs=[SMEM, VMEM, VMEM])(place, kept, received)


def solution(mesh):
    split = Mesh(mesh.devices.reshape(ZN, YN, XN, CN), ALL)
    ctx, kvh = ("z", "y"), ("x", "c")
    in_specs = (
        P(ctx + kvh, None, None),
        P(ctx, kvh, None),
        P(ctx, kvh, None),
        P(ctx),
        P(ctx, None, kvh, None),
        P(ctx, None, kvh, None),
        P(),
    )
    return jax.shard_map(body, mesh=split, in_specs=in_specs, out_specs=P(ctx + kvh, None, None), check_vma=False)
```

time: 837 us -> 99.7 us (0.12)
  waiting for transfers between devices: 506 us -> 16.5 us
  starting transfers between devices: 132 us -> 38.8 us
  blocking collectives: 106 us -> 24.1 us
  matrix products: 39.4 us -> 0 us
  other arithmetic: 22.7 us -> 0.08 us
  local copies, waits for them, and re-layouts: 20.5 us -> 3.32 us
  Pallas kernels: 0 us -> 16.3 us
    ppermute x63 -> x6, waiting for transfers between devices: 506 us -> 16.5 us  [the longest x1 7.56 us: body(): lower = lax.ppermute(kv, ALL, along(3))]
    ppermute x63 -> x6, starting transfers between devices: 121 us -> 31.3 us  [the longest x1 8.79 us: body(): q_received = lax.ppermute(q_sent, ALL, SWAP)]
    all_to_all x1, blocking collectives: 83.9 us -> 24.1 us  [body(): lax.all_to_all(parts, ALL, split_axis=0, concat_axis=0, axis_index_groups...]
    dot_general x128 -> x0, matrix products: 39.4 us -> none  [the longest x64 19.8 us: attend(): jnp.einsum('tgqd,kgd->tgqk', grouped, kv_block[0], preferred_element_type...]
    unnamed x1 -> x0, blocking collectives: 22.2 us -> none
    pallas_call x0 -> x6, Pallas kernels: none -> 16.3 us  [the longest x1 11.9 us: attend(): call(attend_kernel, bf16(BLOCKS, WIRE, HD), megabytes=40, flops=230000000...]
    reduce_sum x64 -> x0, other arithmetic: 15.8 us -> none  [attend(): row_total = row_total * factor + jnp.sum(weights, axis=-1)]
    dynamic_slice x128 -> x0, local copies, waits for them, and re-layouts: 9.77 us -> none  [the longest x64 5.05 us: history_seen(): live = lax.dynamic_slice_in_dim(live_slots, source * slots_dev, slots_dev)]
  transfers between devices with their start and end apart: 64 -> 7, of which waited for: 63 -> 4; matrix products, arithmetic and copies ran while one was open for 3% -> 0% of each run, Pallas kernels for 0% -> 0%
where the time goes in v2:
time: 99.7 us; the launch traced here: 99.2 us
  starting transfers between devices  38.8 us (39%)
  blocking collectives  24.1 us (24%)
  waiting for transfers between devices  16.5 us (17%)
  Pallas kernels  16.3 us (16%)
  local copies, waits for them, and re-layouts  3.32 us (3%)
    all_to_all x1, blocking collectives, body(): lax.all_to_all(parts, ALL, split_axis=0, concat_axis=0, axis_index_groups...  24.1 us
    pallas_call x1, Pallas kernels, attend(): call(attend_kernel, bf16(BLOCKS, WIRE, HD), megabytes=40, flops=230000000...  11.9 us
    ppermute x1, starting transfers between devices, body(): q_received = lax.ppermute(q_sent, ALL, SWAP)  8.79 us
    ppermute x1, starting transfers between devices, body(): below = lax.ppermute(three, ALL, along(1))  7.64 us
    ppermute x1, waiting for transfers between devices, body(): lower = lax.ppermute(kv, ALL, along(3))  7.56 us
    all_to_all x1, starting transfers between devices, body(): lax.all_to_all(q, ALL, split_axis=0, concat_axis=0, axis_index_groups=CRO...  7.51 us
    ppermute x1, waiting for transfers between devices, body(): above = lax.ppermute(two, ALL, along(-1))  7.24 us
    ppermute x1, starting transfers between devices, body(): lower = lax.ppermute(kv, ALL, along(3))  5.23 us
  transfers between devices with their start and end apart: 7, of which 4 were waited for; matrix products, arithmetic and copies ran while one was open for 0% of the time, Pallas kernels for 0%

profile of v2, /device:TPU:1, one launch (start us, length us, event | category | flops | bytes accessed | tf_op | source)
XLA Modules:
  0.0 99.2 jit_solution(2041105261577900986)
XLA Ops:
  0.0 0.0 copy-start.4
  0.0 0.1 pad_add_fusion.place
  0.1 0.0 copy-start.3
  0.1 0.6 copy-done.4
  0.7 0.1 copy-done.3
  0.8 0.0 copy-done.5
  0.8 0.9 copy-done
  1.7 0.9 copy-done.1
  2.6 0.8 copy-done.2
  3.4 0.6 shard_map.73
  4.1 8.8 %collective-permute-start.4 = (bf16[2,4,16,128]{3,2,1,0:T(8,128)(2,1)S(1)}, bf16[2,4,16,128]{3,2,1,0:T(8,128)(2,1)S(1)}, u32[]{:S(2)}, u32[]{:S(2)}) collective-permute-start(bf16[2,4,16,128]{3,2,1,0:T(8,128)(2,1)S(1)} %get-tuple-element.16), channel_id=1, source_target_pairs={{0,1},{1,0},{2,3},{3,2},{4,5},{5,4},{6,7},{7,6},{8,9},{9,8},{10,11... | collective-permute-start | bytes 98312 | tf_op jit(solution)/shard_map/ppermute | solution.py:282
  12.8 0.8 collective-permute-done.4.received
  13.7 1.5 %shard_map.75 = bf16[32,72,128]{2,1,0:T(8,128)(2,1)} custom-call(s32[4]{0:T(128)S(1)} %pad_add_fusion.place, s32[16]{0:T(128)S(1)} %copy-done.5, bf16[2,4,16,128]{3,2,1,0:T(8,128)(2,1)S(1)} %get-tuple-element.15.kept, bf16[2,4,16,128]{3,2,1,0:T(8,128)(2,1)S(1)} %collective-permute-done.4.received), custom_call_target="tpu_custom_call" | custom-call | flops 1000000 | bytes 800000 | tf_op jit(solution)/shard_map/pallas_call | solution.py:283
  15.1 7.5 %all-to-all-start = ((bf16[32,72,128]{2,1,0:T(8,128)(2,1)}), bf16[32,72,128]{2,1,0:T(8,128)(2,1)S(1)}, u32[]{:S(2)}, u32[]{:S(2)}) async-start(bf16[32,72,128]{2,1,0:T(8,128)(2,1)} %shard_map.75), calls=%async_computation | async-start | bytes 1179648 | tf_op jit(solution)/shard_map/all_to_all | solution.py:286
  22.7 5.2 %collective-permute-start = (bf16[2,416,128]{2,1,0:T(8,128)(2,1)S(1)}, bf16[2,416,128]{2,1,0:T(8,128)(2,1)S(1)}, u32[]{:S(2)}, u32[]{:S(2)}) collective-permute-start(bf16[2,416,128]{2,1,0:T(8,128)(2,1)S(1)} %get-tuple-element.12.own), channel_id=1, source_target_pairs={{0,192},{1,25},{2,194},{3,27},{4,196},{5,29},{6,198},{7,31},{8,200... | collective-permute-start | bytes 638984 | tf_op jit(solution)/shard_map/ppermute | solution.py:280
  27.9 3.4 %collective-permute-start.1 = (bf16[2,416,128]{2,1,0:T(8,128)(2,1)S(1)}, bf16[2,416,128]{2,1,0:T(8,128)(2,1)S(1)}, u32[]{:S(2)}, u32[]{:S(2)}) collective-permute-start(bf16[2,416,128]{2,1,0:T(8,128)(2,1)S(1)} %get-tuple-element.12.own), channel_id=1, source_target_pairs={{0,320},{1,41},{2,322},{3,43},{4,324},{5,45},{6,326},{7,47},{8,328... | collective-permute-start | bytes 638984 | tf_op jit(solution)/shard_map/ppermute | solution.py:281
  31.3 7.6 %collective-permute-done.lower = bf16[2,416,128]{2,1,0:T(8,128)(2,1)S(1)} collective-permute-done((bf16[2,416,128]{2,1,0:T(8,128)(2,1)S(1)}, bf16[2,416,128]{2,1,0:T(8,128)(2,1)S(1)}, u32[]{:S(2)}, u32[]{:S(2)}) %collective-permute-start) | collective-permute-done | bytes 213024 | tf_op jit(solution)/shard_map/ppermute | solution.py:280
  38.8 0.0 collective-permute-done.1.upper
  38.8 0.1 shard_map.74
  39.0 0.0 copy-start.6
  39.0 7.6 %collective-permute-start.2 = (bf16[3,2,416,128]{3,2,1,0:T(8,128)(2,1)S(1)}, bf16[3,2,416,128]{3,2,1,0:T(8,128)(2,1)S(1)}, u32[]{:S(2)}, u32[]{:S(2)}) collective-permute-start(bf16[3,2,416,128]{3,2,1,0:T(8,128)(2,1)S(1)} %get-tuple-element.13), channel_id=1, source_target_pairs={{0,64},{1,9},{2,66},{3,11},{4,68},{5,13},{6,70},{7,15},{8,72},{9,1... | collective-permute-start | bytes 1916936 | tf_op jit(solution)/shard_map/ppermute | solution.py:288
  46.6 1.9 %collective-permute-start.3 = (bf16[2,2,416,128]{3,2,1,0:T(8,128)(2,1)S(1)}, bf16[2,2,416,128]{3,2,1,0:T(8,128)(2,1)S(1)}, u32[]{:S(2)}, u32[]{:S(2)}) collective-permute-start(bf16[2,2,416,128]{3,2,1,0:T(8,128)(2,1)S(1)} %get-tuple-element.14), channel_id=1, source_target_pairs={{0,448},{1,57},{2,450},{3,59},{4,452},{5,61},{6,454},{7,63},{8,456... | collective-permute-start | bytes 1277960 | tf_op jit(solution)/shard_map/ppermute | solution.py:289
  48.6 7.2 %collective-permute-done.3.above = bf16[2,2,416,128]{3,2,1,0:T(8,128)(2,1)S(1)} collective-permute-done((bf16[2,2,416,128]{3,2,1,0:T(8,128)(2,1)S(1)}, bf16[2,2,416,128]{3,2,1,0:T(8,128)(2,1)S(1)}, u32[]{:S(2)}, u32[]{:S(2)}) %collective-permute-start.3) | collective-permute-done | bytes 426016 | tf_op jit(solution)/shard_map/ppermute | solution.py:289
  55.8 0.0 collective-permute-done.2.below
  55.8 0.0 all-to-all-done.q
  55.8 0.0 copy-done.6
  55.8 11.9 %shard_map.76 = bf16[32,72,128]{2,1,0:T(8,128)(2,1)S(1)} custom-call(s32[4]{0:T(128)S(1)} %pad_add_fusion.place, s32[128]{0:T(128)S(1)} %copy-done.6, bf16[2,416,128]{2,1,0:T(8,128)(2,1)S(1)} %get-tuple-element.12.own, bf16[2,416,128]{2,1,0:T(8,128)(2,1)S(1)} %collective-permute-done.lower, bf16[2,416,128]{2,1,0:T(8,128)(2,1)S(1)} %collective-permute-done.1.upper, ...), custom_call_target="tpu_custom_call" | custom-call | flops 2300000000 | bytes 5000000 | tf_op jit(solution)/shard_map/pallas_call | solution.py:212
  67.7 24.1 %all_to_all.10.parts = bf16[32,72,128]{2,1,0:T(8,128)(2,1)S(1)} all-to-all(bf16[32,72,128]{2,1,0:T(8,128)(2,1)S(1)} %shard_map.76), channel_id=1, replica_groups={{0,2,4,6,8,10,12,14,16,18,20,22,24,26,28,30,32,34,36,38,40,42,44,46,48,..., dimensions={0} | all-to-all | bytes 1179648 | tf_op jit(solution)/shard_map/all_to_all | solution.py:291
  91.9 0.9 shard_map.77
  92.8 4.4 %collective-permute-start.5 = (bf16[2,4,16,128]{3,2,1,0:T(8,128)(2,1)S(1)}, bf16[2,4,16,128]{3,2,1,0:T(8,128)(2,1)S(1)}, u32[]{:S(2)}, u32[]{:S(2)}) collective-permute-start(bf16[2,4,16,128]{3,2,1,0:T(8,128)(2,1)S(1)} %get-tuple-element.18), channel_id=1, source_target_pairs={{0,1},{1,0},{2,3},{3,2},{4,5},{5,4},{6,7},{7,6},{8,9},{9,8},{10,11... | collective-permute-start | bytes 98312 | tf_op jit(solution)/shard_map/ppermute | solution.py:298
  97.2 0.8 collective-permute-done.5.received
  98.0 1.2 %shard_map.78 = bf16[2,128,128]{2,1,0:T(8,128)(2,1)} custom-call(s32[4]{0:T(128)S(1)} %pad_add_fusion.place, bf16[2,4,16,128]{3,2,1,0:T(8,128)(2,1)S(1)} %get-tuple-element.17.kept, bf16[2,4,16,128]{3,2,1,0:T(8,128)(2,1)S(1)} %collective-permute-done.5.received), custom_call_target="tpu_custom_call" | custom-call | flops 1000000 | bytes 800000 | tf_op jit(solution)/shard_map/pallas_call | solution.py:299
  (4 shorter events, 0.0 us)
Async XLA Ops:
  0.0 0.7 copy-start.4
  0.1 0.7 copy-start.3
  0.1 0.7 copy-start.5
  0.8 0.9 copy-start
  1.7 0.9 copy-start.1
  2.6 0.8 copy-start.2
  4.1 9.6 %collective-permute-start.4 = (bf16[2,4,16,128]{3,2,1,0:T(8,128)(2,1)S(1)}, bf16[2,4,16,128]{3,2,1,0:T(8,128)(2,1)S(1)}, u32[]{:S(2)}, u32[]{:S(2)}) collective-permute-start(bf16[2,4,16,128]{3,2,1,0:T(8,128)(2,1)S(1)} %get-tuple-element.16), channel_id=1, source_target_pairs={{0,1},{1,0},{2,3},{3,2},{4,5},{5,4},{6,7},{7,6},{8,9},{9,8},{10,11... | collective-permute-start | bytes 98312 | tf_op jit(solution)/shard_map/ppermute | solution.py:282
  15.1 40.7 %all-to-all-start = ((bf16[32,72,128]{2,1,0:T(8,128)(2,1)}), bf16[32,72,128]{2,1,0:T(8,128)(2,1)S(1)}, u32[]{:S(2)}, u32[]{:S(2)}) async-start(bf16[32,72,128]{2,1,0:T(8,128)(2,1)} %shard_map.75), calls=%async_computation | async-start | bytes 1179648 | tf_op jit(solution)/shard_map/all_to_all | solution.py:286
  22.7 16.2 %collective-permute-start = (bf16[2,416,128]{2,1,0:T(8,128)(2,1)S(1)}, bf16[2,416,128]{2,1,0:T(8,128)(2,1)S(1)}, u32[]{:S(2)}, u32[]{:S(2)}) collective-permute-start(bf16[2,416,128]{2,1,0:T(8,128)(2,1)S(1)} %get-tuple-element.12.own), channel_id=1, source_target_pairs={{0,192},{1,25},{2,194},{3,27},{4,196},{5,29},{6,198},{7,31},{8,200... | collective-permute-start | bytes 638984 | tf_op jit(solution)/shard_map/ppermute | solution.py:280
  27.9 10.9 %collective-permute-start.1 = (bf16[2,416,128]{2,1,0:T(8,128)(2,1)S(1)}, bf16[2,416,128]{2,1,0:T(8,128)(2,1)S(1)}, u32[]{:S(2)}, u32[]{:S(2)}) collective-permute-start(bf16[2,416,128]{2,1,0:T(8,128)(2,1)S(1)} %get-tuple-element.12.own), channel_id=1, source_target_pairs={{0,320},{1,41},{2,322},{3,43},{4,324},{5,45},{6,326},{7,47},{8,328... | collective-permute-start | bytes 638984 | tf_op jit(solution)/shard_map/ppermute | solution.py:281
  39.0 16.8 %copy-start.6 = (s32[128]{0:T(128)S(1)}, s32[128]{0:T(128)}, u32[]{:S(2)}) copy-start(s32[128]{0:T(128)} %page_slots.1) | copy-start | bytes 1540
  39.0 16.8 %collective-permute-start.2 = (bf16[3,2,416,128]{3,2,1,0:T(8,128)(2,1)S(1)}, bf16[3,2,416,128]{3,2,1,0:T(8,128)(2,1)S(1)}, u32[]{:S(2)}, u32[]{:S(2)}) collective-permute-start(bf16[3,2,416,128]{3,2,1,0:T(8,128)(2,1)S(1)} %get-tuple-element.13), channel_id=1, source_target_pairs={{0,64},{1,9},{2,66},{3,11},{4,68},{5,13},{6,70},{7,15},{8,72},{9,1... | collective-permute-start | bytes 1916936 | tf_op jit(solution)/shard_map/ppermute | solution.py:288
  46.6 9.2 %collective-permute-start.3 = (bf16[2,2,416,128]{3,2,1,0:T(8,128)(2,1)S(1)}, bf16[2,2,416,128]{3,2,1,0:T(8,128)(2,1)S(1)}, u32[]{:S(2)}, u32[]{:S(2)}) collective-permute-start(bf16[2,2,416,128]{3,2,1,0:T(8,128)(2,1)S(1)} %get-tuple-element.14), channel_id=1, source_target_pairs={{0,448},{1,57},{2,450},{3,59},{4,452},{5,61},{6,454},{7,63},{8,456... | collective-permute-start | bytes 1277960 | tf_op jit(solution)/shard_map/ppermute | solution.py:289
  92.8 5.2 %collective-permute-start.5 = (bf16[2,4,16,128]{3,2,1,0:T(8,128)(2,1)S(1)}, bf16[2,4,16,128]{3,2,1,0:T(8,128)(2,1)S(1)}, u32[]{:S(2)}, u32[]{:S(2)}) collective-permute-start(bf16[2,4,16,128]{3,2,1,0:T(8,128)(2,1)S(1)} %get-tuple-element.18), channel_id=1, source_target_pairs={{0,1},{1,0},{2,3},{3,2},{4,5},{5,4},{6,7},{7,6},{8,9},{9,8},{10,11... | collective-permute-start | bytes 98312 | tf_op jit(solution)/shard_map/ppermute | solution.py:298

commit v3 on v2

--- a/solution.py
+++ b/solution.py
@@ -61,25 +61,34 @@
 
 
 SMEM = pl.BlockSpec(memory_space=pltpu.SMEM)
+HBM = pl.BlockSpec(memory_space=pltpu.HBM)
 VMEM = pl.BlockSpec(memory_space=pltpu.VMEM)
 
 
-def pack_kernel(place, positions, queries, hist_keys, hist_values, new_keys, new_values, kv, kept, sent):
+def pack_kernel(
+    place, positions, queries, hist_keys, hist_values, new_keys, new_values, kv, kept, sent, tags, arrived
+):
     core, line = place[0], place[1]
-    for side, (history, fresh) in enumerate(((hist_keys, new_keys), (hist_values, new_values))):
-        kv[side, :HISTORY, :] = history[...]
-        kv[side, HISTORY : HISTORY + NEWT, :] = fresh[...]
-        lane = lax.broadcasted_iota(jnp.int32, (NEWT, HD), 1)
-        tag = jnp.zeros((NEWT, HD), jnp.int32)
-        for i in range(NEWT):
-            digit = positions[i] // 32 if side == 0 else positions[i] % 32
-            tag = jnp.where(lane == line * NEWT + i, digit, tag)
-        kv[side, HISTORY + NEWT :, :] = tag.astype(jnp.float32).astype(jnp.bfloat16)
-    for target, parity in ((kept, core), (sent, 1 - core)):
-        for t in range(OWN):
-            for x in range(XN):
-                first = pl.multiple_of((CN * x + parity) * GROUP, GROUP)
-                target[t, x] = queries[t, pl.ds(first, GROUP), :]
+    copies = [
+        pltpu.make_async_copy(hist_keys, kv.at[0, pl.ds(0, HISTORY)], arrived.at[0]),
+        pltpu.make_async_copy(hist_values, kv.at[1, pl.ds(0, HISTORY)], arrived.at[1]),
+        pltpu.make_async_copy(new_keys, kv.at[0, pl.ds(HISTORY, NEWT)], arrived.at[2]),
+        pltpu.make_async_copy(new_values, kv.at[1, pl.ds(HISTORY, NEWT)], arrived.at[3]),
+        pltpu.make_async_copy(queries.at[:, :, core], kept, arrived.at[4]),
+        pltpu.make_async_copy(queries.at[:, :, 1 - core], sent, arrived.at[5]),
+    ]
+    for copy in copies:
+        copy.start()
+    lane = lax.broadcasted_iota(jnp.int32, (NEWT, HD), 1)
+    tag = jnp.zeros((NEWT, HD), jnp.int32)
+    for i in range(NEWT):
+        tag = jnp.where(lane == line * NEWT + i, positions[i], tag)
+    for side, digit in enumerate((tag // 32, tag % 32)):
+        tags[side] = digit.astype(jnp.float32).astype(jnp.bfloat16)
+    last = pltpu.make_async_copy(tags, kv.at[:, pl.ds(HISTORY + NEWT, NEWT)], arrived.at[6])
+    last.start()
+    for copy in copies + [last]:
+        copy.wait()
 
 
 def spread_kernel(place, positions, kept, received, out):
@@ -267,11 +276,16 @@
     place = jnp.stack([core, jnp.where(core == 0, z, y), x, z * YN + y])
     half = bf16(OWN, XN, GROUP, HD)
     kv, q_kept, q_sent = call(
-        pack_kernel, (bf16(2, KV_ROWS, HD), half, half), in_specs=[SMEM, SMEM] + [VMEM] * 5
+        pack_kernel,
+        (bf16(2, KV_ROWS, HD), half, half),
+        in_specs=[SMEM, SMEM] + [HBM] * 5,
+        out_specs=(HBM, HBM, HBM),
+        scratch_shapes=[pltpu.VMEM((2, NEWT, HD), jnp.bfloat16), pltpu.SemaphoreType.DMA((7,))],
+        megabytes=56,
     )(
         place,
         new_positions,
-        queries,
+        queries.reshape(OWN, XN, CN, GROUP, HD),
         hist_keys.reshape(HISTORY, HD),
         hist_values.reshape(HISTORY, HD),
         new_keys.reshape(NEWT, HD),
@@ -283,8 +297,9 @@
     q = call(spread_kernel, bf16(BLOCKS, WIRE, HD), in_specs=[SMEM, SMEM, VMEM, VMEM])(
         place, new_positions, q_kept, q_received
     )
+    three, two = call(join_kernel, (bf16(3, 2, KV_ROWS, HD), bf16(2, 2, KV_ROWS, HD)))(kv, lower, upper)
+    q, three, two = lax.optimization_barrier((q, three, two))
     q = lax.all_to_all(q, ALL, split_axis=0, concat_axis=0, axis_index_groups=CROSS, tiled=True)
-    three, two = call(join_kernel, (bf16(3, 2, KV_ROWS, HD), bf16(2, 2, KV_ROWS, HD)))(kv, lower, upper)
     below = lax.ppermute(three, ALL, along(1))
     above = lax.ppermute(two, ALL, along(-1))
     parts = attend(place, page_slots, (kv, lower, upper, below, above), q)

time: 99.7 us -> 103 us (1.033)
  Pallas kernels: 16.3 us -> 30 us
  blocking collectives: 24.1 us -> 17.4 us
  local copies, waits for them, and re-layouts: 3.32 us -> 0.78 us
  starting transfers between devices: 38.8 us -> 37.4 us
    pallas_call x1, Pallas kernels: 0.65 us -> 10 us  [body(): call(pack_kernel, (bf16(2, KV_ROWS, HD), half, half), in_specs=[SMEM, SME...]
    all_to_all x1, blocking collectives: 24.1 us -> 17.4 us  [body(): lax.all_to_all(parts, ALL, split_axis=0, concat_axis=0, axis_index_groups...]
    ppermute x1, starting transfers between devices: 7.64 us -> 1.92 us  [body(): below = lax.ppermute(three, ALL, along(1))]
    ppermute x1, waiting for transfers between devices: 7.56 us -> 2.05 us  [body(): lower = lax.ppermute(kv, ALL, along(3))]
    all_to_all x1, starting transfers between devices: 7.51 us -> 12.6 us  [body(): lax.all_to_all(q, ALL, split_axis=0, concat_axis=0, axis_index_groups=CRO...]
    pallas_call x1, Pallas kernels: 11.9 us -> 16.3 us  [attend(): call(attend_kernel, bf16(BLOCKS, WIRE, HD), megabytes=40, flops=230000000...]
    ppermute x1, starting transfers between devices: 3.36 us -> 7.5 us  [body(): upper = lax.ppermute(kv, ALL, along(-3))]
    ppermute x1, starting transfers between devices: 5.23 us -> 1.92 us  [body(): lower = lax.ppermute(kv, ALL, along(3))]
  transfers between devices with their start and end apart: 7 -> 7, of which waited for: 4 -> 5; matrix products, arithmetic and copies ran while one was open for 0% -> 0% of each run, Pallas kernels for 0% -> 1%
where the time goes in v3:
time: 103 us
  starting transfers between devices  37.4 us (36%)
  Pallas kernels  30 us (29%)
  blocking collectives  17.4 us (17%)
  waiting for transfers between devices  16.7 us (16%)
    all_to_all x1, blocking collectives, body(): lax.all_to_all(parts, ALL, split_axis=0, concat_axis=0, axis_index_groups...  17.4 us
    pallas_call x1, Pallas kernels, attend(): call(attend_kernel, bf16(BLOCKS, WIRE, HD), megabytes=40, flops=230000000...  16.3 us
    all_to_all x1, starting transfers between devices, body(): lax.all_to_all(q, ALL, split_axis=0, concat_axis=0, axis_index_groups=CRO...  12.6 us
    pallas_call x1, Pallas kernels, body(): call(pack_kernel, (bf16(2, KV_ROWS, HD), half, half), in_specs=[SMEM, SME...  10 us
    ppermute x1, waiting for transfers between devices, body(): above = lax.ppermute(two, ALL, along(-1))  9.91 us
    ppermute x1, starting transfers between devices, body(): upper = lax.ppermute(kv, ALL, along(-3))  7.5 us
    ppermute x1, starting transfers between devices, body(): q_received = lax.ppermute(q_sent, ALL, SWAP)  7.01 us
    ppermute x1, starting transfers between devices, body(): above = lax.ppermute(two, ALL, along(-1))  4.57 us
  transfers between devices with their start and end apart: 7, of which 5 were waited for; matrix products, arithmetic and copies ran while one was open for 0% of the time, Pallas kernels for 1%

profile of v3, /device:TPU:1, one launch (start us, length us, event | category | flops | bytes accessed | tf_op | source)
XLA Modules:
  0.0 103.0 jit_solution(8131962630058792389)
XLA Ops:
  0.0 0.6 pad_add_fusion.place
  0.6 10.0 %shard_map.73 = (bf16[2,416,128]{2,1,0:T(8,128)(2,1)}, bf16[2,4,16,128]{3,2,1,0:T(8,128)(2,1)}, bf16[2,4,16,128]{3,2,1,0:T(8,128)(2,1)}) custom-call(s32[4]{0:T(128)} %pad_add_fusion.place, s32[16]{0:T(128)} %positions.3, bf16[2,4,2,16,128]{4,3,2,1,0:T(8,128)(2,1)} %bitcast.11, bf16[384,128]{1,0:T(8,128)(2,1)} %bitcast.9, bf16[384,128]{1,0:T(8,128)(2,1)} %bitcast.10, ...), custom_call_target="tpu_custom_call" | custom-call | flops 1000000 | bytes 800000 | tf_op jit(solution)/shard_map/pallas_call | solution.py:278
  10.6 7.5 %collective-permute-start.1 = (bf16[2,416,128]{2,1,0:T(8,128)(2,1)}, bf16[2,416,128]{2,1,0:T(8,128)(2,1)S(1)}, u32[]{:S(2)}, u32[]{:S(2)}) collective-permute-start(bf16[2,416,128]{2,1,0:T(8,128)(2,1)} %get-tuple-element.15.own), channel_id=1, source_target_pairs={{0,320},{1,41},{2,322},{3,43},{4,324},{5,45},{6,326},{7,47},{8,328... | collective-permute-start | bytes 638984 | tf_op jit(solution)/shard_map/ppermute | solution.py:295
  18.1 1.9 %collective-permute-start = (bf16[2,416,128]{2,1,0:T(8,128)(2,1)}, bf16[2,416,128]{2,1,0:T(8,128)(2,1)S(1)}, u32[]{:S(2)}, u32[]{:S(2)}) collective-permute-start(bf16[2,416,128]{2,1,0:T(8,128)(2,1)} %get-tuple-element.15.own), channel_id=1, source_target_pairs={{0,192},{1,25},{2,194},{3,27},{4,196},{5,29},{6,198},{7,31},{8,200... | collective-permute-start | bytes 638984 | tf_op jit(solution)/shard_map/ppermute | solution.py:294
  20.0 0.0 copy-start.2
  20.0 0.0 copy-start.3
  20.0 7.0 %collective-permute-start.2 = (bf16[2,4,16,128]{3,2,1,0:T(8,128)(2,1)}, bf16[2,4,16,128]{3,2,1,0:T(8,128)(2,1)S(1)}, u32[]{:S(2)}, u32[]{:S(2)}) collective-permute-start(bf16[2,4,16,128]{3,2,1,0:T(8,128)(2,1)} %get-tuple-element.17), channel_id=1, source_target_pairs={{0,1},{1,0},{2,3},{3,2},{4,5},{5,4},{6,7},{7,6},{8,9},{9,8},{10,11... | collective-permute-start | bytes 98312 | tf_op jit(solution)/shard_map/ppermute | solution.py:296
  27.1 1.0 %collective-permute-done.2.received = bf16[2,4,16,128]{3,2,1,0:T(8,128)(2,1)S(1)} collective-permute-done((bf16[2,4,16,128]{3,2,1,0:T(8,128)(2,1)}, bf16[2,4,16,128]{3,2,1,0:T(8,128)(2,1)S(1)}, u32[]{:S(2)}, u32[]{:S(2)}) %collective-permute-start.2) | collective-permute-done | bytes 32800 | tf_op jit(solution)/shard_map/ppermute | solution.py:296
  28.1 0.0 copy-done.2
  28.1 0.0 copy-done.3
  28.1 0.0 copy-start.1
  28.1 0.8 copy-done.1
  28.9 0.0 copy-start
  28.9 1.5 %shard_map.74 = bf16[32,72,128]{2,1,0:T(8,128)(2,1)} custom-call(s32[4]{0:T(128)S(1)} %copy-done.2, s32[16]{0:T(128)S(1)} %copy-done.3, bf16[2,4,16,128]{3,2,1,0:T(8,128)(2,1)S(1)} %copy-done.1, bf16[2,4,16,128]{3,2,1,0:T(8,128)(2,1)S(1)} %collective-permute-done.2.received), custom_call_target="tpu_custom_call" | custom-call | flops 1000000 | bytes 800000 | tf_op jit(solution)/shard_map/pallas_call | solution.py:297
  30.3 0.0 collective-permute-done.1.upper
  30.3 2.0 %collective-permute-done.lower = bf16[2,416,128]{2,1,0:T(8,128)(2,1)S(1)} collective-permute-done((bf16[2,416,128]{2,1,0:T(8,128)(2,1)}, bf16[2,416,128]{2,1,0:T(8,128)(2,1)S(1)}, u32[]{:S(2)}, u32[]{:S(2)}) %collective-permute-start) | collective-permute-done | bytes 213024 | tf_op jit(solution)/shard_map/ppermute | solution.py:294
  32.4 0.0 copy-done
  32.4 0.1 shard_map.75
  32.5 0.0 copy-start.4
  32.5 12.6 %all-to-all-start = ((bf16[32,72,128]{2,1,0:T(8,128)(2,1)}), bf16[32,72,128]{2,1,0:T(8,128)(2,1)S(1)}, u32[]{:S(2)}, u32[]{:S(2)}) async-start(bf16[32,72,128]{2,1,0:T(8,128)(2,1)} %shard_map.74), calls=%async_computation | async-start | bytes 1179648 | tf_op jit(solution)/shard_map/all_to_all | solution.py:302
  45.1 1.9 %collective-permute-start.3 = (bf16[3,2,416,128]{3,2,1,0:T(8,128)(2,1)S(1)}, bf16[3,2,416,128]{3,2,1,0:T(8,128)(2,1)S(1)}, u32[]{:S(2)}, u32[]{:S(2)}) collective-permute-start(bf16[3,2,416,128]{3,2,1,0:T(8,128)(2,1)S(1)} %get-tuple-element.20), channel_id=1, source_target_pairs={{0,64},{1,9},{2,66},{3,11},{4,68},{5,13},{6,70},{7,15},{8,72},{9,1... | collective-permute-start | bytes 1916936 | tf_op jit(solution)/shard_map/ppermute | solution.py:303
  47.1 4.6 %collective-permute-start.4 = (bf16[2,2,416,128]{3,2,1,0:T(8,128)(2,1)S(1)}, bf16[2,2,416,128]{3,2,1,0:T(8,128)(2,1)S(1)}, u32[]{:S(2)}, u32[]{:S(2)}) collective-permute-start(bf16[2,2,416,128]{3,2,1,0:T(8,128)(2,1)S(1)} %get-tuple-element.21), channel_id=1, source_target_pairs={{0,448},{1,57},{2,450},{3,59},{4,452},{5,61},{6,454},{7,63},{8,456... | collective-permute-start | bytes 1277960 | tf_op jit(solution)/shard_map/ppermute | solution.py:304
  51.6 9.9 %collective-permute-done.4.above = bf16[2,2,416,128]{3,2,1,0:T(8,128)(2,1)S(1)} collective-permute-done((bf16[2,2,416,128]{3,2,1,0:T(8,128)(2,1)S(1)}, bf16[2,2,416,128]{3,2,1,0:T(8,128)(2,1)S(1)}, u32[]{:S(2)}, u32[]{:S(2)}) %collective-permute-start.4) | collective-permute-done | bytes 426016 | tf_op jit(solution)/shard_map/ppermute | solution.py:304
  61.6 2.5 %collective-permute-done.3.below = bf16[3,2,416,128]{3,2,1,0:T(8,128)(2,1)S(1)} collective-permute-done((bf16[3,2,416,128]{3,2,1,0:T(8,128)(2,1)S(1)}, bf16[3,2,416,128]{3,2,1,0:T(8,128)(2,1)S(1)}, u32[]{:S(2)}, u32[]{:S(2)}) %collective-permute-start.3) | collective-permute-done | bytes 639008 | tf_op jit(solution)/shard_map/ppermute | solution.py:303
  64.1 0.0 all-to-all-done.q
  64.1 0.0 copy-done.4
  64.1 16.3 %shard_map.76 = bf16[32,72,128]{2,1,0:T(8,128)(2,1)S(1)} custom-call(s32[4]{0:T(128)S(1)} %copy-done.2, s32[128]{0:T(128)S(1)} %copy-done.4, bf16[2,416,128]{2,1,0:T(8,128)(2,1)S(1)} %copy-done, bf16[2,416,128]{2,1,0:T(8,128)(2,1)S(1)} %collective-permute-done.lower, bf16[2,416,128]{2,1,0:T(8,128)(2,1)S(1)} %collective-permute-done.1.upper, ...), custom_call_target="tpu_custom_call" | custom-call | flops 2300000000 | bytes 5000000 | tf_op jit(solution)/shard_map/pallas_call | solution.py:221
  80.3 17.4 %all_to_all.10.parts = bf16[32,72,128]{2,1,0:T(8,128)(2,1)S(1)} all-to-all(bf16[32,72,128]{2,1,0:T(8,128)(2,1)S(1)} %shard_map.76), channel_id=1, replica_groups={{0,2,4,6,8,10,12,14,16,18,20,22,24,26,28,30,32,34,36,38,40,42,44,46,48,..., dimensions={0} | all-to-all | bytes 1179648 | tf_op jit(solution)/shard_map/all_to_all | solution.py:306
  97.8 0.9 shard_map.77
  98.7 1.9 %collective-permute-start.5 = (bf16[2,4,16,128]{3,2,1,0:T(8,128)(2,1)S(1)}, bf16[2,4,16,128]{3,2,1,0:T(8,128)(2,1)S(1)}, u32[]{:S(2)}, u32[]{:S(2)}) collective-permute-start(bf16[2,4,16,128]{3,2,1,0:T(8,128)(2,1)S(1)} %get-tuple-element.24), channel_id=1, source_target_pairs={{0,1},{1,0},{2,3},{3,2},{4,5},{5,4},{6,7},{7,6},{8,9},{9,8},{10,11... | collective-permute-start | bytes 98312 | tf_op jit(solution)/shard_map/ppermute | solution.py:313
  100.7 1.2 %collective-permute-done.5.received = bf16[2,4,16,128]{3,2,1,0:T(8,128)(2,1)S(1)} collective-permute-done((bf16[2,4,16,128]{3,2,1,0:T(8,128)(2,1)S(1)}, bf16[2,4,16,128]{3,2,1,0:T(8,128)(2,1)S(1)}, u32[]{:S(2)}, u32[]{:S(2)}) %collective-permute-start.5) | collective-permute-done | bytes 32800 | tf_op jit(solution)/shard_map/ppermute | solution.py:313
  101.8 1.2 %shard_map.78 = bf16[2,128,128]{2,1,0:T(8,128)(2,1)} custom-call(s32[4]{0:T(128)S(1)} %copy-done.2, bf16[2,4,16,128]{3,2,1,0:T(8,128)(2,1)S(1)} %get-tuple-element.23.kept, bf16[2,4,16,128]{3,2,1,0:T(8,128)(2,1)S(1)} %collective-permute-done.5.received), custom_call_target="tpu_custom_call" | custom-call | flops 1000000 | bytes 800000 | tf_op jit(solution)/shard_map/pallas_call | solution.py:314
Async XLA Ops:
  10.6 19.7 %collective-permute-start.1 = (bf16[2,416,128]{2,1,0:T(8,128)(2,1)}, bf16[2,416,128]{2,1,0:T(8,128)(2,1)S(1)}, u32[]{:S(2)}, u32[]{:S(2)}) collective-permute-start(bf16[2,416,128]{2,1,0:T(8,128)(2,1)} %get-tuple-element.15.own), channel_id=1, source_target_pairs={{0,320},{1,41},{2,322},{3,43},{4,324},{5,45},{6,326},{7,47},{8,328... | collective-permute-start | bytes 638984 | tf_op jit(solution)/shard_map/ppermute | solution.py:295
  18.1 14.3 %collective-permute-start = (bf16[2,416,128]{2,1,0:T(8,128)(2,1)}, bf16[2,416,128]{2,1,0:T(8,128)(2,1)S(1)}, u32[]{:S(2)}, u32[]{:S(2)}) collective-permute-start(bf16[2,416,128]{2,1,0:T(8,128)(2,1)} %get-tuple-element.15.own), channel_id=1, source_target_pairs={{0,192},{1,25},{2,194},{3,27},{4,196},{5,29},{6,198},{7,31},{8,200... | collective-permute-start | bytes 638984 | tf_op jit(solution)/shard_map/ppermute | solution.py:294
  20.0 8.1 %copy-start.2 = (s32[4]{0:T(128)S(1)}, s32[4]{0:T(128)}, u32[]{:S(2)}) copy-start(s32[4]{0:T(128)} %pad_add_fusion.place) | copy-start | bytes 52
  20.0 8.1 %copy-start.3 = (s32[16]{0:T(128)S(1)}, s32[16]{0:T(128)}, u32[]{:S(2)}) copy-start(s32[16]{0:T(128)} %positions.3) | copy-start | bytes 196
  20.0 8.1 %collective-permute-start.2 = (bf16[2,4,16,128]{3,2,1,0:T(8,128)(2,1)}, bf16[2,4,16,128]{3,2,1,0:T(8,128)(2,1)S(1)}, u32[]{:S(2)}, u32[]{:S(2)}) collective-permute-start(bf16[2,4,16,128]{3,2,1,0:T(8,128)(2,1)} %get-tuple-element.17), channel_id=1, source_target_pairs={{0,1},{1,0},{2,3},{3,2},{4,5},{5,4},{6,7},{7,6},{8,9},{9,8},{10,11... | collective-permute-start | bytes 98312 | tf_op jit(solution)/shard_map/ppermute | solution.py:296
  28.1 0.8 copy-start.1
  28.9 3.5 %copy-start = (bf16[2,416,128]{2,1,0:T(8,128)(2,1)S(1)}, bf16[2,416,128]{2,1,0:T(8,128)(2,1)}, u32[]{:S(2)}) copy-start(bf16[2,416,128]{2,1,0:T(8,128)(2,1)} %get-tuple-element.15.own) | copy-start | bytes 638980
  32.5 31.6 %copy-start.4 = (s32[128]{0:T(128)S(1)}, s32[128]{0:T(128)}, u32[]{:S(2)}) copy-start(s32[128]{0:T(128)} %page_slots.1) | copy-start | bytes 1540
  32.5 31.5 %all-to-all-start = ((bf16[32,72,128]{2,1,0:T(8,128)(2,1)}), bf16[32,72,128]{2,1,0:T(8,128)(2,1)S(1)}, u32[]{:S(2)}, u32[]{:S(2)}) async-start(bf16[32,72,128]{2,1,0:T(8,128)(2,1)} %shard_map.74), calls=%async_computation | async-start | bytes 1179648 | tf_op jit(solution)/shard_map/all_to_all | solution.py:302
  45.1 18.9 %collective-permute-start.3 = (bf16[3,2,416,128]{3,2,1,0:T(8,128)(2,1)S(1)}, bf16[3,2,416,128]{3,2,1,0:T(8,128)(2,1)S(1)}, u32[]{:S(2)}, u32[]{:S(2)}) collective-permute-start(bf16[3,2,416,128]{3,2,1,0:T(8,128)(2,1)S(1)} %get-tuple-element.20), channel_id=1, source_target_pairs={{0,64},{1,9},{2,66},{3,11},{4,68},{5,13},{6,70},{7,15},{8,72},{9,1... | collective-permute-start | bytes 1916936 | tf_op jit(solution)/shard_map/ppermute | solution.py:303
  47.1 14.5 %collective-permute-start.4 = (bf16[2,2,416,128]{3,2,1,0:T(8,128)(2,1)S(1)}, bf16[2,2,416,128]{3,2,1,0:T(8,128)(2,1)S(1)}, u32[]{:S(2)}, u32[]{:S(2)}) collective-permute-start(bf16[2,2,416,128]{3,2,1,0:T(8,128)(2,1)S(1)} %get-tuple-element.21), channel_id=1, source_target_pairs={{0,448},{1,57},{2,450},{3,59},{4,452},{5,61},{6,454},{7,63},{8,456... | collective-permute-start | bytes 1277960 | tf_op jit(solution)/shard_map/ppermute | solution.py:304
  98.7 3.1 %collective-permute-start.5 = (bf16[2,4,16,128]{3,2,1,0:T(8,128)(2,1)S(1)}, bf16[2,4,16,128]{3,2,1,0:T(8,128)(2,1)S(1)}, u32[]{:S(2)}, u32[]{:S(2)}) collective-permute-start(bf16[2,4,16,128]{3,2,1,0:T(8,128)(2,1)S(1)} %get-tuple-element.24), channel_id=1, source_target_pairs={{0,1},{1,0},{2,3},{3,2},{4,5},{5,4},{6,7},{7,6},{8,9},{9,8},{10,11... | collective-permute-start | bytes 98312 | tf_op jit(solution)/shard_map/ppermute | solution.py:313

commit v4 on v3

--- a/solution.py
+++ b/solution.py
@@ -25,6 +25,8 @@
 BLOCKS = LINE * XN
 STEP_BLOCKS = 8
 ROWS = STEP_BLOCKS * BLOCK
+PARTS = BLOCKS // STEP_BLOCKS
+CHUNK = 512
 OFFSETS = (0, -3, 3, -1, -4, 2, 1, -2)
 TO_BITS = math.log2(math.e) / math.sqrt(HD)
 LOWEST = -1e30
@@ -65,9 +67,7 @@
 VMEM = pl.BlockSpec(memory_space=pltpu.VMEM)
 
 
-def pack_kernel(
-    place, positions, queries, hist_keys, hist_values, new_keys, new_values, kv, kept, sent, tags, arrived
-):
+def pack_kernel(place, positions, queries, hist_keys, hist_values, new_keys, new_values, kv, kept, sent, arrived):
     core, line = place[0], place[1]
     copies = [
         pltpu.make_async_copy(hist_keys, kv.at[0, pl.ds(0, HISTORY)], arrived.at[0]),
@@ -84,10 +84,8 @@
     for i in range(NEWT):
         tag = jnp.where(lane == line * NEWT + i, positions[i], tag)
     for side, digit in enumerate((tag // 32, tag % 32)):
-        tags[side] = digit.astype(jnp.float32).astype(jnp.bfloat16)
-    last = pltpu.make_async_copy(tags, kv.at[:, pl.ds(HISTORY + NEWT, NEWT)], arrived.at[6])
-    last.start()
-    for copy in copies + [last]:
+        kv[side, HISTORY + NEWT :, :] = digit.astype(jnp.float32).astype(jnp.bfloat16)
+    for copy in copies:
         copy.wait()
 
 
@@ -118,61 +116,53 @@
             two[i] = block[...]
 
 
-def attend_kernel(
-    place, page_slots, own, lower, upper, below, above, q, out, keys, values, key_positions, scores, found
-):
+def attend_kernel(place, page_slots, own, lower, upper, below, above, q, out, keys, values, scores):
     core, line, ctx = place[0], place[1], place[3]
-
-    @pl.when(pl.program_id(0) == 0)
-    def _():
-        values[:, HD:] = jnp.ones((KEYS, HD), jnp.bfloat16)
-        blocks = [own, lower, upper] + [below.at[i] for i in range(3)] + [above.at[i] for i in range(2)]
-        stride = jnp.where(core == 0, YN, 1)
-        high = jnp.zeros((NEWT, HD), jnp.float32)
-        low = jnp.zeros((NEWT, HD), jnp.float32)
-        count = jnp.int32(0)
-        for block, offset in zip(blocks, OFFSETS, strict=True):
-            source_line = lax.rem(line + offset + LINE, LINE)
-            source = ctx + (source_line - line) * stride
-            other = lax.rem(source + ZN * YN // 2, ZN * YN)
-            first = pl.multiple_of(source_line * NEWT, NEWT)
-            keys[pl.ds(first, NEWT), :] = block[0, HISTORY : HISTORY + NEWT, :]
-            values[pl.ds(first, NEWT), :HD] = block[1, HISTORY : HISTORY + NEWT, :]
-            high += block[0, HISTORY + NEWT :, :].astype(jnp.float32)
-            low += block[1, HISTORY + NEWT :, :].astype(jnp.float32)
-            candidates = [page_slots[2 * source], page_slots[2 * source + 1]]
-            candidates += [page_slots[2 * other], page_slots[2 * other + 1]]
-            for s in range(SLOTS):
-                slot = source * SLOTS + s
-                live = functools.reduce(jnp.logical_or, [candidate == slot for candidate in candidates])
-                to = pl.multiple_of(FRESH + count * PAGE, PAGE)
-
-                @pl.when(live)
-                def _(block=block, s=s, to=to):
-                    keys[pl.ds(to, PAGE), :] = block[0, s * PAGE : (s + 1) * PAGE, :]
-                    values[pl.ds(to, PAGE), :HD] = block[1, s * PAGE : (s + 1) * PAGE, :]
-
-                count += live.astype(jnp.int32)
-        key_positions[...] = (high * 32.0 + low)[:8]
-        found[0] = count
-        for i in range(1, MOST_PAGES):
-
-            @pl.when(i >= count)
-            def _(i=i):
-                here = slice(FRESH + i * PAGE, FRESH + (i + 1) * PAGE)
-                keys[here, :] = keys[FRESH : FRESH + PAGE, :]
-                values[here, :] = jnp.zeros((PAGE, 2 * HD), jnp.bfloat16)
-
-    count = found[0]
-
-    def attend_to(pages):
-        chunks = [(0, FRESH + 3 * PAGE)]
-        while sum(chunks[-1]) < FRESH + pages * PAGE:
-            start = sum(chunks[-1])
-            chunks.append((start, min(4 * PAGE, FRESH + pages * PAGE - start)))
-        rows = q[:, :BLOCK, :].reshape(ROWS, HD)
-        tags = q[:, BLOCK:, :].astype(jnp.float32)
-        key_at = key_positions[0:1, :]
+    values[:, HD:] = jnp.ones((KEYS, HD), jnp.bfloat16)
+    blocks = [own, lower, upper] + [below.at[i] for i in range(3)] + [above.at[i] for i in range(2)]
+    stride = jnp.where(core == 0, YN, 1)
+    high = jnp.zeros((NEWT, HD), jnp.float32)
+    low = jnp.zeros((NEWT, HD), jnp.float32)
+    count = jnp.int32(0)
+    for block, offset in zip(blocks, OFFSETS, strict=True):
+        source_line = lax.rem(line + offset + LINE, LINE)
+        source = ctx + (source_line - line) * stride
+        other = lax.rem(source + ZN * YN // 2, ZN * YN)
+        first = pl.multiple_of(source_line * NEWT, NEWT)
+        keys[pl.ds(first, NEWT), :] = block[0, HISTORY : HISTORY + NEWT, :]
+        values[pl.ds(first, NEWT), :HD] = block[1, HISTORY : HISTORY + NEWT, :]
+        high += block[0, HISTORY + NEWT :, :].astype(jnp.float32)
+        low += block[1, HISTORY + NEWT :, :].astype(jnp.float32)
+        candidates = [page_slots[2 * source], page_slots[2 * source + 1]]
+        candidates += [page_slots[2 * other], page_slots[2 * other + 1]]
+        for s in range(SLOTS):
+            slot = source * SLOTS + s
+            live = functools.reduce(jnp.logical_or, [candidate == slot for candidate in candidates])
+            to = pl.multiple_of(FRESH + count * PAGE, PAGE)
+
+            @pl.when(live)
+            def _(block=block, s=s, to=to):
+                keys[pl.ds(to, PAGE), :] = block[0, s * PAGE : (s + 1) * PAGE, :]
+                values[pl.ds(to, PAGE), :HD] = block[1, s * PAGE : (s + 1) * PAGE, :]
+
+            count += live.astype(jnp.int32)
+    key_at = (high * 32.0 + low)[0:1]
+    for i in range(LINE, MOST_PAGES):
+
+        @pl.when(i >= count)
+        def _(i=i):
+            here = slice(FRESH + i * PAGE, FRESH + (i + 1) * PAGE)
+            keys[here, :] = keys[FRESH : FRESH + PAGE, :]
+            values[here, :] = jnp.zeros((PAGE, 2 * HD), jnp.bfloat16)
+
+    def chunks(pages):
+        end = FRESH + pages * PAGE
+        return [(start, min(CHUNK, end - start)) for start in range(0, end, CHUNK)]
+
+    def score(part, pages):
+        here = slice(part * STEP_BLOCKS, (part + 1) * STEP_BLOCKS)
+        rows = q[here, :BLOCK, :].reshape(ROWS, HD)
+        tags = q[here, BLOCK:, :].astype(jnp.float32)
         bias = []
         for t in range(TOKENS):
             query_at = tags[:, 2 * t, :] * 32.0 + tags[:, 2 * t + 1, :]
@@ -180,23 +170,27 @@
             bias.append(jnp.broadcast_to(hidden[:, None, :], (STEP_BLOCKS, GROUP, HD)))
         bias = jnp.stack(bias, axis=1).reshape(ROWS, HD)
         top = None
-        for start, size in chunks:
-            part = lax.dot_general(
+        for start, size in chunks(pages):
+            product = lax.dot_general(
                 rows, keys[start : start + size, :], (((1,), (1,)), ((), ())), preferred_element_type=jnp.float32
             )
-            for j in range(size // HD):
-                piece = part[:, j * HD : (j + 1) * HD]
+            for j in range(0, size, HD):
+                piece = product[:, j : j + HD]
                 if start + j == 0:
                     piece = piece + bias
-                scores[:, start + j * HD : start + (j + 1) * HD] = piece
+                scores[part, :, start + j : start + j + HD] = piece
                 top = piece if top is None else jnp.maximum(top, piece)
+        return top
+
+    def weigh(part, pages, top):
+        here = slice(part * STEP_BLOCKS, (part + 1) * STEP_BLOCKS)
         top = jnp.max(top, axis=1, keepdims=True) * TO_BITS
         summed = jnp.zeros((ROWS, 2 * HD), jnp.float32)
-        for start, size in chunks:
-            weights = jnp.exp2(scores[:, start : start + size] * TO_BITS - top).astype(jnp.bfloat16)
+        for start, size in chunks(pages):
+            weights = jnp.exp2(scores[part, :, start : start + size] * TO_BITS - top).astype(jnp.bfloat16)
             summed += jnp.dot(weights, values[start : start + size, :], preferred_element_type=jnp.float32)
         total = summed[:, HD:]
-        out[:, :BLOCK, :] = (summed[:, :HD] / total).astype(jnp.bfloat16).reshape(STEP_BLOCKS, BLOCK, HD)
+        out[here, :BLOCK, :] = (summed[:, :HD] / total).astype(jnp.bfloat16).reshape(STEP_BLOCKS, BLOCK, HD)
         level = (top + jnp.log2(total)).reshape(STEP_BLOCKS, BLOCK, HD)
         row = lax.broadcasted_iota(jnp.int32, (STEP_BLOCKS, BLOCK, HD), 1)
         lane = lax.broadcasted_iota(jnp.int32, (STEP_BLOCKS, BLOCK, HD), 2)
@@ -205,7 +199,14 @@
         rest = level - high
         middle = rest.astype(jnp.bfloat16).astype(jnp.float32)
         zeros = jnp.zeros((STEP_BLOCKS, 5, HD), jnp.float32)
-        out[:, BLOCK:, :] = jnp.concatenate([high, middle, rest - middle, zeros], axis=1).astype(jnp.bfloat16)
+        out[here, BLOCK:, :] = jnp.concatenate([high, middle, rest - middle, zeros], axis=1).astype(jnp.bfloat16)
+
+    def attend_to(pages):
+        top = score(0, pages)
+        for part in range(PARTS):
+            following = score(part + 1, pages) if part + 1 < PARTS else None
+            weigh(part, pages, top)
+            top = following
 
     usual, larger = 2 * LINE, 2 * LINE + LINE // 2
     pl.when(count <= usual)(lambda: attend_to(usual))
@@ -214,29 +215,18 @@
 
 
 def attend(place, page_slots, pieces, q):
-    def whole(array):
-        return pl.BlockSpec(array.shape, lambda i, *_: (0,) * array.ndim)
-
-    wire = pl.BlockSpec((STEP_BLOCKS, WIRE, HD), lambda i, *_: (i, 0, 0))
     return call(
         attend_kernel,
         bf16(BLOCKS, WIRE, HD),
-        megabytes=40,
+        megabytes=36,
         flops=2300000000,
         moved=5000000,
-        grid_spec=pltpu.PrefetchScalarGridSpec(
-            num_scalar_prefetch=2,
-            grid=(BLOCKS // STEP_BLOCKS,),
-            in_specs=[whole(piece) for piece in pieces] + [wire],
-            out_specs=wire,
-            scratch_shapes=[
-                pltpu.VMEM((KEYS, HD), jnp.bfloat16),
-                pltpu.VMEM((KEYS, 2 * HD), jnp.bfloat16),
-                pltpu.VMEM((8, HD), jnp.float32),
-                pltpu.VMEM((ROWS, KEYS), jnp.float32),
-                pltpu.SMEM((1,), jnp.int32),
-            ],
-        ),
+        in_specs=[SMEM, SMEM] + [VMEM] * 6,
+        scratch_shapes=[
+            pltpu.VMEM((KEYS, HD), jnp.bfloat16),
+            pltpu.VMEM((KEYS, 2 * HD), jnp.bfloat16),
+            pltpu.VMEM((PARTS, ROWS, KEYS), jnp.float32),
+        ],
     )(place, page_slots, *pieces, q)
 
 
@@ -279,8 +269,7 @@
         pack_kernel,
         (bf16(2, KV_ROWS, HD), half, half),
         in_specs=[SMEM, SMEM] + [HBM] * 5,
-        out_specs=(HBM, HBM, HBM),
-        scratch_shapes=[pltpu.VMEM((2, NEWT, HD), jnp.bfloat16), pltpu.SemaphoreType.DMA((7,))],
+        scratch_shapes=[pltpu.SemaphoreType.DMA((6,))],
         megabytes=56,
     )(
         place,
@@ -297,8 +286,7 @@
     q = call(spread_kernel, bf16(BLOCKS, WIRE, HD), in_specs=[SMEM, SMEM, VMEM, VMEM])(
         place, new_positions, q_kept, q_received
     )
-    three, two = call(join_kernel, (bf16(3, 2, KV_ROWS, HD), bf16(2, 2, KV_ROWS, HD)))(kv, lower, upper)
-    q, three, two = lax.optimization_barrier((q, three, two))
+    three, two = call(join_kernel, (bf16(3, 2, KV_ROWS, HD), bf16(2, 2, KV_ROWS, HD)), flops=30000000000)(kv, lower, upper)
     q = lax.all_to_all(q, ALL, split_axis=0, concat_axis=0, axis_index_groups=CROSS, tiled=True)
     below = lax.ppermute(three, ALL, along(1))
     above = lax.ppermute(two, ALL, along(-1))

time: 103 us -> 85.3 us (0.83)
  Pallas kernels: 30 us -> 12.9 us
  blocking collectives: 17.4 us -> 21.9 us
  waiting for transfers between devices: 16.7 us -> 13.3 us
  starting transfers between devices: 37.4 us -> 35.2 us
    pallas_call x2, Pallas kernels: 16.4 us -> 6.98 us  [the longest x1 6.86 us: attend(): call(attend_kernel, bf16(BLOCKS, WIRE, HD), megabytes=36, flops=230000000...]
    pallas_call x1, Pallas kernels: 10 us -> 2.36 us  [body(): call(pack_kernel, (bf16(2, KV_ROWS, HD), half, half), in_specs=[SMEM, SME...]
    all_to_all x1, starting transfers between devices: 12.6 us -> 7.63 us  [body(): lax.all_to_all(q, ALL, split_axis=0, concat_axis=0, axis_index_groups=CRO...]
    all_to_all x1, blocking collectives: 17.4 us -> 21.9 us  [body(): lax.all_to_all(parts, ALL, split_axis=0, concat_axis=0, axis_index_groups...]
    ppermute x1, starting transfers between devices: 7.5 us -> 3.36 us  [body(): upper = lax.ppermute(kv, ALL, along(-3))]
    ppermute x1, starting transfers between devices: 1.92 us -> 6.06 us  [body(): lower = lax.ppermute(kv, ALL, along(3))]
    ppermute x1, waiting for transfers between devices: 2.05 us -> 0.01 us  [body(): lower = lax.ppermute(kv, ALL, along(3))]
    ppermute x1, waiting for transfers between devices: 9.91 us -> 8.12 us  [body(): above = lax.ppermute(two, ALL, along(-1))]
  transfers between devices with their start and end apart: 7 -> 7, of which waited for: 5 -> 4; matrix products, arithmetic and copies ran while one was open for 0% -> 0% of each run, Pallas kernels for 1% -> 2%
where the time goes in v4:
time: 85.3 us; the launch traced here: 84.8 us
  starting transfers between devices  35.2 us (41%)
  blocking collectives  21.9 us (26%)
  waiting for transfers between devices  13.3 us (16%)
  Pallas kernels  12.9 us (15%)
    all_to_all x1, blocking collectives, body(): lax.all_to_all(parts, ALL, split_axis=0, concat_axis=0, axis_index_groups...  21.9 us
    ppermute x1, starting transfers between devices, body(): q_received = lax.ppermute(q_sent, ALL, SWAP)  8.22 us
    ppermute x1, waiting for transfers between devices, body(): above = lax.ppermute(two, ALL, along(-1))  8.12 us
    all_to_all x1, starting transfers between devices, body(): lax.all_to_all(q, ALL, split_axis=0, concat_axis=0, axis_index_groups=CRO...  7.63 us
    pallas_call x1, Pallas kernels, attend(): call(attend_kernel, bf16(BLOCKS, WIRE, HD), megabytes=36, flops=230000000...  6.86 us
    ppermute x1, starting transfers between devices, body(): lower = lax.ppermute(kv, ALL, along(3))  6.06 us
    ppermute x1, starting transfers between devices, body(): above = lax.ppermute(two, ALL, along(-1))  3.81 us
    ppermute x1, starting transfers between devices, body(): upper = lax.ppermute(kv, ALL, along(-3))  3.36 us
  transfers between devices with their start and end apart: 7, of which 4 were waited for; matrix products, arithmetic and copies ran while one was open for 0% of the time, Pallas kernels for 2%

profile of v4, /device:TPU:1, one launch (start us, length us, event | category | flops | bytes accessed | tf_op | source)
XLA Modules:
  0.0 84.8 jit_solution(8056709876605619823)
XLA Ops:
  0.0 0.6 pad_add_fusion.place
  0.6 2.4 %shard_map.73 = (bf16[2,416,128]{2,1,0:T(8,128)(2,1)}, bf16[2,4,16,128]{3,2,1,0:T(8,128)(2,1)}, bf16[2,4,16,128]{3,2,1,0:T(8,128)(2,1)}) custom-call(s32[4]{0:T(128)} %pad_add_fusion.place, s32[16]{0:T(128)} %positions.3, bf16[2,4,2,16,128]{4,3,2,1,0:T(8,128)(2,1)} %bitcast.11, bf16[384,128]{1,0:T(8,128)(2,1)} %bitcast.9, bf16[384,128]{1,0:T(8,128)(2,1)} %bitcast.10, ...), custom_call_target="tpu_custom_call" | custom-call | flops 1000000 | bytes 800000 | tf_op jit(solution)/shard_map/pallas_call | solution.py:268
  2.9 6.1 %collective-permute-start = (bf16[2,416,128]{2,1,0:T(8,128)(2,1)}, bf16[2,416,128]{2,1,0:T(8,128)(2,1)S(1)}, u32[]{:S(2)}, u32[]{:S(2)}) collective-permute-start(bf16[2,416,128]{2,1,0:T(8,128)(2,1)} %get-tuple-element.12.own), channel_id=1, source_target_pairs={{0,192},{1,25},{2,194},{3,27},{4,196},{5,29},{6,198},{7,31},{8,200... | collective-permute-start | bytes 638984 | tf_op jit(solution)/shard_map/ppermute | solution.py:283
  9.0 3.4 %collective-permute-start.1 = (bf16[2,416,128]{2,1,0:T(8,128)(2,1)}, bf16[2,416,128]{2,1,0:T(8,128)(2,1)S(1)}, u32[]{:S(2)}, u32[]{:S(2)}) collective-permute-start(bf16[2,416,128]{2,1,0:T(8,128)(2,1)} %get-tuple-element.12.own), channel_id=1, source_target_pairs={{0,320},{1,41},{2,322},{3,43},{4,324},{5,45},{6,326},{7,47},{8,328... | collective-permute-start | bytes 638984 | tf_op jit(solution)/shard_map/ppermute | solution.py:284
  12.4 0.0 copy-start.1
  12.4 0.0 copy-start.2
  12.4 8.2 %collective-permute-start.4 = (bf16[2,4,16,128]{3,2,1,0:T(8,128)(2,1)}, bf16[2,4,16,128]{3,2,1,0:T(8,128)(2,1)S(1)}, u32[]{:S(2)}, u32[]{:S(2)}) collective-permute-start(bf16[2,4,16,128]{3,2,1,0:T(8,128)(2,1)} %get-tuple-element.16), channel_id=1, source_target_pairs={{0,1},{1,0},{2,3},{3,2},{4,5},{5,4},{6,7},{7,6},{8,9},{9,8},{10,11... | collective-permute-start | bytes 98312 | tf_op jit(solution)/shard_map/ppermute | solution.py:285
  20.6 1.0 %collective-permute-done.4.received = bf16[2,4,16,128]{3,2,1,0:T(8,128)(2,1)S(1)} collective-permute-done((bf16[2,4,16,128]{3,2,1,0:T(8,128)(2,1)}, bf16[2,4,16,128]{3,2,1,0:T(8,128)(2,1)S(1)}, u32[]{:S(2)}, u32[]{:S(2)}) %collective-permute-start.4) | collective-permute-done | bytes 32800 | tf_op jit(solution)/shard_map/ppermute | solution.py:285
  21.7 0.0 copy-done.1
  21.7 0.0 copy-done.2
  21.7 0.0 copy-start
  21.7 0.8 copy-done
  22.4 1.5 %shard_map.75 = bf16[32,72,128]{2,1,0:T(8,128)(2,1)} custom-call(s32[4]{0:T(128)S(1)} %copy-done.1, s32[16]{0:T(128)S(1)} %copy-done.2, bf16[2,4,16,128]{3,2,1,0:T(8,128)(2,1)S(1)} %copy-done, bf16[2,4,16,128]{3,2,1,0:T(8,128)(2,1)S(1)} %collective-permute-done.4.received), custom_call_target="tpu_custom_call" | custom-call | flops 1000000 | bytes 800000 | tf_op jit(solution)/shard_map/pallas_call | solution.py:286
  23.9 0.0 copy-start.3
  23.9 7.6 %all-to-all-start = ((bf16[32,72,128]{2,1,0:T(8,128)(2,1)}), bf16[32,72,128]{2,1,0:T(8,128)(2,1)S(1)}, u32[]{:S(2)}, u32[]{:S(2)}) async-start(bf16[32,72,128]{2,1,0:T(8,128)(2,1)} %shard_map.75), calls=%async_computation | async-start | bytes 1179648 | tf_op jit(solution)/shard_map/all_to_all | solution.py:290
  31.5 0.0 collective-permute-done.lower
  31.5 0.0 collective-permute-done.1.upper
  31.5 0.0 copy-done.3
  31.6 0.1 shard_map.74
  31.7 0.0 copy-start.4
  31.7 3.2 %collective-permute-start.2 = (bf16[3,2,416,128]{3,2,1,0:T(8,128)(2,1)S(1)}, bf16[3,2,416,128]{3,2,1,0:T(8,128)(2,1)S(1)}, u32[]{:S(2)}, u32[]{:S(2)}) collective-permute-start(bf16[3,2,416,128]{3,2,1,0:T(8,128)(2,1)S(1)} %get-tuple-element.13), channel_id=1, source_target_pairs={{0,64},{1,9},{2,66},{3,11},{4,68},{5,13},{6,70},{7,15},{8,72},{9,1... | collective-permute-start | bytes 1916936 | tf_op jit(solution)/shard_map/ppermute | solution.py:291
  34.9 3.8 %collective-permute-start.3 = (bf16[2,2,416,128]{3,2,1,0:T(8,128)(2,1)S(1)}, bf16[2,2,416,128]{3,2,1,0:T(8,128)(2,1)S(1)}, u32[]{:S(2)}, u32[]{:S(2)}) collective-permute-start(bf16[2,2,416,128]{3,2,1,0:T(8,128)(2,1)S(1)} %get-tuple-element.14), channel_id=1, source_target_pairs={{0,448},{1,57},{2,450},{3,59},{4,452},{5,61},{6,454},{7,63},{8,456... | collective-permute-start | bytes 1277960 | tf_op jit(solution)/shard_map/ppermute | solution.py:292
  38.7 8.1 %collective-permute-done.3.above = bf16[2,2,416,128]{3,2,1,0:T(8,128)(2,1)S(1)} collective-permute-done((bf16[2,2,416,128]{3,2,1,0:T(8,128)(2,1)S(1)}, bf16[2,2,416,128]{3,2,1,0:T(8,128)(2,1)S(1)}, u32[]{:S(2)}, u32[]{:S(2)}) %collective-permute-start.3) | collective-permute-done | bytes 426016 | tf_op jit(solution)/shard_map/ppermute | solution.py:292
  46.9 3.3 %collective-permute-done.2.below = bf16[3,2,416,128]{3,2,1,0:T(8,128)(2,1)S(1)} collective-permute-done((bf16[3,2,416,128]{3,2,1,0:T(8,128)(2,1)S(1)}, bf16[3,2,416,128]{3,2,1,0:T(8,128)(2,1)S(1)}, u32[]{:S(2)}, u32[]{:S(2)}) %collective-permute-start.2) | collective-permute-done | bytes 639008 | tf_op jit(solution)/shard_map/ppermute | solution.py:291
  50.1 0.0 all-to-all-done.q
  50.1 0.0 copy-done.4
  50.1 6.9 %shard_map.76 = bf16[32,72,128]{2,1,0:T(8,128)(2,1)S(1)} custom-call(s32[4]{0:T(128)S(1)} %copy-done.1, s32[128]{0:T(128)S(1)} %copy-done.4, bf16[2,416,128]{2,1,0:T(8,128)(2,1)S(1)} %copy-done.3, bf16[2,416,128]{2,1,0:T(8,128)(2,1)S(1)} %collective-permute-done.lower, bf16[2,416,128]{2,1,0:T(8,128)(2,1)S(1)} %collective-permute-done.1.upper, ...), custom_call_target="tpu_custom_call" | custom-call | flops 2300000000 | bytes 5000000 | tf_op jit(solution)/shard_map/pallas_call | solution.py:218
  57.0 21.9 %all_to_all.10.parts = bf16[32,72,128]{2,1,0:T(8,128)(2,1)S(1)} all-to-all(bf16[32,72,128]{2,1,0:T(8,128)(2,1)S(1)} %shard_map.76), channel_id=1, replica_groups={{0,2,4,6,8,10,12,14,16,18,20,22,24,26,28,30,32,34,36,38,40,42,44,46,48,..., dimensions={0} | all-to-all | bytes 1179648 | tf_op jit(solution)/shard_map/all_to_all | solution.py:294
  78.9 0.9 %shard_map.77 = (bf16[2,4,16,128]{3,2,1,0:T(8,128)(2,1)S(1)}, bf16[2,4,16,128]{3,2,1,0:T(8,128)(2,1)S(1)}) custom-call(s32[4]{0:T(128)S(1)} %copy-done.1, bf16[32,72,128]{2,1,0:T(8,128)(2,1)S(1)} %all_to_all.10.parts), custom_call_target="tpu_custom_call" | custom-call | flops 1000000 | bytes 800000 | tf_op jit(solution)/shard_map/pallas_call | solution.py:295
  79.8 3.0 %collective-permute-start.5 = (bf16[2,4,16,128]{3,2,1,0:T(8,128)(2,1)S(1)}, bf16[2,4,16,128]{3,2,1,0:T(8,128)(2,1)S(1)}, u32[]{:S(2)}, u32[]{:S(2)}) collective-permute-start(bf16[2,4,16,128]{3,2,1,0:T(8,128)(2,1)S(1)} %get-tuple-element.18), channel_id=1, source_target_pairs={{0,1},{1,0},{2,3},{3,2},{4,5},{5,4},{6,7},{7,6},{8,9},{9,8},{10,11... | collective-permute-start | bytes 98312 | tf_op jit(solution)/shard_map/ppermute | solution.py:301
  82.8 0.8 collective-permute-done.5.received
  83.6 1.2 %shard_map.78 = bf16[2,128,128]{2,1,0:T(8,128)(2,1)} custom-call(s32[4]{0:T(128)S(1)} %copy-done.1, bf16[2,4,16,128]{3,2,1,0:T(8,128)(2,1)S(1)} %get-tuple-element.17.kept, bf16[2,4,16,128]{3,2,1,0:T(8,128)(2,1)S(1)} %collective-permute-done.5.received), custom_call_target="tpu_custom_call" | custom-call | flops 1000000 | bytes 800000 | tf_op jit(solution)/shard_map/pallas_call | solution.py:302
Async XLA Ops:
  2.9 28.6 %collective-permute-start = (bf16[2,416,128]{2,1,0:T(8,128)(2,1)}, bf16[2,416,128]{2,1,0:T(8,128)(2,1)S(1)}, u32[]{:S(2)}, u32[]{:S(2)}) collective-permute-start(bf16[2,416,128]{2,1,0:T(8,128)(2,1)} %get-tuple-element.12.own), channel_id=1, source_target_pairs={{0,192},{1,25},{2,194},{3,27},{4,196},{5,29},{6,198},{7,31},{8,200... | collective-permute-start | bytes 638984 | tf_op jit(solution)/shard_map/ppermute | solution.py:283
  9.0 22.5 %collective-permute-start.1 = (bf16[2,416,128]{2,1,0:T(8,128)(2,1)}, bf16[2,416,128]{2,1,0:T(8,128)(2,1)S(1)}, u32[]{:S(2)}, u32[]{:S(2)}) collective-permute-start(bf16[2,416,128]{2,1,0:T(8,128)(2,1)} %get-tuple-element.12.own), channel_id=1, source_target_pairs={{0,320},{1,41},{2,322},{3,43},{4,324},{5,45},{6,326},{7,47},{8,328... | collective-permute-start | bytes 638984 | tf_op jit(solution)/shard_map/ppermute | solution.py:284
  12.4 9.3 %copy-start.1 = (s32[4]{0:T(128)S(1)}, s32[4]{0:T(128)}, u32[]{:S(2)}) copy-start(s32[4]{0:T(128)} %pad_add_fusion.place) | copy-start | bytes 52
  12.4 9.3 %copy-start.2 = (s32[16]{0:T(128)S(1)}, s32[16]{0:T(128)}, u32[]{:S(2)}) copy-start(s32[16]{0:T(128)} %positions.3) | copy-start | bytes 196
  12.4 9.3 %collective-permute-start.4 = (bf16[2,4,16,128]{3,2,1,0:T(8,128)(2,1)}, bf16[2,4,16,128]{3,2,1,0:T(8,128)(2,1)S(1)}, u32[]{:S(2)}, u32[]{:S(2)}) collective-permute-start(bf16[2,4,16,128]{3,2,1,0:T(8,128)(2,1)} %get-tuple-element.16), channel_id=1, source_target_pairs={{0,1},{1,0},{2,3},{3,2},{4,5},{5,4},{6,7},{7,6},{8,9},{9,8},{10,11... | collective-permute-start | bytes 98312 | tf_op jit(solution)/shard_map/ppermute | solution.py:285
  21.7 0.8 copy-start
  23.9 7.7 %copy-start.3 = (bf16[2,416,128]{2,1,0:T(8,128)(2,1)S(1)}, bf16[2,416,128]{2,1,0:T(8,128)(2,1)}, u32[]{:S(2)}) copy-start(bf16[2,416,128]{2,1,0:T(8,128)(2,1)} %get-tuple-element.12.own) | copy-start | bytes 638980
  23.9 26.2 %all-to-all-start = ((bf16[32,72,128]{2,1,0:T(8,128)(2,1)}), bf16[32,72,128]{2,1,0:T(8,128)(2,1)S(1)}, u32[]{:S(2)}, u32[]{:S(2)}) async-start(bf16[32,72,128]{2,1,0:T(8,128)(2,1)} %shard_map.75), calls=%async_computation | async-start | bytes 1179648 | tf_op jit(solution)/shard_map/all_to_all | solution.py:290
  31.7 18.4 %copy-start.4 = (s32[128]{0:T(128)S(1)}, s32[128]{0:T(128)}, u32[]{:S(2)}) copy-start(s32[128]{0:T(128)} %page_slots.1) | copy-start | bytes 1540
  31.7 18.4 %collective-permute-start.2 = (bf16[3,2,416,128]{3,2,1,0:T(8,128)(2,1)S(1)}, bf16[3,2,416,128]{3,2,1,0:T(8,128)(2,1)S(1)}, u32[]{:S(2)}, u32[]{:S(2)}) collective-permute-start(bf16[3,2,416,128]{3,2,1,0:T(8,128)(2,1)S(1)} %get-tuple-element.13), channel_id=1, source_target_pairs={{0,64},{1,9},{2,66},{3,11},{4,68},{5,13},{6,70},{7,15},{8,72},{9,1... | collective-permute-start | bytes 1916936 | tf_op jit(solution)/shard_map/ppermute | solution.py:291
  34.9 11.9 %collective-permute-start.3 = (bf16[2,2,416,128]{3,2,1,0:T(8,128)(2,1)S(1)}, bf16[2,2,416,128]{3,2,1,0:T(8,128)(2,1)S(1)}, u32[]{:S(2)}, u32[]{:S(2)}) collective-permute-start(bf16[2,2,416,128]{3,2,1,0:T(8,128)(2,1)S(1)} %get-tuple-element.14), channel_id=1, source_target_pairs={{0,448},{1,57},{2,450},{3,59},{4,452},{5,61},{6,454},{7,63},{8,456... | collective-permute-start | bytes 1277960 | tf_op jit(solution)/shard_map/ppermute | solution.py:292
  79.8 3.8 %collective-permute-start.5 = (bf16[2,4,16,128]{3,2,1,0:T(8,128)(2,1)S(1)}, bf16[2,4,16,128]{3,2,1,0:T(8,128)(2,1)S(1)}, u32[]{:S(2)}, u32[]{:S(2)}) collective-permute-start(bf16[2,4,16,128]{3,2,1,0:T(8,128)(2,1)S(1)} %get-tuple-element.18), channel_id=1, source_target_pairs={{0,1},{1,0},{2,3},{3,2},{4,5},{5,4},{6,7},{7,6},{8,9},{9,8},{10,11... | collective-permute-start | bytes 98312 | tf_op jit(solution)/shard_map/ppermute | solution.py:301

commit v5 on v4

--- a/solution.py
+++ b/solution.py
@@ -27,6 +27,7 @@
 ROWS = STEP_BLOCKS * BLOCK
 PARTS = BLOCKS // STEP_BLOCKS
 CHUNK = 512
+SIZES = (16, 18, 20, 24)
 OFFSETS = (0, -3, 3, -1, -4, 2, 1, -2)
 TO_BITS = math.log2(math.e) / math.sqrt(HD)
 LOWEST = -1e30
@@ -67,8 +68,13 @@
 VMEM = pl.BlockSpec(memory_space=pltpu.VMEM)
 
 
-def pack_kernel(place, positions, queries, hist_keys, hist_values, new_keys, new_values, kv, kept, sent, arrived):
-    core, line = place[0], place[1]
+def own_place():
+    core = lax.axis_index("c")
+    return core, jnp.where(core == 0, lax.axis_index("z"), lax.axis_index("y"))
+
+
+def pack_kernel(positions, queries, hist_keys, hist_values, new_keys, new_values, kv, kept, sent, arrived):
+    core, line = own_place()
     copies = [
         pltpu.make_async_copy(hist_keys, kv.at[0, pl.ds(0, HISTORY)], arrived.at[0]),
         pltpu.make_async_copy(hist_values, kv.at[1, pl.ds(0, HISTORY)], arrived.at[1]),
@@ -89,8 +95,8 @@
         copy.wait()
 
 
-def spread_kernel(place, positions, kept, received, out):
-    core, x_here = place[0], place[2]
+def spread_kernel(positions, kept, received, out):
+    core, x_here = lax.axis_index("c"), lax.axis_index("x")
     row = lax.broadcasted_iota(jnp.int32, (8, HD), 0)
     tag = jnp.zeros((8, HD), jnp.int32)
     for i in range(TOKENS):
@@ -116,11 +122,12 @@
             two[i] = block[...]
 
 
-def attend_kernel(place, page_slots, own, lower, upper, below, above, q, out, keys, values, scores):
-    core, line, ctx = place[0], place[1], place[3]
+def attend_kernel(page_slots, own, lower, upper, below, above, q, out, keys, values, scores):
+    core, line = own_place()
+    ctx = lax.axis_index("z") * YN + lax.axis_index("y")
+    stride = jnp.where(core == 0, YN, 1)
     values[:, HD:] = jnp.ones((KEYS, HD), jnp.bfloat16)
     blocks = [own, lower, upper] + [below.at[i] for i in range(3)] + [above.at[i] for i in range(2)]
-    stride = jnp.where(core == 0, YN, 1)
     high = jnp.zeros((NEWT, HD), jnp.float32)
     low = jnp.zeros((NEWT, HD), jnp.float32)
     count = jnp.int32(0)
@@ -139,28 +146,26 @@
             slot = source * SLOTS + s
             live = functools.reduce(jnp.logical_or, [candidate == slot for candidate in candidates])
             to = pl.multiple_of(FRESH + count * PAGE, PAGE)
-
-            @pl.when(live)
-            def _(block=block, s=s, to=to):
-                keys[pl.ds(to, PAGE), :] = block[0, s * PAGE : (s + 1) * PAGE, :]
-                values[pl.ds(to, PAGE), :HD] = block[1, s * PAGE : (s + 1) * PAGE, :]
-
+            keys[pl.ds(to, PAGE), :] = block[0, s * PAGE : (s + 1) * PAGE, :]
+            values[pl.ds(to, PAGE), :HD] = block[1, s * PAGE : (s + 1) * PAGE, :]
             count += live.astype(jnp.int32)
     key_at = (high * 32.0 + low)[0:1]
-    for i in range(LINE, MOST_PAGES):
-
-        @pl.when(i >= count)
-        def _(i=i):
-            here = slice(FRESH + i * PAGE, FRESH + (i + 1) * PAGE)
-            keys[here, :] = keys[FRESH : FRESH + PAGE, :]
-            values[here, :] = jnp.zeros((PAGE, 2 * HD), jnp.bfloat16)
+    places = functools.reduce(lambda size, less: jnp.where(count <= less, less, size), SIZES[-2::-1], SIZES[-1])
+
+    def repeat(i, carry):
+        here = pl.ds(pl.multiple_of(FRESH + i * PAGE, PAGE), PAGE)
+        keys[here, :] = keys[FRESH : FRESH + PAGE, :]
+        values[here, :] = jnp.zeros((PAGE, 2 * HD), jnp.bfloat16)
+        return carry
+
+    lax.fori_loop(count, places, repeat, 0)
 
     def chunks(pages):
         end = FRESH + pages * PAGE
         return [(start, min(CHUNK, end - start)) for start in range(0, end, CHUNK)]
 
-    def score(part, pages):
-        here = slice(part * STEP_BLOCKS, (part + 1) * STEP_BLOCKS)
+    def score(part, side, pages):
+        here = pl.ds(part * STEP_BLOCKS, STEP_BLOCKS)
         rows = q[here, :BLOCK, :].reshape(ROWS, HD)
         tags = q[here, BLOCK:, :].astype(jnp.float32)
         bias = []
@@ -178,16 +183,16 @@
                 piece = product[:, j : j + HD]
                 if start + j == 0:
                     piece = piece + bias
-                scores[part, :, start + j : start + j + HD] = piece
+                scores[side, :, start + j : start + j + HD] = piece
                 top = piece if top is None else jnp.maximum(top, piece)
         return top
 
-    def weigh(part, pages, top):
-        here = slice(part * STEP_BLOCKS, (part + 1) * STEP_BLOCKS)
+    def weigh(part, side, pages, top):
+        here = pl.ds(part * STEP_BLOCKS, STEP_BLOCKS)
         top = jnp.max(top, axis=1, keepdims=True) * TO_BITS
         summed = jnp.zeros((ROWS, 2 * HD), jnp.float32)
         for start, size in chunks(pages):
-            weights = jnp.exp2(scores[part, :, start : start + size] * TO_BITS - top).astype(jnp.bfloat16)
+            weights = jnp.exp2(scores[side, :, start : start + size] * TO_BITS - top).astype(jnp.bfloat16)
             summed += jnp.dot(weights, values[start : start + size, :], preferred_element_type=jnp.float32)
         total = summed[:, HD:]
         out[here, :BLOCK, :] = (summed[:, :HD] / total).astype(jnp.bfloat16).reshape(STEP_BLOCKS, BLOCK, HD)
@@ -202,36 +207,36 @@
         out[here, BLOCK:, :] = jnp.concatenate([high, middle, rest - middle, zeros], axis=1).astype(jnp.bfloat16)
 
     def attend_to(pages):
-        top = score(0, pages)
-        for part in range(PARTS):
-            following = score(part + 1, pages) if part + 1 < PARTS else None
-            weigh(part, pages, top)
-            top = following
-
-    usual, larger = 2 * LINE, 2 * LINE + LINE // 2
-    pl.when(count <= usual)(lambda: attend_to(usual))
-    pl.when((count > usual) & (count <= larger))(lambda: attend_to(larger))
-    pl.when(count > larger)(lambda: attend_to(MOST_PAGES))
-
-
-def attend(place, page_slots, pieces, q):
+        def pair(i, carry):
+            tops = [score(2 * i + side, side, pages) for side in range(2)]
+            for side in range(2):
+                weigh(2 * i + side, side, pages, tops[side])
+            return carry
+
+        lax.fori_loop(0, PARTS // 2, pair, 0)
+
+    for pages in SIZES:
+        pl.when(places == pages)(functools.partial(attend_to, pages))
+
+
+def attend(page_slots, pieces, q):
     return call(
         attend_kernel,
         bf16(BLOCKS, WIRE, HD),
-        megabytes=36,
+        megabytes=20,
         flops=2300000000,
         moved=5000000,
-        in_specs=[SMEM, SMEM] + [VMEM] * 6,
+        in_specs=[SMEM] + [VMEM] * 6,
         scratch_shapes=[
             pltpu.VMEM((KEYS, HD), jnp.bfloat16),
             pltpu.VMEM((KEYS, 2 * HD), jnp.bfloat16),
-            pltpu.VMEM((PARTS, ROWS, KEYS), jnp.float32),
+            pltpu.VMEM((2, ROWS, KEYS), jnp.float32),
         ],
-    )(place, page_slots, *pieces, q)
-
-
-def combine_kernel(place, parts, kept, sent, merged_rows):
-    core = place[0]
+    )(page_slots, *pieces, q)
+
+
+def combine_kernel(other, parts, out, merged_rows):
+    owner = lax.axis_index("c") ^ other
     tags = parts[:, BLOCK:, :].astype(jnp.float32)
     level = tags[:, 0:1, :] + tags[:, 1:2, :] + tags[:, 2:3, :]
     level = level.reshape(LINE, XN, 1, HD)
@@ -245,15 +250,14 @@
             column = jnp.sum(jnp.where(row == lane, weight[line, x], 0.0), axis=1, keepdims=True)
             merged += column * parts[line * XN + x, :BLOCK, :].astype(jnp.float32)
         merged_rows[x] = merged.astype(jnp.bfloat16)
-    for target, owner in ((kept, core), (sent, 1 - core)):
-        for t in range(OWN):
-            for x in range(XN):
-                first = pl.multiple_of((owner * OWN + t) * GROUP, GROUP)
-                target[t, x] = merged_rows[x, pl.ds(first, GROUP), :]
-
-
-def finish_kernel(place, kept, received, out):
-    core = place[0]
+    for t in range(OWN):
+        for x in range(XN):
+            first = pl.multiple_of((owner * OWN + t) * GROUP, GROUP)
+            out[t, x] = merged_rows[x, pl.ds(first, GROUP), :]
+
+
+def finish_kernel(kept, received, out):
+    core = lax.axis_index("c")
     for array, parity in ((kept, core), (received, 1 - core)):
         for t in range(OWN):
             for x in range(XN):
@@ -262,44 +266,42 @@
 
 
 def body(queries, new_keys, new_values, new_positions, hist_keys, hist_values, page_slots):
-    z, y, x, core = (lax.axis_index(name).astype(jnp.int32) for name in ALL)
-    place = jnp.stack([core, jnp.where(core == 0, z, y), x, z * YN + y])
     half = bf16(OWN, XN, GROUP, HD)
-    kv, q_kept, q_sent = call(
-        pack_kernel,
-        (bf16(2, KV_ROWS, HD), half, half),
-        in_specs=[SMEM, SMEM] + [HBM] * 5,
-        scratch_shapes=[pltpu.SemaphoreType.DMA((6,))],
-        megabytes=56,
-    )(
-        place,
-        new_positions,
+    sources = [
         queries.reshape(OWN, XN, CN, GROUP, HD),
         hist_keys.reshape(HISTORY, HD),
         hist_values.reshape(HISTORY, HD),
         new_keys.reshape(NEWT, HD),
         new_values.reshape(NEWT, HD),
-    )
+    ]
+    kv, q_kept, q_sent = call(
+        pack_kernel,
+        (bf16(2, KV_ROWS, HD), half, half),
+        in_specs=[SMEM] + [HBM] * 5,
+        scratch_shapes=[pltpu.SemaphoreType.DMA((6,))],
+    )(new_positions, *(pltpu.with_memory_space_constraint(source, pltpu.HBM) for source in sources))
     lower = lax.ppermute(kv, ALL, along(3))
     upper = lax.ppermute(kv, ALL, along(-3))
     q_received = lax.ppermute(q_sent, ALL, SWAP)
-    q = call(spread_kernel, bf16(BLOCKS, WIRE, HD), in_specs=[SMEM, SMEM, VMEM, VMEM])(
-        place, new_positions, q_kept, q_received
+    q = call(spread_kernel, bf16(BLOCKS, WIRE, HD), in_specs=[SMEM, VMEM, VMEM])(
+        new_positions, q_kept, q_received
     )
     three, two = call(join_kernel, (bf16(3, 2, KV_ROWS, HD), bf16(2, 2, KV_ROWS, HD)), flops=30000000000)(kv, lower, upper)
     q = lax.all_to_all(q, ALL, split_axis=0, concat_axis=0, axis_index_groups=CROSS, tiled=True)
     below = lax.ppermute(three, ALL, along(1))
     above = lax.ppermute(two, ALL, along(-1))
-    parts = attend(place, page_slots, (kv, lower, upper, below, above), q)
+    parts = attend(page_slots, (kv, lower, upper, below, above), q)
     parts = lax.all_to_all(parts, ALL, split_axis=0, concat_axis=0, axis_index_groups=CROSS, tiled=True)
-    kept, sent = call(
-        combine_kernel,
-        (half, half),
-        in_specs=[SMEM, VMEM],
-        scratch_shapes=[pltpu.VMEM((XN, BLOCK, HD), jnp.bfloat16)],
-    )(place, parts)
-    received = lax.ppermute(sent, ALL, SWAP)
-    return call(finish_kernel, bf16(OWN, HEADS, HD), in_specs=[SMEM, VMEM, VMEM])(place, kept, received)
+
+    def combined(other):
+        return call(
+            functools.partial(combine_kernel, other),
+            half,
+            scratch_shapes=[pltpu.VMEM((XN, BLOCK, HD), jnp.bfloat16)],
+        )(parts)
+
+    received = lax.ppermute(combined(1), ALL, SWAP)
+    return call(finish_kernel, bf16(OWN, HEADS, HD))(combined(0), received)
 
 
 def solution(mesh):

time: 85.3 us -> 83.9 us (0.984)
  blocking collectives: 21.9 us -> 23.6 us
  starting transfers between devices: 35.2 us -> 34.1 us
  Pallas kernels: 12.9 us -> 12 us
    all_to_all x1, blocking collectives: 21.9 us -> 23.6 us  [body(): lax.all_to_all(parts, ALL, split_axis=0, concat_axis=0, axis_index_groups...]
    ppermute x1, starting transfers between devices: 2.95 us -> 1.92 us  [body(): received = lax.ppermute(combined(1), ALL, SWAP)]
    pallas_call x5 -> x6, Pallas kernels: 12.8 us -> 11.9 us  [the longest x1 7.46 us: attend(): call(attend_kernel, bf16(BLOCKS, WIRE, HD), megabytes=20, flops=230000000...]
where the time goes in v5:
time: 83.9 us; the launch traced here: 83.5 us
  starting transfers between devices  34.1 us (41%)
  blocking collectives  23.6 us (28%)
  waiting for transfers between devices  13 us (15%)
  Pallas kernels  12 us (14%)
    all_to_all x1, blocking collectives, body(): lax.all_to_all(parts, ALL, split_axis=0, concat_axis=0, axis_index_groups...  23.6 us
    ppermute x1, starting transfers between devices, body(): q_received = lax.ppermute(q_sent, ALL, SWAP)  8.22 us
    ppermute x1, waiting for transfers between devices, body(): above = lax.ppermute(two, ALL, along(-1))  8.13 us
    all_to_all x1, starting transfers between devices, body(): lax.all_to_all(q, ALL, split_axis=0, concat_axis=0, axis_index_groups=CRO...  7.5 us
    pallas_call x1, Pallas kernels, attend(): call(attend_kernel, bf16(BLOCKS, WIRE, HD), megabytes=20, flops=230000000...  7.46 us
    ppermute x1, starting transfers between devices, body(): lower = lax.ppermute(kv, ALL, along(3))  6.06 us
    ppermute x1, starting transfers between devices, body(): above = lax.ppermute(two, ALL, along(-1))  3.81 us
    ppermute x1, starting transfers between devices, body(): upper = lax.ppermute(kv, ALL, along(-3))  3.36 us
  transfers between devices with their start and end apart: 7, of which 4 were waited for; matrix products, arithmetic and copies ran while one was open for 0% of the time, Pallas kernels for 2%

profile of v5, /device:TPU:1, one launch (start us, length us, event | category | flops | bytes accessed | tf_op | source)
XLA Modules:
  0.0 83.5 jit_solution(3016511893115821521)
XLA Ops:
  0.0 0.0 copy-start
  0.0 0.7 copy-done
  0.7 1.5 %shard_map.73 = (bf16[2,416,128]{2,1,0:T(8,128)(2,1)S(1)}, bf16[2,4,16,128]{3,2,1,0:T(8,128)(2,1)S(1)}, bf16[2,4,16,128]{3,2,1,0:T(8,128)(2,1)S(1)}) custom-call(s32[16]{0:T(128)S(1)} %copy-done, bf16[2,4,2,16,128]{4,3,2,1,0:T(8,128)(2,1)} %bitcast.7, bf16[384,128]{1,0:T(8,128)(2,1)} %bitcast.5, bf16[384,128]{1,0:T(8,128)(2,1)} %bitcast.6, ...), custom_call_target="tpu_custom_call" | custom-call | flops 1000000 | bytes 800000 | tf_op jit(solution)/shard_map/pallas_call | solution.py:277
  2.2 6.1 %collective-permute-start = (bf16[2,416,128]{2,1,0:T(8,128)(2,1)S(1)}, bf16[2,416,128]{2,1,0:T(8,128)(2,1)S(1)}, u32[]{:S(2)}, u32[]{:S(2)}) collective-permute-start(bf16[2,416,128]{2,1,0:T(8,128)(2,1)S(1)} %get-tuple-element.10.own), channel_id=1, source_target_pairs={{0,192},{1,25},{2,194},{3,27},{4,196},{5,29},{6,198},{7,31},{8,200... | collective-permute-start | bytes 638984 | tf_op jit(solution)/shard_map/ppermute | solution.py:283
  8.3 3.4 %collective-permute-start.1 = (bf16[2,416,128]{2,1,0:T(8,128)(2,1)S(1)}, bf16[2,416,128]{2,1,0:T(8,128)(2,1)S(1)}, u32[]{:S(2)}, u32[]{:S(2)}) collective-permute-start(bf16[2,416,128]{2,1,0:T(8,128)(2,1)S(1)} %get-tuple-element.10.own), channel_id=1, source_target_pairs={{0,320},{1,41},{2,322},{3,43},{4,324},{5,45},{6,326},{7,47},{8,328... | collective-permute-start | bytes 638984 | tf_op jit(solution)/shard_map/ppermute | solution.py:284
  11.6 8.2 %collective-permute-start.4 = (bf16[2,4,16,128]{3,2,1,0:T(8,128)(2,1)S(1)}, bf16[2,4,16,128]{3,2,1,0:T(8,128)(2,1)S(1)}, u32[]{:S(2)}, u32[]{:S(2)}) collective-permute-start(bf16[2,4,16,128]{3,2,1,0:T(8,128)(2,1)S(1)} %get-tuple-element.14), channel_id=1, source_target_pairs={{0,1},{1,0},{2,3},{3,2},{4,5},{5,4},{6,7},{7,6},{8,9},{9,8},{10,11... | collective-permute-start | bytes 98312 | tf_op jit(solution)/shard_map/ppermute | solution.py:285
  19.9 0.8 %collective-permute-done.4.received = bf16[2,4,16,128]{3,2,1,0:T(8,128)(2,1)S(1)} collective-permute-done((bf16[2,4,16,128]{3,2,1,0:T(8,128)(2,1)S(1)}, bf16[2,4,16,128]{3,2,1,0:T(8,128)(2,1)S(1)}, u32[]{:S(2)}, u32[]{:S(2)}) %collective-permute-start.4) | collective-permute-done | bytes 32800 | tf_op jit(solution)/shard_map/ppermute | solution.py:285
  20.7 1.4 %shard_map.75 = bf16[32,72,128]{2,1,0:T(8,128)(2,1)} custom-call(s32[16]{0:T(128)S(1)} %copy-done, bf16[2,4,16,128]{3,2,1,0:T(8,128)(2,1)S(1)} %get-tuple-element.13.kept, bf16[2,4,16,128]{3,2,1,0:T(8,128)(2,1)S(1)} %collective-permute-done.4.received), custom_call_target="tpu_custom_call" | custom-call | flops 1000000 | bytes 800000 | tf_op jit(solution)/shard_map/pallas_call | solution.py:286
  22.1 7.5 %all-to-all-start = ((bf16[32,72,128]{2,1,0:T(8,128)(2,1)}), bf16[32,72,128]{2,1,0:T(8,128)(2,1)S(1)}, u32[]{:S(2)}, u32[]{:S(2)}) async-start(bf16[32,72,128]{2,1,0:T(8,128)(2,1)} %shard_map.75), calls=%async_computation | async-start | bytes 1179648 | tf_op jit(solution)/shard_map/all_to_all | solution.py:290
  29.6 0.0 collective-permute-done.lower
  29.7 0.0 collective-permute-done.1.upper
  29.7 0.1 shard_map.74
  29.8 0.0 copy-start.1
  29.8 3.2 %collective-permute-start.2 = (bf16[3,2,416,128]{3,2,1,0:T(8,128)(2,1)S(1)}, bf16[3,2,416,128]{3,2,1,0:T(8,128)(2,1)S(1)}, u32[]{:S(2)}, u32[]{:S(2)}) collective-permute-start(bf16[3,2,416,128]{3,2,1,0:T(8,128)(2,1)S(1)} %get-tuple-element.11), channel_id=1, source_target_pairs={{0,64},{1,9},{2,66},{3,11},{4,68},{5,13},{6,70},{7,15},{8,72},{9,1... | collective-permute-start | bytes 1916936 | tf_op jit(solution)/shard_map/ppermute | solution.py:291
  33.0 3.8 %collective-permute-start.3 = (bf16[2,2,416,128]{3,2,1,0:T(8,128)(2,1)S(1)}, bf16[2,2,416,128]{3,2,1,0:T(8,128)(2,1)S(1)}, u32[]{:S(2)}, u32[]{:S(2)}) collective-permute-start(bf16[2,2,416,128]{3,2,1,0:T(8,128)(2,1)S(1)} %get-tuple-element.12), channel_id=1, source_target_pairs={{0,448},{1,57},{2,450},{3,59},{4,452},{5,61},{6,454},{7,63},{8,456... | collective-permute-start | bytes 1277960 | tf_op jit(solution)/shard_map/ppermute | solution.py:292
  36.8 8.1 %collective-permute-done.3.above = bf16[2,2,416,128]{3,2,1,0:T(8,128)(2,1)S(1)} collective-permute-done((bf16[2,2,416,128]{3,2,1,0:T(8,128)(2,1)S(1)}, bf16[2,2,416,128]{3,2,1,0:T(8,128)(2,1)S(1)}, u32[]{:S(2)}, u32[]{:S(2)}) %collective-permute-start.3) | collective-permute-done | bytes 426016 | tf_op jit(solution)/shard_map/ppermute | solution.py:292
  45.0 3.3 %collective-permute-done.2.below = bf16[3,2,416,128]{3,2,1,0:T(8,128)(2,1)S(1)} collective-permute-done((bf16[3,2,416,128]{3,2,1,0:T(8,128)(2,1)S(1)}, bf16[3,2,416,128]{3,2,1,0:T(8,128)(2,1)S(1)}, u32[]{:S(2)}, u32[]{:S(2)}) %collective-permute-start.2) | collective-permute-done | bytes 639008 | tf_op jit(solution)/shard_map/ppermute | solution.py:291
  48.2 0.0 all-to-all-done.q
  48.2 0.0 copy-done.1
  48.3 7.5 %shard_map.76 = bf16[32,72,128]{2,1,0:T(8,128)(2,1)S(1)} custom-call(s32[128]{0:T(128)S(1)} %copy-done.1, bf16[2,416,128]{2,1,0:T(8,128)(2,1)S(1)} %get-tuple-element.10.own, bf16[2,416,128]{2,1,0:T(8,128)(2,1)S(1)} %collective-permute-done.lower, bf16[2,416,128]{2,1,0:T(8,128)(2,1)S(1)} %collective-permute-done.1.upper, ...), custom_call_target="tpu_custom_call" | custom-call | flops 2300000000 | bytes 5000000 | tf_op jit(solution)/shard_map/pallas_call | solution.py:223
  55.7 23.6 %all_to_all.10.parts = bf16[32,72,128]{2,1,0:T(8,128)(2,1)S(1)} all-to-all(bf16[32,72,128]{2,1,0:T(8,128)(2,1)S(1)} %shard_map.76), channel_id=1, replica_groups={{0,2,4,6,8,10,12,14,16,18,20,22,24,26,28,30,32,34,36,38,40,42,44,46,48,..., dimensions={0} | all-to-all | bytes 1179648 | tf_op jit(solution)/shard_map/all_to_all | solution.py:294
  79.3 0.4 shard_map.78
  79.7 1.9 %collective-permute-start.5 = (bf16[2,4,16,128]{3,2,1,0:T(8,128)(2,1)S(1)}, bf16[2,4,16,128]{3,2,1,0:T(8,128)(2,1)S(1)}, u32[]{:S(2)}, u32[]{:S(2)}) collective-permute-start(bf16[2,4,16,128]{3,2,1,0:T(8,128)(2,1)S(1)} %shard_map.78), channel_id=1, source_target_pairs={{0,1},{1,0},{2,3},{3,2},{4,5},{5,4},{6,7},{7,6},{8,9},{9,8},{10,11... | collective-permute-start | bytes 98312 | tf_op jit(solution)/shard_map/ppermute | solution.py:303
  81.7 0.4 shard_map.77.kept
  82.1 0.8 collective-permute-done.5.received
  82.8 0.6 shard_map.79
Async XLA Ops:
  0.0 0.7 copy-start
  2.2 27.4 %collective-permute-start = (bf16[2,416,128]{2,1,0:T(8,128)(2,1)S(1)}, bf16[2,416,128]{2,1,0:T(8,128)(2,1)S(1)}, u32[]{:S(2)}, u32[]{:S(2)}) collective-permute-start(bf16[2,416,128]{2,1,0:T(8,128)(2,1)S(1)} %get-tuple-element.10.own), channel_id=1, source_target_pairs={{0,192},{1,25},{2,194},{3,27},{4,196},{5,29},{6,198},{7,31},{8,200... | collective-permute-start | bytes 638984 | tf_op jit(solution)/shard_map/ppermute | solution.py:283
  8.3 21.4 %collective-permute-start.1 = (bf16[2,416,128]{2,1,0:T(8,128)(2,1)S(1)}, bf16[2,416,128]{2,1,0:T(8,128)(2,1)S(1)}, u32[]{:S(2)}, u32[]{:S(2)}) collective-permute-start(bf16[2,416,128]{2,1,0:T(8,128)(2,1)S(1)} %get-tuple-element.10.own), channel_id=1, source_target_pairs={{0,320},{1,41},{2,322},{3,43},{4,324},{5,45},{6,326},{7,47},{8,328... | collective-permute-start | bytes 638984 | tf_op jit(solution)/shard_map/ppermute | solution.py:284
  11.6 9.1 %collective-permute-start.4 = (bf16[2,4,16,128]{3,2,1,0:T(8,128)(2,1)S(1)}, bf16[2,4,16,128]{3,2,1,0:T(8,128)(2,1)S(1)}, u32[]{:S(2)}, u32[]{:S(2)}) collective-permute-start(bf16[2,4,16,128]{3,2,1,0:T(8,128)(2,1)S(1)} %get-tuple-element.14), channel_id=1, source_target_pairs={{0,1},{1,0},{2,3},{3,2},{4,5},{5,4},{6,7},{7,6},{8,9},{9,8},{10,11... | collective-permute-start | bytes 98312 | tf_op jit(solution)/shard_map/ppermute | solution.py:285
  22.1 26.1 %all-to-all-start = ((bf16[32,72,128]{2,1,0:T(8,128)(2,1)}), bf16[32,72,128]{2,1,0:T(8,128)(2,1)S(1)}, u32[]{:S(2)}, u32[]{:S(2)}) async-start(bf16[32,72,128]{2,1,0:T(8,128)(2,1)} %shard_map.75), calls=%async_computation | async-start | bytes 1179648 | tf_op jit(solution)/shard_map/all_to_all | solution.py:290
  29.8 18.5 %copy-start.1 = (s32[128]{0:T(128)S(1)}, s32[128]{0:T(128)}, u32[]{:S(2)}) copy-start(s32[128]{0:T(128)} %page_slots.1) | copy-start | bytes 1540
  29.8 18.4 %collective-permute-start.2 = (bf16[3,2,416,128]{3,2,1,0:T(8,128)(2,1)S(1)}, bf16[3,2,416,128]{3,2,1,0:T(8,128)(2,1)S(1)}, u32[]{:S(2)}, u32[]{:S(2)}) collective-permute-start(bf16[3,2,416,128]{3,2,1,0:T(8,128)(2,1)S(1)} %get-tuple-element.11), channel_id=1, source_target_pairs={{0,64},{1,9},{2,66},{3,11},{4,68},{5,13},{6,70},{7,15},{8,72},{9,1... | collective-permute-start | bytes 1916936 | tf_op jit(solution)/shard_map/ppermute | solution.py:291
  33.0 12.0 %collective-permute-start.3 = (bf16[2,2,416,128]{3,2,1,0:T(8,128)(2,1)S(1)}, bf16[2,2,416,128]{3,2,1,0:T(8,128)(2,1)S(1)}, u32[]{:S(2)}, u32[]{:S(2)}) collective-permute-start(bf16[2,2,416,128]{3,2,1,0:T(8,128)(2,1)S(1)} %get-tuple-element.12), channel_id=1, source_target_pairs={{0,448},{1,57},{2,450},{3,59},{4,452},{5,61},{6,454},{7,63},{8,456... | collective-permute-start | bytes 1277960 | tf_op jit(solution)/shard_map/ppermute | solution.py:292
  79.7 3.1 %collective-permute-start.5 = (bf16[2,4,16,128]{3,2,1,0:T(8,128)(2,1)S(1)}, bf16[2,4,16,128]{3,2,1,0:T(8,128)(2,1)S(1)}, u32[]{:S(2)}, u32[]{:S(2)}) collective-permute-start(bf16[2,4,16,128]{3,2,1,0:T(8,128)(2,1)S(1)} %shard_map.78), channel_id=1, source_target_pairs={{0,1},{1,0},{2,3},{3,2},{4,5},{5,4},{6,7},{7,6},{8,9},{9,8},{10,11... | collective-permute-start | bytes 98312 | tf_op jit(solution)/shard_map/ppermute | solution.py:303

commit v6 on v5

--- a/solution.py
+++ b/solution.py
@@ -11,6 +11,7 @@
 
 ZN, YN, XN, CN = 8, 8, 4, 2
 LINE = 8
+KN = XN * CN
 ALL = ("z", "y", "x", "c")
 HEADS, GROUP, HD, PAGE, SLOTS, NEWT = 128, 16, 128, 128, 3, 16
 HISTORY = SLOTS * PAGE
@@ -21,19 +22,26 @@
 OWN = 2
 TOKENS = OWN * CN
 BLOCK = TOKENS * GROUP
+LINE_ROWS = NEWT * GROUP
+LINE_WIRE = LINE_ROWS + 2 * NEWT
 WIRE = BLOCK + 8
 BLOCKS = LINE * XN
-STEP_BLOCKS = 8
+STEP_LINES = 2
+STEP_BLOCKS = STEP_LINES * XN
 ROWS = STEP_BLOCKS * BLOCK
 PARTS = BLOCKS // STEP_BLOCKS
 CHUNK = 512
 SIZES = (16, 18, 20, 24)
-OFFSETS = (0, -3, 3, -1, -4, 2, 1, -2)
+OFFSETS = (0, -3, 2, 1, -2, 3, -1, -4)
 TO_BITS = math.log2(math.e) / math.sqrt(HD)
 LOWEST = -1e30
+JOIN = 30000000000
 
 IDS = np.arange(ZN * YN * XN * CN).reshape(ZN, YN, XN, CN)
 CROSS = [IDS[z, :, :, 0].ravel().tolist() for z in range(ZN)] + [IDS[:, y, :, 1].ravel().tolist() for y in range(YN)]
+
+CROSS_LINES = [IDS[z, :, x, 0].tolist() for z in range(ZN) for x in range(XN)]
+CROSS_LINES += [IDS[:, y, x, 1].tolist() for y in range(YN) for x in range(XN)]
 
 
 def along(distance):
@@ -73,46 +81,43 @@
     return core, jnp.where(core == 0, lax.axis_index("z"), lax.axis_index("y"))
 
 
-def pack_kernel(positions, queries, hist_keys, hist_values, new_keys, new_values, kv, kept, sent, arrived):
+def pack_kernel(positions, queries, hist_keys, hist_values, new_keys, new_values, kv, sent, tags, at, arrived):
     core, line = own_place()
+    first = pltpu.make_async_copy(positions, at, arrived.at[6])
     copies = [
         pltpu.make_async_copy(hist_keys, kv.at[0, pl.ds(0, HISTORY)], arrived.at[0]),
         pltpu.make_async_copy(hist_values, kv.at[1, pl.ds(0, HISTORY)], arrived.at[1]),
         pltpu.make_async_copy(new_keys, kv.at[0, pl.ds(HISTORY, NEWT)], arrived.at[2]),
         pltpu.make_async_copy(new_values, kv.at[1, pl.ds(HISTORY, NEWT)], arrived.at[3]),
-        pltpu.make_async_copy(queries.at[:, :, core], kept, arrived.at[4]),
-        pltpu.make_async_copy(queries.at[:, :, 1 - core], sent, arrived.at[5]),
+        pltpu.make_async_copy(queries.at[0], sent.at[:, 0], arrived.at[4]),
+        pltpu.make_async_copy(queries.at[1], sent.at[:, 1], arrived.at[5]),
     ]
+    for copy in [first] + copies:
+        copy.start()
+    first.wait()
+    lane = lax.broadcasted_iota(jnp.int32, (NEWT, HD), 1)
+    row = lax.broadcasted_iota(jnp.int32, (NEWT, HD), 0)
+    key_tag = jnp.zeros((NEWT, HD), jnp.int32)
+    query_tag = jnp.zeros((NEWT, HD), jnp.int32)
+    for i in range(NEWT):
+        key_tag = jnp.where(lane == line * NEWT + i, at[i], key_tag)
+        query_tag = jnp.where(row == i, at[i], query_tag)
+    for side, digit in enumerate((lambda tag: tag // 32, lambda tag: tag % 32)):
+        kv[side, HISTORY + NEWT :, :] = digit(key_tag).astype(jnp.float32).astype(jnp.bfloat16)
+        tags[side * NEWT : (side + 1) * NEWT, :] = digit(query_tag).astype(jnp.float32).astype(jnp.bfloat16)
+    for copy in copies:
+        copy.wait()
+
+
+def spread_kernel(queries, tags, out, done):
+    copies = []
+    for line in range(LINE):
+        copies.append(pltpu.make_async_copy(queries, out.at[line, pl.ds(0, LINE_ROWS)], done.at[2 * line]))
+        copies.append(pltpu.make_async_copy(tags, out.at[line, pl.ds(LINE_ROWS, 2 * NEWT)], done.at[2 * line + 1]))
     for copy in copies:
         copy.start()
-    lane = lax.broadcasted_iota(jnp.int32, (NEWT, HD), 1)
-    tag = jnp.zeros((NEWT, HD), jnp.int32)
-    for i in range(NEWT):
-        tag = jnp.where(lane == line * NEWT + i, positions[i], tag)
-    for side, digit in enumerate((tag // 32, tag % 32)):
-        kv[side, HISTORY + NEWT :, :] = digit.astype(jnp.float32).astype(jnp.bfloat16)
     for copy in copies:
         copy.wait()
-
-
-def spread_kernel(positions, kept, received, out):
-    core, x_here = lax.axis_index("c"), lax.axis_index("x")
-    row = lax.broadcasted_iota(jnp.int32, (8, HD), 0)
-    tag = jnp.zeros((8, HD), jnp.int32)
-    for i in range(TOKENS):
-        position = positions[x_here * TOKENS + i]
-        tag = jnp.where(row == 2 * i, position // 32, tag)
-        tag = jnp.where(row == 2 * i + 1, position % 32, tag)
-    tag = tag.astype(jnp.float32).astype(jnp.bfloat16)
-    for x in range(XN):
-        for other, array in ((0, kept), (1, received)):
-            owner = core if other == 0 else 1 - core
-            rows = array[:, x].reshape(OWN * GROUP, HD)
-            first = pl.multiple_of(owner * OWN * GROUP, OWN * GROUP)
-            for line in range(LINE):
-                out[line * XN + x, pl.ds(first, OWN * GROUP), :] = rows
-        for line in range(LINE):
-            out[line * XN + x, BLOCK:, :] = tag
 
 
 def join_kernel(own, lower, upper, three, two):
@@ -122,12 +127,12 @@
             two[i] = block[...]
 
 
-def attend_kernel(page_slots, own, lower, upper, below, above, q, out, keys, values, scores):
+def attend_kernel(page_slots, own, lower, upper, above, below, q, out, keys, values, scores):
     core, line = own_place()
     ctx = lax.axis_index("z") * YN + lax.axis_index("y")
     stride = jnp.where(core == 0, YN, 1)
     values[:, HD:] = jnp.ones((KEYS, HD), jnp.bfloat16)
-    blocks = [own, lower, upper] + [below.at[i] for i in range(3)] + [above.at[i] for i in range(2)]
+    blocks = [own, lower, upper] + [above.at[i] for i in range(3)] + [below.at[i] for i in range(2)]
     high = jnp.zeros((NEWT, HD), jnp.float32)
     low = jnp.zeros((NEWT, HD), jnp.float32)
     count = jnp.int32(0)
@@ -165,15 +170,12 @@
         return [(start, min(CHUNK, end - start)) for start in range(0, end, CHUNK)]
 
     def score(part, side, pages):
-        here = pl.ds(part * STEP_BLOCKS, STEP_BLOCKS)
-        rows = q[here, :BLOCK, :].reshape(ROWS, HD)
-        tags = q[here, BLOCK:, :].astype(jnp.float32)
-        bias = []
-        for t in range(TOKENS):
-            query_at = tags[:, 2 * t, :] * 32.0 + tags[:, 2 * t + 1, :]
-            hidden = jnp.where(key_at <= query_at, 0.0, LOWEST)
-            bias.append(jnp.broadcast_to(hidden[:, None, :], (STEP_BLOCKS, GROUP, HD)))
-        bias = jnp.stack(bias, axis=1).reshape(ROWS, HD)
+        here = pl.ds(part * STEP_LINES, STEP_LINES)
+        rows = q[here, :LINE_ROWS, :].reshape(ROWS, HD)
+        tags = q[here, LINE_ROWS:, :].astype(jnp.float32)
+        query_at = tags[:, :NEWT, :] * 32.0 + tags[:, NEWT:, :]
+        hidden = jnp.where(key_at <= query_at, 0.0, LOWEST)
+        bias = jnp.broadcast_to(hidden[:, :, None, :], (STEP_LINES, NEWT, GROUP, HD)).reshape(ROWS, HD)
         top = None
         for start, size in chunks(pages):
             product = lax.dot_general(
@@ -268,29 +270,33 @@
 def body(queries, new_keys, new_values, new_positions, hist_keys, hist_values, page_slots):
     half = bf16(OWN, XN, GROUP, HD)
     sources = [
-        queries.reshape(OWN, XN, CN, GROUP, HD),
+        new_positions,
+        queries.reshape(OWN, KN, GROUP, HD),
         hist_keys.reshape(HISTORY, HD),
         hist_values.reshape(HISTORY, HD),
         new_keys.reshape(NEWT, HD),
         new_values.reshape(NEWT, HD),
     ]
-    kv, q_kept, q_sent = call(
+    kv, q_sent, tags = call(
         pack_kernel,
-        (bf16(2, KV_ROWS, HD), half, half),
-        in_specs=[SMEM] + [HBM] * 5,
-        scratch_shapes=[pltpu.SemaphoreType.DMA((6,))],
-    )(new_positions, *(pltpu.with_memory_space_constraint(source, pltpu.HBM) for source in sources))
+        (bf16(2, KV_ROWS, HD), bf16(KN, OWN, GROUP, HD), bf16(2 * NEWT, HD)),
+        in_specs=[HBM] * 6,
+        scratch_shapes=[pltpu.SMEM((NEWT,), jnp.int32), pltpu.SemaphoreType.DMA((7,))],
+    )(*(pltpu.with_memory_space_constraint(source, pltpu.HBM) for source in sources))
     lower = lax.ppermute(kv, ALL, along(3))
-    upper = lax.ppermute(kv, ALL, along(-3))
-    q_received = lax.ppermute(q_sent, ALL, SWAP)
-    q = call(spread_kernel, bf16(BLOCKS, WIRE, HD), in_specs=[SMEM, VMEM, VMEM])(
-        new_positions, q_kept, q_received
-    )
-    three, two = call(join_kernel, (bf16(3, 2, KV_ROWS, HD), bf16(2, 2, KV_ROWS, HD)), flops=30000000000)(kv, lower, upper)
-    q = lax.all_to_all(q, ALL, split_axis=0, concat_axis=0, axis_index_groups=CROSS, tiled=True)
-    below = lax.ppermute(three, ALL, along(1))
-    above = lax.ppermute(two, ALL, along(-1))
-    parts = attend(page_slots, (kv, lower, upper, below, above), q)
+    upper = lax.ppermute(kv, ALL, along(-2))
+    q = lax.all_to_all(q_sent, ("x", "c"), split_axis=0, concat_axis=0, tiled=True)
+    q = call(
+        spread_kernel,
+        bf16(LINE, LINE_WIRE, HD),
+        out_specs=HBM,
+        scratch_shapes=[pltpu.SemaphoreType.DMA((2 * LINE,))],
+    )(q.reshape(LINE_ROWS, HD), tags)
+    q = lax.all_to_all(q, ALL, split_axis=0, concat_axis=0, axis_index_groups=CROSS_LINES, tiled=True)
+    three, two = call(join_kernel, (bf16(3, 2, KV_ROWS, HD), bf16(2, 2, KV_ROWS, HD)), flops=JOIN)(kv, lower, upper)
+    above = lax.ppermute(three, ALL, along(-1))
+    below = lax.ppermute(two, ALL, along(1))
+    parts = attend(page_slots, (kv, lower, upper, above, below), q)
     parts = lax.all_to_all(parts, ALL, split_axis=0, concat_axis=0, axis_index_groups=CROSS, tiled=True)
 
     def combined(other):

time: 83.9 us -> 83.1 us (level)
  blocking collectives: 23.6 us -> 33.7 us
  starting transfers between devices: 34.1 us -> 26.7 us
  waiting for transfers between devices: 13 us -> 11.2 us
  Pallas kernels: 12 us -> 11 us
    all_to_all x0 -> x1, blocking collectives: none -> 14.1 us  [body(): lax.all_to_all(q_sent, ('x', 'c'), split_axis=0, concat_axis=0, tiled=True)]
    ppermute x4 -> x3, starting transfers between devices: 18.6 us -> 10.2 us  [the longest x1 5.1 us: body(): above = lax.ppermute(three, ALL, along(-1))]
    all_to_all x1, blocking collectives: 23.6 us -> 19.7 us  [body(): lax.all_to_all(parts, ALL, split_axis=0, concat_axis=0, axis_index_groups...]
    ppermute x1, starting transfers between devices: 1.92 us -> 4.43 us  [body(): received = lax.ppermute(combined(1), ALL, SWAP)]
    ppermute x4 -> x3, waiting for transfers between devices: 12.2 us -> 10.7 us  [the longest x1 10.3 us: body(): below = lax.ppermute(two, ALL, along(1))]
    all_to_all x1, starting transfers between devices: 7.5 us -> 6.03 us  [body(): lax.all_to_all(q, ALL, split_axis=0, concat_axis=0, axis_index_groups=CRO...]
    pallas_call x2, Pallas kernels: 2.97 us -> 1.97 us  [the longest x1 1.01 us: body(): call(pack_kernel, (bf16(2, KV_ROWS, HD), bf16(KN, OWN, GROUP, HD), bf16(2...]
  transfers between devices with their start and end apart: 7 -> 6, of which waited for: 4 -> 3; matrix products, arithmetic and copies ran while one was open for 0% -> 0% of each run, Pallas kernels for 2% -> 2%
where the time goes in v6:
time: 83.1 us; the launch traced here: 82.7 us
  blocking collectives  33.7 us (41%)
  starting transfers between devices  26.7 us (32%)
  waiting for transfers between devices  11.2 us (13%)
  Pallas kernels  11 us (13%)
    all_to_all x1, blocking collectives, body(): lax.all_to_all(parts, ALL, split_axis=0, concat_axis=0, axis_index_groups...  19.7 us
    all_to_all x1, blocking collectives, body(): lax.all_to_all(q_sent, ('x', 'c'), split_axis=0, concat_axis=0, tiled=True)  14.1 us
    ppermute x1, waiting for transfers between devices, body(): below = lax.ppermute(two, ALL, along(1))  10.3 us
    pallas_call x1, Pallas kernels, attend(): call(attend_kernel, bf16(BLOCKS, WIRE, HD), megabytes=20, flops=230000000...  7.45 us
    ppermute x1, starting transfers between devices, body(): lower = lax.ppermute(kv, ALL, along(3))  6.06 us
    all_to_all x1, starting transfers between devices, body(): lax.all_to_all(q, ALL, split_axis=0, concat_axis=0, axis_index_groups=CRO...  6.03 us
    ppermute x1, starting transfers between devices, body(): above = lax.ppermute(three, ALL, along(-1))  5.1 us
    ppermute x1, starting transfers between devices, body(): received = lax.ppermute(combined(1), ALL, SWAP)  4.43 us
  transfers between devices with their start and end apart: 6, of which 3 were waited for; matrix products, arithmetic and copies ran while one was open for 0% of the time, Pallas kernels for 2%

profile of v6, /device:TPU:1, one launch (start us, length us, event | category | flops | bytes accessed | tf_op | source)
XLA Modules:
  0.0 82.7 jit_solution(14560812523019655890)
XLA Ops:
  0.0 1.0 %shard_map.73 = (bf16[2,416,128]{2,1,0:T(8,128)(2,1)S(1)}, bf16[8,2,16,128]{3,2,1,0:T(8,128)(2,1)S(1)}, bf16[32,128]{1,0:T(8,128)(2,1)S(1)}) custom-call(s32[16]{0:T(128)} %positions.1, bf16[2,8,16,128]{3,2,1,0:T(8,128)(2,1)} %bitcast.9, bf16[384,128]{1,0:T(8,128)(2,1)} %bitcast.7, bf16[384,128]{1,0:T(8,128)(2,1)} %bitcast.8, bf16[16,128]{1,0:T(8,128)(2,1)} %bitcast.10, ...), custom_call_target="tpu_custom_call" | custom-call | flops 1000000 | bytes 800000 | tf_op jit(solution)/shard_map/pallas_call | solution.py:280
  1.0 6.1 %collective-permute-start = (bf16[2,416,128]{2,1,0:T(8,128)(2,1)S(1)}, bf16[2,416,128]{2,1,0:T(8,128)(2,1)S(1)}, u32[]{:S(2)}, u32[]{:S(2)}) collective-permute-start(bf16[2,416,128]{2,1,0:T(8,128)(2,1)S(1)} %get-tuple-element.10.own), channel_id=1, source_target_pairs={{0,192},{1,25},{2,194},{3,27},{4,196},{5,29},{6,198},{7,31},{8,200... | collective-permute-start | bytes 638984 | tf_op jit(solution)/shard_map/ppermute | solution.py:286
  7.1 3.2 %collective-permute-start.1 = (bf16[2,416,128]{2,1,0:T(8,128)(2,1)S(1)}, bf16[2,416,128]{2,1,0:T(8,128)(2,1)S(1)}, u32[]{:S(2)}, u32[]{:S(2)}) collective-permute-start(bf16[2,416,128]{2,1,0:T(8,128)(2,1)S(1)} %get-tuple-element.10.own), channel_id=1, source_target_pairs={{0,384},{1,49},{2,386},{3,51},{4,388},{5,53},{6,390},{7,55},{8,392... | collective-permute-start | bytes 638984 | tf_op jit(solution)/shard_map/ppermute | solution.py:287
  10.3 14.1 %all_to_all.15 = bf16[8,2,16,128]{3,2,1,0:T(8,128)(2,1)S(1)} all-to-all(bf16[8,2,16,128]{3,2,1,0:T(8,128)(2,1)S(1)} %get-tuple-element.13), channel_id=1, replica_groups=mesh['z'=8,'y'=8,'x'=4,'c'=2] {'x','c'}, dimensions={0} | all-to-all | bytes 131072 | tf_op jit(solution)/shard_map/all_to_all | solution.py:288
  24.3 1.0 %shard_map.75 = bf16[8,288,128]{2,1,0:T(8,128)(2,1)} custom-call(bf16[256,128]{1,0:T(8,128)(2,1)S(1)} %bitcast.6, bf16[32,128]{1,0:T(8,128)(2,1)S(1)} %get-tuple-element.14.tags), custom_call_target="tpu_custom_call" | custom-call | flops 1000000 | bytes 800000 | tf_op jit(solution)/shard_map/pallas_call | solution.py:289
  25.3 6.0 %all-to-all-start.1 = ((bf16[8,288,128]{2,1,0:T(8,128)(2,1)}), bf16[8,288,128]{2,1,0:T(8,128)(2,1)S(1)}, u32[]{:S(2)}, u32[]{:S(2)}) async-start(bf16[8,288,128]{2,1,0:T(8,128)(2,1)} %shard_map.75), calls=%async_computation.1 | async-start | bytes 1179648 | tf_op jit(solution)/shard_map/all_to_all | solution.py:295
  31.3 0.0 collective-permute-done.lower
  31.3 0.0 collective-permute-done.1.upper
  31.4 0.1 shard_map.74
  31.5 0.0 copy-start
  31.5 5.1 %collective-permute-start.2 = (bf16[3,2,416,128]{3,2,1,0:T(8,128)(2,1)S(1)}, bf16[3,2,416,128]{3,2,1,0:T(8,128)(2,1)S(1)}, u32[]{:S(2)}, u32[]{:S(2)}) collective-permute-start(bf16[3,2,416,128]{3,2,1,0:T(8,128)(2,1)S(1)} %get-tuple-element.11), channel_id=1, source_target_pairs={{0,448},{1,57},{2,450},{3,59},{4,452},{5,61},{6,454},{7,63},{8,456... | collective-permute-start | bytes 1916936 | tf_op jit(solution)/shard_map/ppermute | solution.py:297
  36.6 1.9 %collective-permute-start.3 = (bf16[2,2,416,128]{3,2,1,0:T(8,128)(2,1)S(1)}, bf16[2,2,416,128]{3,2,1,0:T(8,128)(2,1)S(1)}, u32[]{:S(2)}, u32[]{:S(2)}) collective-permute-start(bf16[2,2,416,128]{3,2,1,0:T(8,128)(2,1)S(1)} %get-tuple-element.12), channel_id=1, source_target_pairs={{0,64},{1,9},{2,66},{3,11},{4,68},{5,13},{6,70},{7,15},{8,72},{9,1... | collective-permute-start | bytes 1277960 | tf_op jit(solution)/shard_map/ppermute | solution.py:298
  38.5 10.3 %collective-permute-done.3.below = bf16[2,2,416,128]{3,2,1,0:T(8,128)(2,1)S(1)} collective-permute-done((bf16[2,2,416,128]{3,2,1,0:T(8,128)(2,1)S(1)}, bf16[2,2,416,128]{3,2,1,0:T(8,128)(2,1)S(1)}, u32[]{:S(2)}, u32[]{:S(2)}) %collective-permute-start.3) | collective-permute-done | bytes 426016 | tf_op jit(solution)/shard_map/ppermute | solution.py:298
  48.8 0.4 collective-permute-done.2.above
  49.2 0.0 all-to-all-done.1.q
  49.2 0.0 copy-done
  49.2 7.5 %shard_map.76 = bf16[32,72,128]{2,1,0:T(8,128)(2,1)S(1)} custom-call(s32[128]{0:T(128)S(1)} %copy-done, bf16[2,416,128]{2,1,0:T(8,128)(2,1)S(1)} %get-tuple-element.10.own, bf16[2,416,128]{2,1,0:T(8,128)(2,1)S(1)} %collective-permute-done.lower, bf16[2,416,128]{2,1,0:T(8,128)(2,1)S(1)} %collective-permute-done.1.upper, ...), custom_call_target="tpu_custom_call" | custom-call | flops 2300000000 | bytes 5000000 | tf_op jit(solution)/shard_map/pallas_call | solution.py:225
  56.7 19.7 %all_to_all.16.parts = bf16[32,72,128]{2,1,0:T(8,128)(2,1)S(1)} all-to-all(bf16[32,72,128]{2,1,0:T(8,128)(2,1)S(1)} %shard_map.76), channel_id=1, replica_groups={{0,2,4,6,8,10,12,14,16,18,20,22,24,26,28,30,32,34,36,38,40,42,44,46,48,..., dimensions={0} | all-to-all | bytes 1179648 | tf_op jit(solution)/shard_map/all_to_all | solution.py:300
  76.4 0.4 shard_map.78
  76.8 4.4 %collective-permute-start.4 = (bf16[2,4,16,128]{3,2,1,0:T(8,128)(2,1)S(1)}, bf16[2,4,16,128]{3,2,1,0:T(8,128)(2,1)S(1)}, u32[]{:S(2)}, u32[]{:S(2)}) collective-permute-start(bf16[2,4,16,128]{3,2,1,0:T(8,128)(2,1)S(1)} %shard_map.78), channel_id=1, source_target_pairs={{0,1},{1,0},{2,3},{3,2},{4,5},{5,4},{6,7},{7,6},{8,9},{9,8},{10,11... | collective-permute-start | bytes 98312 | tf_op jit(solution)/shard_map/ppermute | solution.py:309
  81.2 0.4 shard_map.77.kept
  81.6 0.4 collective-permute-done.4.received
  82.1 0.6 shard_map.79
Async XLA Ops:
  1.0 30.3 %collective-permute-start = (bf16[2,416,128]{2,1,0:T(8,128)(2,1)S(1)}, bf16[2,416,128]{2,1,0:T(8,128)(2,1)S(1)}, u32[]{:S(2)}, u32[]{:S(2)}) collective-permute-start(bf16[2,416,128]{2,1,0:T(8,128)(2,1)S(1)} %get-tuple-element.10.own), channel_id=1, source_target_pairs={{0,192},{1,25},{2,194},{3,27},{4,196},{5,29},{6,198},{7,31},{8,200... | collective-permute-start | bytes 638984 | tf_op jit(solution)/shard_map/ppermute | solution.py:286
  7.1 24.3 %collective-permute-start.1 = (bf16[2,416,128]{2,1,0:T(8,128)(2,1)S(1)}, bf16[2,416,128]{2,1,0:T(8,128)(2,1)S(1)}, u32[]{:S(2)}, u32[]{:S(2)}) collective-permute-start(bf16[2,416,128]{2,1,0:T(8,128)(2,1)S(1)} %get-tuple-element.10.own), channel_id=1, source_target_pairs={{0,384},{1,49},{2,386},{3,51},{4,388},{5,53},{6,390},{7,55},{8,392... | collective-permute-start | bytes 638984 | tf_op jit(solution)/shard_map/ppermute | solution.py:287
  25.3 23.9 %all-to-all-start.1 = ((bf16[8,288,128]{2,1,0:T(8,128)(2,1)}), bf16[8,288,128]{2,1,0:T(8,128)(2,1)S(1)}, u32[]{:S(2)}, u32[]{:S(2)}) async-start(bf16[8,288,128]{2,1,0:T(8,128)(2,1)} %shard_map.75), calls=%async_computation.1 | async-start | bytes 1179648 | tf_op jit(solution)/shard_map/all_to_all | solution.py:295
  31.5 17.8 %copy-start = (s32[128]{0:T(128)S(1)}, s32[128]{0:T(128)}, u32[]{:S(2)}) copy-start(s32[128]{0:T(128)} %page_slots.1) | copy-start | bytes 1540
  31.5 17.7 %collective-permute-start.2 = (bf16[3,2,416,128]{3,2,1,0:T(8,128)(2,1)S(1)}, bf16[3,2,416,128]{3,2,1,0:T(8,128)(2,1)S(1)}, u32[]{:S(2)}, u32[]{:S(2)}) collective-permute-start(bf16[3,2,416,128]{3,2,1,0:T(8,128)(2,1)S(1)} %get-tuple-element.11), channel_id=1, source_target_pairs={{0,448},{1,57},{2,450},{3,59},{4,452},{5,61},{6,454},{7,63},{8,456... | collective-permute-start | bytes 1916936 | tf_op jit(solution)/shard_map/ppermute | solution.py:297
  36.6 12.2 %collective-permute-start.3 = (bf16[2,2,416,128]{3,2,1,0:T(8,128)(2,1)S(1)}, bf16[2,2,416,128]{3,2,1,0:T(8,128)(2,1)S(1)}, u32[]{:S(2)}, u32[]{:S(2)}) collective-permute-start(bf16[2,2,416,128]{3,2,1,0:T(8,128)(2,1)S(1)} %get-tuple-element.12), channel_id=1, source_target_pairs={{0,64},{1,9},{2,66},{3,11},{4,68},{5,13},{6,70},{7,15},{8,72},{9,1... | collective-permute-start | bytes 1277960 | tf_op jit(solution)/shard_map/ppermute | solution.py:298
  76.8 5.3 %collective-permute-start.4 = (bf16[2,4,16,128]{3,2,1,0:T(8,128)(2,1)S(1)}, bf16[2,4,16,128]{3,2,1,0:T(8,128)(2,1)S(1)}, u32[]{:S(2)}, u32[]{:S(2)}) collective-permute-start(bf16[2,4,16,128]{3,2,1,0:T(8,128)(2,1)S(1)} %shard_map.78), channel_id=1, source_target_pairs={{0,1},{1,0},{2,3},{3,2},{4,5},{5,4},{6,7},{7,6},{8,9},{9,8},{10,11... | collective-permute-start | bytes 98312 | tf_op jit(solution)/shard_map/ppermute | solution.py:309

commit v7 on v6

--- a/solution.py
+++ b/solution.py
@@ -11,7 +11,6 @@
 
 ZN, YN, XN, CN = 8, 8, 4, 2
 LINE = 8
-KN = XN * CN
 ALL = ("z", "y", "x", "c")
 HEADS, GROUP, HD, PAGE, SLOTS, NEWT = 128, 16, 128, 128, 3, 16
 HISTORY = SLOTS * PAGE
@@ -22,12 +21,9 @@
 OWN = 2
 TOKENS = OWN * CN
 BLOCK = TOKENS * GROUP
-LINE_ROWS = NEWT * GROUP
-LINE_WIRE = LINE_ROWS + 2 * NEWT
 WIRE = BLOCK + 8
 BLOCKS = LINE * XN
-STEP_LINES = 2
-STEP_BLOCKS = STEP_LINES * XN
+STEP_BLOCKS = 8
 ROWS = STEP_BLOCKS * BLOCK
 PARTS = BLOCKS // STEP_BLOCKS
 CHUNK = 512
@@ -40,9 +36,6 @@
 IDS = np.arange(ZN * YN * XN * CN).reshape(ZN, YN, XN, CN)
 CROSS = [IDS[z, :, :, 0].ravel().tolist() for z in range(ZN)] + [IDS[:, y, :, 1].ravel().tolist() for y in range(YN)]
 
-CROSS_LINES = [IDS[z, :, x, 0].tolist() for z in range(ZN) for x in range(XN)]
-CROSS_LINES += [IDS[:, y, x, 1].tolist() for y in range(YN) for x in range(XN)]
-
 
 def along(distance):
     route = []
@@ -81,7 +74,9 @@
     return core, jnp.where(core == 0, lax.axis_index("z"), lax.axis_index("y"))
 
 
-def pack_kernel(positions, queries, hist_keys, hist_values, new_keys, new_values, kv, sent, tags, at, arrived):
+def pack_kernel(
+    positions, queries, hist_keys, hist_values, new_keys, new_values, kv, kept, sent, tags, at, arrived
+):
     core, line = own_place()
     first = pltpu.make_async_copy(positions, at, arrived.at[6])
     copies = [
@@ -89,31 +84,39 @@
         pltpu.make_async_copy(hist_values, kv.at[1, pl.ds(0, HISTORY)], arrived.at[1]),
         pltpu.make_async_copy(new_keys, kv.at[0, pl.ds(HISTORY, NEWT)], arrived.at[2]),
         pltpu.make_async_copy(new_values, kv.at[1, pl.ds(HISTORY, NEWT)], arrived.at[3]),
-        pltpu.make_async_copy(queries.at[0], sent.at[:, 0], arrived.at[4]),
-        pltpu.make_async_copy(queries.at[1], sent.at[:, 1], arrived.at[5]),
+        pltpu.make_async_copy(queries.at[:, :, core], kept, arrived.at[4]),
+        pltpu.make_async_copy(queries.at[:, :, 1 - core], sent, arrived.at[5]),
     ]
     for copy in [first] + copies:
         copy.start()
     first.wait()
     lane = lax.broadcasted_iota(jnp.int32, (NEWT, HD), 1)
-    row = lax.broadcasted_iota(jnp.int32, (NEWT, HD), 0)
+    row = lax.broadcasted_iota(jnp.int32, (8, HD), 0)
     key_tag = jnp.zeros((NEWT, HD), jnp.int32)
-    query_tag = jnp.zeros((NEWT, HD), jnp.int32)
     for i in range(NEWT):
         key_tag = jnp.where(lane == line * NEWT + i, at[i], key_tag)
-        query_tag = jnp.where(row == i, at[i], query_tag)
-    for side, digit in enumerate((lambda tag: tag // 32, lambda tag: tag % 32)):
-        kv[side, HISTORY + NEWT :, :] = digit(key_tag).astype(jnp.float32).astype(jnp.bfloat16)
-        tags[side * NEWT : (side + 1) * NEWT, :] = digit(query_tag).astype(jnp.float32).astype(jnp.bfloat16)
+    for side, digit in enumerate((key_tag // 32, key_tag % 32)):
+        kv[side, HISTORY + NEWT :, :] = digit.astype(jnp.float32).astype(jnp.bfloat16)
+    query_tag = jnp.zeros((8, HD), jnp.int32)
+    for i in range(TOKENS):
+        position = at[lax.axis_index("x") * TOKENS + i]
+        query_tag = jnp.where(row == i, position // 32, query_tag)
+        query_tag = jnp.where(row == TOKENS + i, position % 32, query_tag)
+    tags[...] = query_tag.astype(jnp.float32).astype(jnp.bfloat16)
     for copy in copies:
         copy.wait()
 
 
-def spread_kernel(queries, tags, out, done):
-    copies = []
-    for line in range(LINE):
-        copies.append(pltpu.make_async_copy(queries, out.at[line, pl.ds(0, LINE_ROWS)], done.at[2 * line]))
-        copies.append(pltpu.make_async_copy(tags, out.at[line, pl.ds(LINE_ROWS, 2 * NEWT)], done.at[2 * line + 1]))
+def spread_kernel(kept, received, tags, out, blocks, done):
+    core = lax.axis_index("c")
+    for x in range(XN):
+        for owner, array in ((core, kept), (1 - core, received)):
+            first = pl.multiple_of(owner * OWN * GROUP, OWN * GROUP)
+            blocks[x, pl.ds(first, OWN * GROUP), :] = array[:, x].reshape(OWN * GROUP, HD)
+        blocks[x, BLOCK:, :] = tags[...]
+    copies = [
+        pltpu.make_async_copy(blocks, out.at[pl.ds(line * XN, XN)], done.at[line]) for line in range(LINE)
+    ]
     for copy in copies:
         copy.start()
     for copy in copies:
@@ -170,12 +173,12 @@
         return [(start, min(CHUNK, end - start)) for start in range(0, end, CHUNK)]
 
     def score(part, side, pages):
-        here = pl.ds(part * STEP_LINES, STEP_LINES)
-        rows = q[here, :LINE_ROWS, :].reshape(ROWS, HD)
-        tags = q[here, LINE_ROWS:, :].astype(jnp.float32)
-        query_at = tags[:, :NEWT, :] * 32.0 + tags[:, NEWT:, :]
+        here = pl.ds(part * STEP_BLOCKS, STEP_BLOCKS)
+        rows = q[here, :BLOCK, :].reshape(ROWS, HD)
+        tags = q[here, BLOCK:, :].astype(jnp.float32)
+        query_at = tags[:, :TOKENS, :] * 32.0 + tags[:, TOKENS:, :]
         hidden = jnp.where(key_at <= query_at, 0.0, LOWEST)
-        bias = jnp.broadcast_to(hidden[:, :, None, :], (STEP_LINES, NEWT, GROUP, HD)).reshape(ROWS, HD)
+        bias = jnp.broadcast_to(hidden[:, :, None, :], (STEP_BLOCKS, TOKENS, GROUP, HD)).reshape(ROWS, HD)
         top = None
         for start, size in chunks(pages):
             product = lax.dot_general(
@@ -271,28 +274,28 @@
     half = bf16(OWN, XN, GROUP, HD)
     sources = [
         new_positions,
-        queries.reshape(OWN, KN, GROUP, HD),
+        queries.reshape(OWN, XN, CN, GROUP, HD),
         hist_keys.reshape(HISTORY, HD),
         hist_values.reshape(HISTORY, HD),
         new_keys.reshape(NEWT, HD),
         new_values.reshape(NEWT, HD),
     ]
-    kv, q_sent, tags = call(
+    kv, q_kept, q_sent, tags = call(
         pack_kernel,
-        (bf16(2, KV_ROWS, HD), bf16(KN, OWN, GROUP, HD), bf16(2 * NEWT, HD)),
+        (bf16(2, KV_ROWS, HD), half, half, bf16(8, HD)),
         in_specs=[HBM] * 6,
         scratch_shapes=[pltpu.SMEM((NEWT,), jnp.int32), pltpu.SemaphoreType.DMA((7,))],
     )(*(pltpu.with_memory_space_constraint(source, pltpu.HBM) for source in sources))
     lower = lax.ppermute(kv, ALL, along(3))
     upper = lax.ppermute(kv, ALL, along(-2))
-    q = lax.all_to_all(q_sent, ("x", "c"), split_axis=0, concat_axis=0, tiled=True)
+    q_received = lax.ppermute(q_sent, ALL, SWAP)
     q = call(
         spread_kernel,
-        bf16(LINE, LINE_WIRE, HD),
+        bf16(BLOCKS, WIRE, HD),
         out_specs=HBM,
-        scratch_shapes=[pltpu.SemaphoreType.DMA((2 * LINE,))],
-    )(q.reshape(LINE_ROWS, HD), tags)
-    q = lax.all_to_all(q, ALL, split_axis=0, concat_axis=0, axis_index_groups=CROSS_LINES, tiled=True)
+        scratch_shapes=[pltpu.VMEM((XN, WIRE, HD), jnp.bfloat16), pltpu.SemaphoreType.DMA((LINE,))],
+    )(q_kept, q_received, tags)
+    q = lax.all_to_all(q, ALL, split_axis=0, concat_axis=0, axis_index_groups=CROSS, tiled=True)
     three, two = call(join_kernel, (bf16(3, 2, KV_ROWS, HD), bf16(2, 2, KV_ROWS, HD)), flops=JOIN)(kv, lower, upper)
     above = lax.ppermute(three, ALL, along(-1))
     below = lax.ppermute(two, ALL, along(1))

time: 83.1 us -> 80.9 us (0.974)
  blocking collectives: 33.7 us -> 22.1 us
  starting transfers between devices: 26.7 us -> 36.4 us
    all_to_all x1 -> x0, blocking collectives: 14.1 us -> none  [body(): lax.all_to_all(q_sent, ('x', 'c'), split_axis=0, concat_axis=0, tiled=True)]
    ppermute x0 -> x1, starting transfers between devices: none -> 7.04 us  [body(): q_received = lax.ppermute(q_sent, ALL, SWAP)]
    all_to_all x1, starting transfers between devices: 6.03 us -> 8.88 us  [body(): lax.all_to_all(q, ALL, split_axis=0, concat_axis=0, axis_index_groups=CRO...]
    all_to_all x1, blocking collectives: 19.7 us -> 22.1 us  [body(): lax.all_to_all(parts, ALL, split_axis=0, concat_axis=0, axis_index_groups...]
    ppermute x0 -> x1, waiting for transfers between devices: none -> 0.84 us  [body(): q_received = lax.ppermute(q_sent, ALL, SWAP)]
  transfers between devices with their start and end apart: 6 -> 7, of which waited for: 3 -> 4; matrix products, arithmetic and copies ran while one was open for 0% -> 0% of each run, Pallas kernels for 2% -> 2%
where the time goes in v7:
time: 80.9 us; the launch traced here: 80.5 us
  starting transfers between devices  36.4 us (45%)
  blocking collectives  22.1 us (27%)
  waiting for transfers between devices  11.6 us (14%)
  Pallas kernels  10.3 us (13%)
    all_to_all x1, blocking collectives, body(): lax.all_to_all(parts, ALL, split_axis=0, concat_axis=0, axis_index_groups...  22.1 us
    ppermute x1, waiting for transfers between devices, body(): below = lax.ppermute(two, ALL, along(1))  9.68 us
    all_to_all x1, starting transfers between devices, body(): lax.all_to_all(q, ALL, split_axis=0, concat_axis=0, axis_index_groups=CRO...  8.88 us
    ppermute x1, starting transfers between devices, body(): q_received = lax.ppermute(q_sent, ALL, SWAP)  7.04 us
    pallas_call x1, Pallas kernels, attend(): call(attend_kernel, bf16(BLOCKS, WIRE, HD), megabytes=20, flops=230000000...  6.87 us
    ppermute x1, starting transfers between devices, body(): lower = lax.ppermute(kv, ALL, along(3))  6.06 us
    ppermute x1, starting transfers between devices, body(): above = lax.ppermute(three, ALL, along(-1))  5.1 us
    ppermute x1, starting transfers between devices, body(): received = lax.ppermute(combined(1), ALL, SWAP)  4.2 us
  transfers between devices with their start and end apart: 7, of which 4 were waited for; matrix products, arithmetic and copies ran while one was open for 0% of the time, Pallas kernels for 2%

profile of v7, /device:TPU:1, one launch (start us, length us, event | category | flops | bytes accessed | tf_op | source)
XLA Modules:
  0.0 80.5 jit_solution(3140852682047950078)
XLA Ops:
  0.0 1.0 %shard_map.73 = (bf16[2,416,128]{2,1,0:T(8,128)(2,1)S(1)}, bf16[2,4,16,128]{3,2,1,0:T(8,128)(2,1)S(1)}, bf16[2,4,16,128]{3,2,1,0:T(8,128)(2,1)S(1)}, bf16[8,128]{1,0:T(8,128)(2,1)S(1)}) custom-call(s32[16]{0:T(128)} %positions.1, bf16[2,4,2,16,128]{4,3,2,1,0:T(8,128)(2,1)} %bitcast.7, bf16[384,128]{1,0:T(8,128)(2,1)} %bitcast.5, bf16[384,128]{1,0:T(8,128)(2,1)} %bitcast.6, ...), custom_call_target="tpu_custom_call" | custom-call | flops 1000000 | bytes 800000 | tf_op jit(solution)/shard_map/pallas_call | solution.py:283
  1.0 6.1 %collective-permute-start = (bf16[2,416,128]{2,1,0:T(8,128)(2,1)S(1)}, bf16[2,416,128]{2,1,0:T(8,128)(2,1)S(1)}, u32[]{:S(2)}, u32[]{:S(2)}) collective-permute-start(bf16[2,416,128]{2,1,0:T(8,128)(2,1)S(1)} %get-tuple-element.11.own), channel_id=1, source_target_pairs={{0,192},{1,25},{2,194},{3,27},{4,196},{5,29},{6,198},{7,31},{8,200... | collective-permute-start | bytes 638984 | tf_op jit(solution)/shard_map/ppermute | solution.py:289
  7.1 3.2 %collective-permute-start.1 = (bf16[2,416,128]{2,1,0:T(8,128)(2,1)S(1)}, bf16[2,416,128]{2,1,0:T(8,128)(2,1)S(1)}, u32[]{:S(2)}, u32[]{:S(2)}) collective-permute-start(bf16[2,416,128]{2,1,0:T(8,128)(2,1)S(1)} %get-tuple-element.11.own), channel_id=1, source_target_pairs={{0,384},{1,49},{2,386},{3,51},{4,388},{5,53},{6,390},{7,55},{8,392... | collective-permute-start | bytes 638984 | tf_op jit(solution)/shard_map/ppermute | solution.py:290
  10.3 7.0 %collective-permute-start.4 = (bf16[2,4,16,128]{3,2,1,0:T(8,128)(2,1)S(1)}, bf16[2,4,16,128]{3,2,1,0:T(8,128)(2,1)S(1)}, u32[]{:S(2)}, u32[]{:S(2)}) collective-permute-start(bf16[2,4,16,128]{3,2,1,0:T(8,128)(2,1)S(1)} %get-tuple-element.15), channel_id=1, source_target_pairs={{0,1},{1,0},{2,3},{3,2},{4,5},{5,4},{6,7},{7,6},{8,9},{9,8},{10,11... | collective-permute-start | bytes 98312 | tf_op jit(solution)/shard_map/ppermute | solution.py:291
  17.3 0.8 %collective-permute-done.4.received = bf16[2,4,16,128]{3,2,1,0:T(8,128)(2,1)S(1)} collective-permute-done((bf16[2,4,16,128]{3,2,1,0:T(8,128)(2,1)S(1)}, bf16[2,4,16,128]{3,2,1,0:T(8,128)(2,1)S(1)}, u32[]{:S(2)}, u32[]{:S(2)}) %collective-permute-start.4) | collective-permute-done | bytes 32800 | tf_op jit(solution)/shard_map/ppermute | solution.py:291
  18.1 0.9 %shard_map.75 = bf16[32,72,128]{2,1,0:T(8,128)(2,1)} custom-call(bf16[2,4,16,128]{3,2,1,0:T(8,128)(2,1)S(1)} %get-tuple-element.14.kept, bf16[2,4,16,128]{3,2,1,0:T(8,128)(2,1)S(1)} %collective-permute-done.4.received, bf16[8,128]{1,0:T(8,128)(2,1)S(1)} %get-tuple-element.16.tags), custom_call_target="tpu_custom_call" | custom-call | flops 1000000 | bytes 800000 | tf_op jit(solution)/shard_map/pallas_call | solution.py:292
  19.0 8.9 %all-to-all-start = ((bf16[32,72,128]{2,1,0:T(8,128)(2,1)}), bf16[32,72,128]{2,1,0:T(8,128)(2,1)S(1)}, u32[]{:S(2)}, u32[]{:S(2)}) async-start(bf16[32,72,128]{2,1,0:T(8,128)(2,1)} %shard_map.75), calls=%async_computation | async-start | bytes 1179648 | tf_op jit(solution)/shard_map/all_to_all | solution.py:298
  27.9 0.0 collective-permute-done.lower
  27.9 0.0 collective-permute-done.1.upper
  28.0 0.1 shard_map.74
  28.1 0.0 copy-start
  28.1 5.1 %collective-permute-start.2 = (bf16[3,2,416,128]{3,2,1,0:T(8,128)(2,1)S(1)}, bf16[3,2,416,128]{3,2,1,0:T(8,128)(2,1)S(1)}, u32[]{:S(2)}, u32[]{:S(2)}) collective-permute-start(bf16[3,2,416,128]{3,2,1,0:T(8,128)(2,1)S(1)} %get-tuple-element.12), channel_id=1, source_target_pairs={{0,448},{1,57},{2,450},{3,59},{4,452},{5,61},{6,454},{7,63},{8,456... | collective-permute-start | bytes 1916936 | tf_op jit(solution)/shard_map/ppermute | solution.py:300
  33.2 1.9 %collective-permute-start.3 = (bf16[2,2,416,128]{3,2,1,0:T(8,128)(2,1)S(1)}, bf16[2,2,416,128]{3,2,1,0:T(8,128)(2,1)S(1)}, u32[]{:S(2)}, u32[]{:S(2)}) collective-permute-start(bf16[2,2,416,128]{3,2,1,0:T(8,128)(2,1)S(1)} %get-tuple-element.13), channel_id=1, source_target_pairs={{0,64},{1,9},{2,66},{3,11},{4,68},{5,13},{6,70},{7,15},{8,72},{9,1... | collective-permute-start | bytes 1277960 | tf_op jit(solution)/shard_map/ppermute | solution.py:301
  35.1 9.7 %collective-permute-done.3.below = bf16[2,2,416,128]{3,2,1,0:T(8,128)(2,1)S(1)} collective-permute-done((bf16[2,2,416,128]{3,2,1,0:T(8,128)(2,1)S(1)}, bf16[2,2,416,128]{3,2,1,0:T(8,128)(2,1)S(1)}, u32[]{:S(2)}, u32[]{:S(2)}) %collective-permute-start.3) | collective-permute-done | bytes 426016 | tf_op jit(solution)/shard_map/ppermute | solution.py:301
  44.8 0.6 collective-permute-done.2.above
  45.5 0.0 all-to-all-done.q
  45.5 0.0 copy-done
  45.5 6.9 %shard_map.76 = bf16[32,72,128]{2,1,0:T(8,128)(2,1)S(1)} custom-call(s32[128]{0:T(128)S(1)} %copy-done, bf16[2,416,128]{2,1,0:T(8,128)(2,1)S(1)} %get-tuple-element.11.own, bf16[2,416,128]{2,1,0:T(8,128)(2,1)S(1)} %collective-permute-done.lower, bf16[2,416,128]{2,1,0:T(8,128)(2,1)S(1)} %collective-permute-done.1.upper, ...), custom_call_target="tpu_custom_call" | custom-call | flops 2300000000 | bytes 5000000 | tf_op jit(solution)/shard_map/pallas_call | solution.py:228
  52.4 22.1 %all_to_all.10.parts = bf16[32,72,128]{2,1,0:T(8,128)(2,1)S(1)} all-to-all(bf16[32,72,128]{2,1,0:T(8,128)(2,1)S(1)} %shard_map.76), channel_id=1, replica_groups={{0,2,4,6,8,10,12,14,16,18,20,22,24,26,28,30,32,34,36,38,40,42,44,46,48,..., dimensions={0} | all-to-all | bytes 1179648 | tf_op jit(solution)/shard_map/all_to_all | solution.py:303
  74.4 0.4 shard_map.78
  74.8 4.2 %collective-permute-start.5 = (bf16[2,4,16,128]{3,2,1,0:T(8,128)(2,1)S(1)}, bf16[2,4,16,128]{3,2,1,0:T(8,128)(2,1)S(1)}, u32[]{:S(2)}, u32[]{:S(2)}) collective-permute-start(bf16[2,4,16,128]{3,2,1,0:T(8,128)(2,1)S(1)} %shard_map.78), channel_id=1, source_target_pairs={{0,1},{1,0},{2,3},{3,2},{4,5},{5,4},{6,7},{7,6},{8,9},{9,8},{10,11... | collective-permute-start | bytes 98312 | tf_op jit(solution)/shard_map/ppermute | solution.py:312
  79.0 0.4 shard_map.77.kept
  79.4 0.4 collective-permute-done.5.received
  79.9 0.6 shard_map.79
Async XLA Ops:
  1.0 26.9 %collective-permute-start = (bf16[2,416,128]{2,1,0:T(8,128)(2,1)S(1)}, bf16[2,416,128]{2,1,0:T(8,128)(2,1)S(1)}, u32[]{:S(2)}, u32[]{:S(2)}) collective-permute-start(bf16[2,416,128]{2,1,0:T(8,128)(2,1)S(1)} %get-tuple-element.11.own), channel_id=1, source_target_pairs={{0,192},{1,25},{2,194},{3,27},{4,196},{5,29},{6,198},{7,31},{8,200... | collective-permute-start | bytes 638984 | tf_op jit(solution)/shard_map/ppermute | solution.py:289
  7.1 20.9 %collective-permute-start.1 = (bf16[2,416,128]{2,1,0:T(8,128)(2,1)S(1)}, bf16[2,416,128]{2,1,0:T(8,128)(2,1)S(1)}, u32[]{:S(2)}, u32[]{:S(2)}) collective-permute-start(bf16[2,416,128]{2,1,0:T(8,128)(2,1)S(1)} %get-tuple-element.11.own), channel_id=1, source_target_pairs={{0,384},{1,49},{2,386},{3,51},{4,388},{5,53},{6,390},{7,55},{8,392... | collective-permute-start | bytes 638984 | tf_op jit(solution)/shard_map/ppermute | solution.py:290
  10.3 7.9 %collective-permute-start.4 = (bf16[2,4,16,128]{3,2,1,0:T(8,128)(2,1)S(1)}, bf16[2,4,16,128]{3,2,1,0:T(8,128)(2,1)S(1)}, u32[]{:S(2)}, u32[]{:S(2)}) collective-permute-start(bf16[2,4,16,128]{3,2,1,0:T(8,128)(2,1)S(1)} %get-tuple-element.15), channel_id=1, source_target_pairs={{0,1},{1,0},{2,3},{3,2},{4,5},{5,4},{6,7},{7,6},{8,9},{9,8},{10,11... | collective-permute-start | bytes 98312 | tf_op jit(solution)/shard_map/ppermute | solution.py:291
  19.0 26.4 %all-to-all-start = ((bf16[32,72,128]{2,1,0:T(8,128)(2,1)}), bf16[32,72,128]{2,1,0:T(8,128)(2,1)S(1)}, u32[]{:S(2)}, u32[]{:S(2)}) async-start(bf16[32,72,128]{2,1,0:T(8,128)(2,1)} %shard_map.75), calls=%async_computation | async-start | bytes 1179648 | tf_op jit(solution)/shard_map/all_to_all | solution.py:298
  28.1 17.4 %copy-start = (s32[128]{0:T(128)S(1)}, s32[128]{0:T(128)}, u32[]{:S(2)}) copy-start(s32[128]{0:T(128)} %page_slots.1) | copy-start | bytes 1540
  28.1 17.4 %collective-permute-start.2 = (bf16[3,2,416,128]{3,2,1,0:T(8,128)(2,1)S(1)}, bf16[3,2,416,128]{3,2,1,0:T(8,128)(2,1)S(1)}, u32[]{:S(2)}, u32[]{:S(2)}) collective-permute-start(bf16[3,2,416,128]{3,2,1,0:T(8,128)(2,1)S(1)} %get-tuple-element.12), channel_id=1, source_target_pairs={{0,448},{1,57},{2,450},{3,59},{4,452},{5,61},{6,454},{7,63},{8,456... | collective-permute-start | bytes 1916936 | tf_op jit(solution)/shard_map/ppermute | solution.py:300
  33.2 11.6 %collective-permute-start.3 = (bf16[2,2,416,128]{3,2,1,0:T(8,128)(2,1)S(1)}, bf16[2,2,416,128]{3,2,1,0:T(8,128)(2,1)S(1)}, u32[]{:S(2)}, u32[]{:S(2)}) collective-permute-start(bf16[2,2,416,128]{3,2,1,0:T(8,128)(2,1)S(1)} %get-tuple-element.13), channel_id=1, source_target_pairs={{0,64},{1,9},{2,66},{3,11},{4,68},{5,13},{6,70},{7,15},{8,72},{9,1... | collective-permute-start | bytes 1277960 | tf_op jit(solution)/shard_map/ppermute | solution.py:301
  74.8 5.0 %collective-permute-start.5 = (bf16[2,4,16,128]{3,2,1,0:T(8,128)(2,1)S(1)}, bf16[2,4,16,128]{3,2,1,0:T(8,128)(2,1)S(1)}, u32[]{:S(2)}, u32[]{:S(2)}) collective-permute-start(bf16[2,4,16,128]{3,2,1,0:T(8,128)(2,1)S(1)} %shard_map.78), channel_id=1, source_target_pairs={{0,1},{1,0},{2,3},{3,2},{4,5},{5,4},{6,7},{7,6},{8,9},{9,8},{10,11... | collective-permute-start | bytes 98312 | tf_op jit(solution)/shard_map/ppermute | solution.py:312

commit v8 on v7

--- a/solution.py
+++ b/solution.py
@@ -286,9 +286,10 @@
         in_specs=[HBM] * 6,
         scratch_shapes=[pltpu.SMEM((NEWT,), jnp.int32), pltpu.SemaphoreType.DMA((7,))],
     )(*(pltpu.with_memory_space_constraint(source, pltpu.HBM) for source in sources))
+    q_received = lax.ppermute(q_sent, ALL, SWAP)
+    kv, q_received = lax.optimization_barrier((kv, q_received))
     lower = lax.ppermute(kv, ALL, along(3))
     upper = lax.ppermute(kv, ALL, along(-2))
-    q_received = lax.ppermute(q_sent, ALL, SWAP)
     q = call(
         spread_kernel,
         bf16(BLOCKS, WIRE, HD),

time: 80.9 us -> 79.7 us (0.985)
  starting transfers between devices: 36.4 us -> 31.9 us
  waiting for transfers between devices: 11.6 us -> 13.8 us
  blocking collectives: 22.1 us -> 23.1 us
    ppermute x1, starting transfers between devices: 6.06 us -> 1.91 us  [body(): lower = lax.ppermute(kv, ALL, along(3))]
    all_to_all x1, starting transfers between devices: 8.88 us -> 12.1 us  [body(): lax.all_to_all(q, ALL, split_axis=0, concat_axis=0, axis_index_groups=CRO...]
    ppermute x1, starting transfers between devices: 5.1 us -> 2.38 us  [body(): above = lax.ppermute(three, ALL, along(-1))]
    ppermute x1, starting transfers between devices: 4.2 us -> 1.92 us  [body(): received = lax.ppermute(combined(1), ALL, SWAP)]
    ppermute x1, waiting for transfers between devices: 9.68 us -> 11.6 us  [body(): below = lax.ppermute(two, ALL, along(1))]
    ppermute x1, starting transfers between devices: 7.04 us -> 8.79 us  [body(): q_received = lax.ppermute(q_sent, ALL, SWAP)]
    ppermute x1, starting transfers between devices: 3.17 us -> 1.92 us  [body(): upper = lax.ppermute(kv, ALL, along(-2))]
    ppermute x1, starting transfers between devices: 1.92 us -> 2.92 us  [body(): below = lax.ppermute(two, ALL, along(1))]
where the time goes in v8:
time: 79.7 us; the launch traced here: 79.3 us
  starting transfers between devices  31.9 us (40%)
  blocking collectives  23.1 us (29%)
  waiting for transfers between devices  13.8 us (17%)
  Pallas kernels  10.4 us (13%)
    all_to_all x1, blocking collectives, body(): lax.all_to_all(parts, ALL, split_axis=0, concat_axis=0, axis_index_groups...  23.1 us
    all_to_all x1, starting transfers between devices, body(): lax.all_to_all(q, ALL, split_axis=0, concat_axis=0, axis_index_groups=CRO...  12.1 us
    ppermute x1, waiting for transfers between devices, body(): below = lax.ppermute(two, ALL, along(1))  11.6 us
    ppermute x1, starting transfers between devices, body(): q_received = lax.ppermute(q_sent, ALL, SWAP)  8.79 us
    pallas_call x1, Pallas kernels, attend(): call(attend_kernel, bf16(BLOCKS, WIRE, HD), megabytes=20, flops=230000000...  6.92 us
    ppermute x1, starting transfers between devices, body(): below = lax.ppermute(two, ALL, along(1))  2.92 us
    ppermute x1, starting transfers between devices, body(): above = lax.ppermute(three, ALL, along(-1))  2.38 us
    ppermute x1, starting transfers between devices, body(): upper = lax.ppermute(kv, ALL, along(-2))  1.92 us
  transfers between devices with their start and end apart: 7, of which 4 were waited for; matrix products, arithmetic and copies ran while one was open for 0% of the time, Pallas kernels for 2%

profile of v8, /device:TPU:1, one launch (start us, length us, event | category | flops | bytes accessed | tf_op | source)
XLA Modules:
  0.0 79.3 jit_solution(12646712035871590563)
XLA Ops:
  0.0 1.0 %shard_map.73 = (bf16[2,416,128]{2,1,0:T(8,128)(2,1)S(1)}, bf16[2,4,16,128]{3,2,1,0:T(8,128)(2,1)S(1)}, bf16[2,4,16,128]{3,2,1,0:T(8,128)(2,1)S(1)}, bf16[8,128]{1,0:T(8,128)(2,1)S(1)}) custom-call(s32[16]{0:T(128)} %positions.1, bf16[2,4,2,16,128]{4,3,2,1,0:T(8,128)(2,1)} %bitcast.7, bf16[384,128]{1,0:T(8,128)(2,1)} %bitcast.5, bf16[384,128]{1,0:T(8,128)(2,1)} %bitcast.6, ...), custom_call_target="tpu_custom_call" | custom-call | flops 1000000 | bytes 800000 | tf_op jit(solution)/shard_map/pallas_call | solution.py:283
  1.0 8.8 %collective-permute-start = (bf16[2,4,16,128]{3,2,1,0:T(8,128)(2,1)S(1)}, bf16[2,4,16,128]{3,2,1,0:T(8,128)(2,1)S(1)}, u32[]{:S(2)}, u32[]{:S(2)}) collective-permute-start(bf16[2,4,16,128]{3,2,1,0:T(8,128)(2,1)S(1)} %get-tuple-element.14), channel_id=1, source_target_pairs={{0,1},{1,0},{2,3},{3,2},{4,5},{5,4},{6,7},{7,6},{8,9},{9,8},{10,11... | collective-permute-start | bytes 98312 | tf_op jit(solution)/shard_map/ppermute | solution.py:289
  9.8 0.8 %collective-permute-done.received = bf16[2,4,16,128]{3,2,1,0:T(8,128)(2,1)S(1)} collective-permute-done((bf16[2,4,16,128]{3,2,1,0:T(8,128)(2,1)S(1)}, bf16[2,4,16,128]{3,2,1,0:T(8,128)(2,1)S(1)}, u32[]{:S(2)}, u32[]{:S(2)}) %collective-permute-start) | collective-permute-done | bytes 32800 | tf_op jit(solution)/shard_map/ppermute | solution.py:289
  10.6 1.9 %collective-permute-start.1 = (bf16[2,416,128]{2,1,0:T(8,128)(2,1)S(1)}, bf16[2,416,128]{2,1,0:T(8,128)(2,1)S(1)}, u32[]{:S(2)}, u32[]{:S(2)}) collective-permute-start(bf16[2,416,128]{2,1,0:T(8,128)(2,1)S(1)} %get-tuple-element.15.own), channel_id=1, source_target_pairs={{0,192},{1,25},{2,194},{3,27},{4,196},{5,29},{6,198},{7,31},{8,200... | collective-permute-start | bytes 638984 | tf_op jit(solution)/shard_map/ppermute | solution.py:291
  12.6 1.9 %collective-permute-start.2 = (bf16[2,416,128]{2,1,0:T(8,128)(2,1)S(1)}, bf16[2,416,128]{2,1,0:T(8,128)(2,1)S(1)}, u32[]{:S(2)}, u32[]{:S(2)}) collective-permute-start(bf16[2,416,128]{2,1,0:T(8,128)(2,1)S(1)} %get-tuple-element.15.own), channel_id=1, source_target_pairs={{0,384},{1,49},{2,386},{3,51},{4,388},{5,53},{6,390},{7,55},{8,392... | collective-permute-start | bytes 638984 | tf_op jit(solution)/shard_map/ppermute | solution.py:292
  14.5 0.9 %shard_map.75 = bf16[32,72,128]{2,1,0:T(8,128)(2,1)} custom-call(bf16[2,4,16,128]{3,2,1,0:T(8,128)(2,1)S(1)} %get-tuple-element.18.kept, bf16[2,4,16,128]{3,2,1,0:T(8,128)(2,1)S(1)} %collective-permute-done.received, bf16[8,128]{1,0:T(8,128)(2,1)S(1)} %get-tuple-element.20.tags), custom_call_target="tpu_custom_call" | custom-call | flops 1000000 | bytes 800000 | tf_op jit(solution)/shard_map/pallas_call | solution.py:293
  15.4 12.1 %all-to-all-start = ((bf16[32,72,128]{2,1,0:T(8,128)(2,1)}), bf16[32,72,128]{2,1,0:T(8,128)(2,1)S(1)}, u32[]{:S(2)}, u32[]{:S(2)}) async-start(bf16[32,72,128]{2,1,0:T(8,128)(2,1)} %shard_map.75), calls=%async_computation | async-start | bytes 1179648 | tf_op jit(solution)/shard_map/all_to_all | solution.py:299
  27.5 0.0 collective-permute-done.1.lower
  27.5 0.0 collective-permute-done.2.upper
  27.5 0.1 shard_map.74
  27.7 0.0 copy-start
  27.7 2.4 %collective-permute-start.3 = (bf16[3,2,416,128]{3,2,1,0:T(8,128)(2,1)S(1)}, bf16[3,2,416,128]{3,2,1,0:T(8,128)(2,1)S(1)}, u32[]{:S(2)}, u32[]{:S(2)}) collective-permute-start(bf16[3,2,416,128]{3,2,1,0:T(8,128)(2,1)S(1)} %get-tuple-element.16), channel_id=1, source_target_pairs={{0,448},{1,57},{2,450},{3,59},{4,452},{5,61},{6,454},{7,63},{8,456... | collective-permute-start | bytes 1916936 | tf_op jit(solution)/shard_map/ppermute | solution.py:301
  30.0 2.9 %collective-permute-start.4 = (bf16[2,2,416,128]{3,2,1,0:T(8,128)(2,1)S(1)}, bf16[2,2,416,128]{3,2,1,0:T(8,128)(2,1)S(1)}, u32[]{:S(2)}, u32[]{:S(2)}) collective-permute-start(bf16[2,2,416,128]{3,2,1,0:T(8,128)(2,1)S(1)} %get-tuple-element.17), channel_id=1, source_target_pairs={{0,64},{1,9},{2,66},{3,11},{4,68},{5,13},{6,70},{7,15},{8,72},{9,1... | collective-permute-start | bytes 1277960 | tf_op jit(solution)/shard_map/ppermute | solution.py:302
  33.0 11.6 %collective-permute-done.4.below = bf16[2,2,416,128]{3,2,1,0:T(8,128)(2,1)S(1)} collective-permute-done((bf16[2,2,416,128]{3,2,1,0:T(8,128)(2,1)S(1)}, bf16[2,2,416,128]{3,2,1,0:T(8,128)(2,1)S(1)}, u32[]{:S(2)}, u32[]{:S(2)}) %collective-permute-start.4) | collective-permute-done | bytes 426016 | tf_op jit(solution)/shard_map/ppermute | solution.py:302
  44.6 0.6 collective-permute-done.3.above
  45.2 0.0 all-to-all-done.q
  45.2 0.0 copy-done
  45.2 6.9 %shard_map.76 = bf16[32,72,128]{2,1,0:T(8,128)(2,1)S(1)} custom-call(s32[128]{0:T(128)S(1)} %copy-done, bf16[2,416,128]{2,1,0:T(8,128)(2,1)S(1)} %get-tuple-element.15.own, bf16[2,416,128]{2,1,0:T(8,128)(2,1)S(1)} %collective-permute-done.1.lower, bf16[2,416,128]{2,1,0:T(8,128)(2,1)S(1)} %collective-permute-done.2.upper, ...), custom_call_target="tpu_custom_call" | custom-call | flops 2300000000 | bytes 5000000 | tf_op jit(solution)/shard_map/pallas_call | solution.py:228
  52.1 23.1 %all_to_all.10.parts = bf16[32,72,128]{2,1,0:T(8,128)(2,1)S(1)} all-to-all(bf16[32,72,128]{2,1,0:T(8,128)(2,1)S(1)} %shard_map.76), channel_id=1, replica_groups={{0,2,4,6,8,10,12,14,16,18,20,22,24,26,28,30,32,34,36,38,40,42,44,46,48,..., dimensions={0} | all-to-all | bytes 1179648 | tf_op jit(solution)/shard_map/all_to_all | solution.py:304
  75.1 0.4 shard_map.78
  75.5 1.9 %collective-permute-start.5 = (bf16[2,4,16,128]{3,2,1,0:T(8,128)(2,1)S(1)}, bf16[2,4,16,128]{3,2,1,0:T(8,128)(2,1)S(1)}, u32[]{:S(2)}, u32[]{:S(2)}) collective-permute-start(bf16[2,4,16,128]{3,2,1,0:T(8,128)(2,1)S(1)} %shard_map.78), channel_id=1, source_target_pairs={{0,1},{1,0},{2,3},{3,2},{4,5},{5,4},{6,7},{7,6},{8,9},{9,8},{10,11... | collective-permute-start | bytes 98312 | tf_op jit(solution)/shard_map/ppermute | solution.py:313
  77.5 0.4 shard_map.77.kept
  77.9 0.8 collective-permute-done.5.received
  78.6 0.6 shard_map.79
Async XLA Ops:
  1.0 9.6 %collective-permute-start = (bf16[2,4,16,128]{3,2,1,0:T(8,128)(2,1)S(1)}, bf16[2,4,16,128]{3,2,1,0:T(8,128)(2,1)S(1)}, u32[]{:S(2)}, u32[]{:S(2)}) collective-permute-start(bf16[2,4,16,128]{3,2,1,0:T(8,128)(2,1)S(1)} %get-tuple-element.14), channel_id=1, source_target_pairs={{0,1},{1,0},{2,3},{3,2},{4,5},{5,4},{6,7},{7,6},{8,9},{9,8},{10,11... | collective-permute-start | bytes 98312 | tf_op jit(solution)/shard_map/ppermute | solution.py:289
  10.6 16.9 %collective-permute-start.1 = (bf16[2,416,128]{2,1,0:T(8,128)(2,1)S(1)}, bf16[2,416,128]{2,1,0:T(8,128)(2,1)S(1)}, u32[]{:S(2)}, u32[]{:S(2)}) collective-permute-start(bf16[2,416,128]{2,1,0:T(8,128)(2,1)S(1)} %get-tuple-element.15.own), channel_id=1, source_target_pairs={{0,192},{1,25},{2,194},{3,27},{4,196},{5,29},{6,198},{7,31},{8,200... | collective-permute-start | bytes 638984 | tf_op jit(solution)/shard_map/ppermute | solution.py:291
  12.6 14.9 %collective-permute-start.2 = (bf16[2,416,128]{2,1,0:T(8,128)(2,1)S(1)}, bf16[2,416,128]{2,1,0:T(8,128)(2,1)S(1)}, u32[]{:S(2)}, u32[]{:S(2)}) collective-permute-start(bf16[2,416,128]{2,1,0:T(8,128)(2,1)S(1)} %get-tuple-element.15.own), channel_id=1, source_target_pairs={{0,384},{1,49},{2,386},{3,51},{4,388},{5,53},{6,390},{7,55},{8,392... | collective-permute-start | bytes 638984 | tf_op jit(solution)/shard_map/ppermute | solution.py:292
  15.4 29.8 %all-to-all-start = ((bf16[32,72,128]{2,1,0:T(8,128)(2,1)}), bf16[32,72,128]{2,1,0:T(8,128)(2,1)S(1)}, u32[]{:S(2)}, u32[]{:S(2)}) async-start(bf16[32,72,128]{2,1,0:T(8,128)(2,1)} %shard_map.75), calls=%async_computation | async-start | bytes 1179648 | tf_op jit(solution)/shard_map/all_to_all | solution.py:299
  27.7 17.5 %copy-start = (s32[128]{0:T(128)S(1)}, s32[128]{0:T(128)}, u32[]{:S(2)}) copy-start(s32[128]{0:T(128)} %page_slots.1) | copy-start | bytes 1540
  27.7 17.5 %collective-permute-start.3 = (bf16[3,2,416,128]{3,2,1,0:T(8,128)(2,1)S(1)}, bf16[3,2,416,128]{3,2,1,0:T(8,128)(2,1)S(1)}, u32[]{:S(2)}, u32[]{:S(2)}) collective-permute-start(bf16[3,2,416,128]{3,2,1,0:T(8,128)(2,1)S(1)} %get-tuple-element.16), channel_id=1, source_target_pairs={{0,448},{1,57},{2,450},{3,59},{4,452},{5,61},{6,454},{7,63},{8,456... | collective-permute-start | bytes 1916936 | tf_op jit(solution)/shard_map/ppermute | solution.py:301
  30.0 14.5 %collective-permute-start.4 = (bf16[2,2,416,128]{3,2,1,0:T(8,128)(2,1)S(1)}, bf16[2,2,416,128]{3,2,1,0:T(8,128)(2,1)S(1)}, u32[]{:S(2)}, u32[]{:S(2)}) collective-permute-start(bf16[2,2,416,128]{3,2,1,0:T(8,128)(2,1)S(1)} %get-tuple-element.17), channel_id=1, source_target_pairs={{0,64},{1,9},{2,66},{3,11},{4,68},{5,13},{6,70},{7,15},{8,72},{9,1... | collective-permute-start | bytes 1277960 | tf_op jit(solution)/shard_map/ppermute | solution.py:302
  75.5 3.1 %collective-permute-start.5 = (bf16[2,4,16,128]{3,2,1,0:T(8,128)(2,1)S(1)}, bf16[2,4,16,128]{3,2,1,0:T(8,128)(2,1)S(1)}, u32[]{:S(2)}, u32[]{:S(2)}) collective-permute-start(bf16[2,4,16,128]{3,2,1,0:T(8,128)(2,1)S(1)} %shard_map.78), channel_id=1, source_target_pairs={{0,1},{1,0},{2,3},{3,2},{4,5},{5,4},{6,7},{7,6},{8,9},{9,8},{10,11... | collective-permute-start | bytes 98312 | tf_op jit(solution)/shard_map/ppermute | solution.py:313

commit v9 on v8

--- a/solution.py
+++ b/solution.py
@@ -123,11 +123,11 @@
         copy.wait()
 
 
-def join_kernel(own, lower, upper, three, two):
-    for i, block in enumerate((own, lower, upper)):
-        three[i] = block[...]
-        if i < 2:
-            two[i] = block[...]
+def join_kernel(own, lower, upper, down, up):
+    for i, half in enumerate((own.at[0], lower.at[0], lower.at[1], upper.at[0], upper.at[1])):
+        down[i] = half[...]
+    for i, half in enumerate((own.at[0], own.at[1], lower.at[0], lower.at[1], upper.at[1])):
+        up[i] = half[...]
 
 
 def attend_kernel(page_slots, own, lower, upper, above, below, q, out, keys, values, scores):
@@ -135,27 +135,29 @@
     ctx = lax.axis_index("z") * YN + lax.axis_index("y")
     stride = jnp.where(core == 0, YN, 1)
     values[:, HD:] = jnp.ones((KEYS, HD), jnp.bfloat16)
-    blocks = [own, lower, upper] + [above.at[i] for i in range(3)] + [below.at[i] for i in range(2)]
+    blocks = [(block.at[0], block.at[1]) for block in (own, lower, upper)]
+    blocks += [(above.at[0], below.at[4]), (above.at[1], above.at[2]), (above.at[3], above.at[4])]
+    blocks += [(below.at[0], below.at[1]), (below.at[2], below.at[3])]
     high = jnp.zeros((NEWT, HD), jnp.float32)
     low = jnp.zeros((NEWT, HD), jnp.float32)
     count = jnp.int32(0)
-    for block, offset in zip(blocks, OFFSETS, strict=True):
+    for (block_keys, block_values), offset in zip(blocks, OFFSETS, strict=True):
         source_line = lax.rem(line + offset + LINE, LINE)
         source = ctx + (source_line - line) * stride
         other = lax.rem(source + ZN * YN // 2, ZN * YN)
         first = pl.multiple_of(source_line * NEWT, NEWT)
-        keys[pl.ds(first, NEWT), :] = block[0, HISTORY : HISTORY + NEWT, :]
-        values[pl.ds(first, NEWT), :HD] = block[1, HISTORY : HISTORY + NEWT, :]
-        high += block[0, HISTORY + NEWT :, :].astype(jnp.float32)
-        low += block[1, HISTORY + NEWT :, :].astype(jnp.float32)
+        keys[pl.ds(first, NEWT), :] = block_keys[HISTORY : HISTORY + NEWT, :]
+        values[pl.ds(first, NEWT), :HD] = block_values[HISTORY : HISTORY + NEWT, :]
+        high += block_keys[HISTORY + NEWT :, :].astype(jnp.float32)
+        low += block_values[HISTORY + NEWT :, :].astype(jnp.float32)
         candidates = [page_slots[2 * source], page_slots[2 * source + 1]]
         candidates += [page_slots[2 * other], page_slots[2 * other + 1]]
         for s in range(SLOTS):
             slot = source * SLOTS + s
             live = functools.reduce(jnp.logical_or, [candidate == slot for candidate in candidates])
             to = pl.multiple_of(FRESH + count * PAGE, PAGE)
-            keys[pl.ds(to, PAGE), :] = block[0, s * PAGE : (s + 1) * PAGE, :]
-            values[pl.ds(to, PAGE), :HD] = block[1, s * PAGE : (s + 1) * PAGE, :]
+            keys[pl.ds(to, PAGE), :] = block_keys[s * PAGE : (s + 1) * PAGE, :]
+            values[pl.ds(to, PAGE), :HD] = block_values[s * PAGE : (s + 1) * PAGE, :]
             count += live.astype(jnp.int32)
     key_at = (high * 32.0 + low)[0:1]
     places = functools.reduce(lambda size, less: jnp.where(count <= less, less, size), SIZES[-2::-1], SIZES[-1])
@@ -297,9 +299,10 @@
         scratch_shapes=[pltpu.VMEM((XN, WIRE, HD), jnp.bfloat16), pltpu.SemaphoreType.DMA((LINE,))],
     )(q_kept, q_received, tags)
     q = lax.all_to_all(q, ALL, split_axis=0, concat_axis=0, axis_index_groups=CROSS, tiled=True)
-    three, two = call(join_kernel, (bf16(3, 2, KV_ROWS, HD), bf16(2, 2, KV_ROWS, HD)), flops=JOIN)(kv, lower, upper)
-    above = lax.ppermute(three, ALL, along(-1))
-    below = lax.ppermute(two, ALL, along(1))
+    halves = bf16(5, KV_ROWS, HD)
+    down, up = call(join_kernel, (halves, halves), flops=JOIN)(kv, lower, upper)
+    above = lax.ppermute(down, ALL, along(-1))
+    below = lax.ppermute(up, ALL, along(1))
     parts = attend(page_slots, (kv, lower, upper, above, below), q)
     parts = lax.all_to_all(parts, ALL, split_axis=0, concat_axis=0, axis_index_groups=CROSS, tiled=True)
 

time: 79.7 us -> 81.2 us (1.019)
  blocking collectives: 23.1 us -> 20.5 us
  starting transfers between devices: 31.9 us -> 34.5 us
  Pallas kernels: 10.4 us -> 11.4 us
    ppermute x1, starting transfers between devices: 1.92 us -> 4.68 us  [body(): received = lax.ppermute(combined(1), ALL, SWAP)]
    all_to_all x1, blocking collectives: 23.1 us -> 20.5 us  [body(): lax.all_to_all(parts, ALL, split_axis=0, concat_axis=0, axis_index_groups...]
    pallas_call x1, Pallas kernels: 6.92 us -> 8.03 us  [attend(): call(attend_kernel, bf16(BLOCKS, WIRE, HD), megabytes=20, flops=230000000...]
where the time goes in v9:
time: 81.2 us; the launch traced here: 80.8 us
  starting transfers between devices  34.5 us (42%)
  blocking collectives  20.5 us (25%)
  waiting for transfers between devices  14.2 us (17%)
  Pallas kernels  11.4 us (14%)
    all_to_all x1, blocking collectives, body(): lax.all_to_all(parts, ALL, split_axis=0, concat_axis=0, axis_index_groups...  20.5 us
    all_to_all x1, starting transfers between devices, body(): lax.all_to_all(q, ALL, split_axis=0, concat_axis=0, axis_index_groups=CRO...  11.5 us
    ppermute x1, waiting for transfers between devices, body(): above = lax.ppermute(down, ALL, along(-1))  11.3 us
    ppermute x1, starting transfers between devices, body(): q_received = lax.ppermute(q_sent, ALL, SWAP)  8.79 us
    pallas_call x1, Pallas kernels, attend(): call(attend_kernel, bf16(BLOCKS, WIRE, HD), megabytes=20, flops=230000000...  8.03 us
    ppermute x1, starting transfers between devices, body(): received = lax.ppermute(combined(1), ALL, SWAP)  4.68 us
    ppermute x1, starting transfers between devices, body(): above = lax.ppermute(down, ALL, along(-1))  2.98 us
    ppermute x1, starting transfers between devices, body(): below = lax.ppermute(up, ALL, along(1))  2.75 us
  transfers between devices with their start and end apart: 7, of which 4 were waited for; matrix products, arithmetic and copies ran while one was open for 0% of the time, Pallas kernels for 2%

profile of v9, /device:TPU:1, one launch (start us, length us, event | category | flops | bytes accessed | tf_op | source)
XLA Modules:
  0.0 80.8 jit_solution(11540858126055299588)
XLA Ops:
  0.0 1.0 %shard_map.73 = (bf16[2,416,128]{2,1,0:T(8,128)(2,1)S(1)}, bf16[2,4,16,128]{3,2,1,0:T(8,128)(2,1)S(1)}, bf16[2,4,16,128]{3,2,1,0:T(8,128)(2,1)S(1)}, bf16[8,128]{1,0:T(8,128)(2,1)S(1)}) custom-call(s32[16]{0:T(128)} %positions.1, bf16[2,4,2,16,128]{4,3,2,1,0:T(8,128)(2,1)} %bitcast.7, bf16[384,128]{1,0:T(8,128)(2,1)} %bitcast.5, bf16[384,128]{1,0:T(8,128)(2,1)} %bitcast.6, ...), custom_call_target="tpu_custom_call" | custom-call | flops 1000000 | bytes 800000 | tf_op jit(solution)/shard_map/pallas_call | solution.py:285
  1.0 8.8 %collective-permute-start = (bf16[2,4,16,128]{3,2,1,0:T(8,128)(2,1)S(1)}, bf16[2,4,16,128]{3,2,1,0:T(8,128)(2,1)S(1)}, u32[]{:S(2)}, u32[]{:S(2)}) collective-permute-start(bf16[2,4,16,128]{3,2,1,0:T(8,128)(2,1)S(1)} %get-tuple-element.14), channel_id=1, source_target_pairs={{0,1},{1,0},{2,3},{3,2},{4,5},{5,4},{6,7},{7,6},{8,9},{9,8},{10,11... | collective-permute-start | bytes 98312 | tf_op jit(solution)/shard_map/ppermute | solution.py:291
  9.8 0.8 %collective-permute-done.received = bf16[2,4,16,128]{3,2,1,0:T(8,128)(2,1)S(1)} collective-permute-done((bf16[2,4,16,128]{3,2,1,0:T(8,128)(2,1)S(1)}, bf16[2,4,16,128]{3,2,1,0:T(8,128)(2,1)S(1)}, u32[]{:S(2)}, u32[]{:S(2)}) %collective-permute-start) | collective-permute-done | bytes 32800 | tf_op jit(solution)/shard_map/ppermute | solution.py:291
  10.6 1.9 %collective-permute-start.2 = (bf16[2,416,128]{2,1,0:T(8,128)(2,1)S(1)}, bf16[2,416,128]{2,1,0:T(8,128)(2,1)S(1)}, u32[]{:S(2)}, u32[]{:S(2)}) collective-permute-start(bf16[2,416,128]{2,1,0:T(8,128)(2,1)S(1)} %get-tuple-element.15.own), channel_id=1, source_target_pairs={{0,384},{1,49},{2,386},{3,51},{4,388},{5,53},{6,390},{7,55},{8,392... | collective-permute-start | bytes 638984 | tf_op jit(solution)/shard_map/ppermute | solution.py:294
  12.6 1.9 %collective-permute-start.1 = (bf16[2,416,128]{2,1,0:T(8,128)(2,1)S(1)}, bf16[2,416,128]{2,1,0:T(8,128)(2,1)S(1)}, u32[]{:S(2)}, u32[]{:S(2)}) collective-permute-start(bf16[2,416,128]{2,1,0:T(8,128)(2,1)S(1)} %get-tuple-element.15.own), channel_id=1, source_target_pairs={{0,192},{1,25},{2,194},{3,27},{4,196},{5,29},{6,198},{7,31},{8,200... | collective-permute-start | bytes 638984 | tf_op jit(solution)/shard_map/ppermute | solution.py:293
  14.5 0.9 %shard_map.75 = bf16[32,72,128]{2,1,0:T(8,128)(2,1)} custom-call(bf16[2,4,16,128]{3,2,1,0:T(8,128)(2,1)S(1)} %get-tuple-element.18.kept, bf16[2,4,16,128]{3,2,1,0:T(8,128)(2,1)S(1)} %collective-permute-done.received, bf16[8,128]{1,0:T(8,128)(2,1)S(1)} %get-tuple-element.20.tags), custom_call_target="tpu_custom_call" | custom-call | flops 1000000 | bytes 800000 | tf_op jit(solution)/shard_map/pallas_call | solution.py:295
  15.4 11.5 %all-to-all-start = ((bf16[32,72,128]{2,1,0:T(8,128)(2,1)}), bf16[32,72,128]{2,1,0:T(8,128)(2,1)S(1)}, u32[]{:S(2)}, u32[]{:S(2)}) async-start(bf16[32,72,128]{2,1,0:T(8,128)(2,1)} %shard_map.75), calls=%async_computation | async-start | bytes 1179648 | tf_op jit(solution)/shard_map/all_to_all | solution.py:301
  26.9 0.0 collective-permute-done.2.upper
  26.9 0.0 collective-permute-done.1.lower
  26.9 0.1 shard_map.74
  27.0 0.0 copy-start
  27.0 3.0 %collective-permute-start.3 = (bf16[5,416,128]{2,1,0:T(8,128)(2,1)S(1)}, bf16[5,416,128]{2,1,0:T(8,128)(2,1)S(1)}, u32[]{:S(2)}, u32[]{:S(2)}) collective-permute-start(bf16[5,416,128]{2,1,0:T(8,128)(2,1)S(1)} %get-tuple-element.16), channel_id=1, source_target_pairs={{0,448},{1,57},{2,450},{3,59},{4,452},{5,61},{6,454},{7,63},{8,456... | collective-permute-start | bytes 1597448 | tf_op jit(solution)/shard_map/ppermute | solution.py:304
  30.0 2.8 %collective-permute-start.4 = (bf16[5,416,128]{2,1,0:T(8,128)(2,1)S(1)}, bf16[5,416,128]{2,1,0:T(8,128)(2,1)S(1)}, u32[]{:S(2)}, u32[]{:S(2)}) collective-permute-start(bf16[5,416,128]{2,1,0:T(8,128)(2,1)S(1)} %get-tuple-element.17), channel_id=1, source_target_pairs={{0,64},{1,9},{2,66},{3,11},{4,68},{5,13},{6,70},{7,15},{8,72},{9,1... | collective-permute-start | bytes 1597448 | tf_op jit(solution)/shard_map/ppermute | solution.py:305
  32.8 11.3 %collective-permute-done.3.above = bf16[5,416,128]{2,1,0:T(8,128)(2,1)S(1)} collective-permute-done((bf16[5,416,128]{2,1,0:T(8,128)(2,1)S(1)}, bf16[5,416,128]{2,1,0:T(8,128)(2,1)S(1)}, u32[]{:S(2)}, u32[]{:S(2)}) %collective-permute-start.3) | collective-permute-done | bytes 532512 | tf_op jit(solution)/shard_map/ppermute | solution.py:304
  44.1 1.6 %collective-permute-done.4.below = bf16[5,416,128]{2,1,0:T(8,128)(2,1)S(1)} collective-permute-done((bf16[5,416,128]{2,1,0:T(8,128)(2,1)S(1)}, bf16[5,416,128]{2,1,0:T(8,128)(2,1)S(1)}, u32[]{:S(2)}, u32[]{:S(2)}) %collective-permute-start.4) | collective-permute-done | bytes 532512 | tf_op jit(solution)/shard_map/ppermute | solution.py:305
  45.7 0.0 all-to-all-done.q
  45.7 0.0 copy-done
  45.7 8.0 %shard_map.76 = bf16[32,72,128]{2,1,0:T(8,128)(2,1)S(1)} custom-call(s32[128]{0:T(128)S(1)} %copy-done, bf16[2,416,128]{2,1,0:T(8,128)(2,1)S(1)} %get-tuple-element.15.own, bf16[2,416,128]{2,1,0:T(8,128)(2,1)S(1)} %collective-permute-done.1.lower, bf16[2,416,128]{2,1,0:T(8,128)(2,1)S(1)} %collective-permute-done.2.upper, ...), custom_call_target="tpu_custom_call" | custom-call | flops 2300000000 | bytes 5000000 | tf_op jit(solution)/shard_map/pallas_call | solution.py:230
  53.7 20.5 %all_to_all.10.parts = bf16[32,72,128]{2,1,0:T(8,128)(2,1)S(1)} all-to-all(bf16[32,72,128]{2,1,0:T(8,128)(2,1)S(1)} %shard_map.76), channel_id=1, replica_groups={{0,2,4,6,8,10,12,14,16,18,20,22,24,26,28,30,32,34,36,38,40,42,44,46,48,..., dimensions={0} | all-to-all | bytes 1179648 | tf_op jit(solution)/shard_map/all_to_all | solution.py:307
  74.2 0.4 shard_map.78
  74.6 4.7 %collective-permute-start.5 = (bf16[2,4,16,128]{3,2,1,0:T(8,128)(2,1)S(1)}, bf16[2,4,16,128]{3,2,1,0:T(8,128)(2,1)S(1)}, u32[]{:S(2)}, u32[]{:S(2)}) collective-permute-start(bf16[2,4,16,128]{3,2,1,0:T(8,128)(2,1)S(1)} %shard_map.78), channel_id=1, source_target_pairs={{0,1},{1,0},{2,3},{3,2},{4,5},{5,4},{6,7},{7,6},{8,9},{9,8},{10,11... | collective-permute-start | bytes 98312 | tf_op jit(solution)/shard_map/ppermute | solution.py:316
  79.3 0.4 shard_map.77.kept
  79.7 0.4 collective-permute-done.5.received
  80.1 0.6 shard_map.79
Async XLA Ops:
  1.0 9.6 %collective-permute-start = (bf16[2,4,16,128]{3,2,1,0:T(8,128)(2,1)S(1)}, bf16[2,4,16,128]{3,2,1,0:T(8,128)(2,1)S(1)}, u32[]{:S(2)}, u32[]{:S(2)}) collective-permute-start(bf16[2,4,16,128]{3,2,1,0:T(8,128)(2,1)S(1)} %get-tuple-element.14), channel_id=1, source_target_pairs={{0,1},{1,0},{2,3},{3,2},{4,5},{5,4},{6,7},{7,6},{8,9},{9,8},{10,11... | collective-permute-start | bytes 98312 | tf_op jit(solution)/shard_map/ppermute | solution.py:291
  10.6 16.2 %collective-permute-start.2 = (bf16[2,416,128]{2,1,0:T(8,128)(2,1)S(1)}, bf16[2,416,128]{2,1,0:T(8,128)(2,1)S(1)}, u32[]{:S(2)}, u32[]{:S(2)}) collective-permute-start(bf16[2,416,128]{2,1,0:T(8,128)(2,1)S(1)} %get-tuple-element.15.own), channel_id=1, source_target_pairs={{0,384},{1,49},{2,386},{3,51},{4,388},{5,53},{6,390},{7,55},{8,392... | collective-permute-start | bytes 638984 | tf_op jit(solution)/shard_map/ppermute | solution.py:294
  12.6 14.3 %collective-permute-start.1 = (bf16[2,416,128]{2,1,0:T(8,128)(2,1)S(1)}, bf16[2,416,128]{2,1,0:T(8,128)(2,1)S(1)}, u32[]{:S(2)}, u32[]{:S(2)}) collective-permute-start(bf16[2,416,128]{2,1,0:T(8,128)(2,1)S(1)} %get-tuple-element.15.own), channel_id=1, source_target_pairs={{0,192},{1,25},{2,194},{3,27},{4,196},{5,29},{6,198},{7,31},{8,200... | collective-permute-start | bytes 638984 | tf_op jit(solution)/shard_map/ppermute | solution.py:293
  15.4 30.3 %all-to-all-start = ((bf16[32,72,128]{2,1,0:T(8,128)(2,1)}), bf16[32,72,128]{2,1,0:T(8,128)(2,1)S(1)}, u32[]{:S(2)}, u32[]{:S(2)}) async-start(bf16[32,72,128]{2,1,0:T(8,128)(2,1)} %shard_map.75), calls=%async_computation | async-start | bytes 1179648 | tf_op jit(solution)/shard_map/all_to_all | solution.py:301
  27.0 18.7 %copy-start = (s32[128]{0:T(128)S(1)}, s32[128]{0:T(128)}, u32[]{:S(2)}) copy-start(s32[128]{0:T(128)} %page_slots.1) | copy-start | bytes 1540
  27.0 17.1 %collective-permute-start.3 = (bf16[5,416,128]{2,1,0:T(8,128)(2,1)S(1)}, bf16[5,416,128]{2,1,0:T(8,128)(2,1)S(1)}, u32[]{:S(2)}, u32[]{:S(2)}) collective-permute-start(bf16[5,416,128]{2,1,0:T(8,128)(2,1)S(1)} %get-tuple-element.16), channel_id=1, source_target_pairs={{0,448},{1,57},{2,450},{3,59},{4,452},{5,61},{6,454},{7,63},{8,456... | collective-permute-start | bytes 1597448 | tf_op jit(solution)/shard_map/ppermute | solution.py:304
  30.0 15.7 %collective-permute-start.4 = (bf16[5,416,128]{2,1,0:T(8,128)(2,1)S(1)}, bf16[5,416,128]{2,1,0:T(8,128)(2,1)S(1)}, u32[]{:S(2)}, u32[]{:S(2)}) collective-permute-start(bf16[5,416,128]{2,1,0:T(8,128)(2,1)S(1)} %get-tuple-element.17), channel_id=1, source_target_pairs={{0,64},{1,9},{2,66},{3,11},{4,68},{5,13},{6,70},{7,15},{8,72},{9,1... | collective-permute-start | bytes 1597448 | tf_op jit(solution)/shard_map/ppermute | solution.py:305
  74.6 5.5 %collective-permute-start.5 = (bf16[2,4,16,128]{3,2,1,0:T(8,128)(2,1)S(1)}, bf16[2,4,16,128]{3,2,1,0:T(8,128)(2,1)S(1)}, u32[]{:S(2)}, u32[]{:S(2)}) collective-permute-start(bf16[2,4,16,128]{3,2,1,0:T(8,128)(2,1)S(1)} %shard_map.78), channel_id=1, source_target_pairs={{0,1},{1,0},{2,3},{3,2},{4,5},{5,4},{6,7},{7,6},{8,9},{9,8},{10,11... | collective-permute-start | bytes 98312 | tf_op jit(solution)/shard_map/ppermute | solution.py:316

commit v10 on v8

--- a/solution.py
+++ b/solution.py
@@ -32,6 +32,7 @@
 TO_BITS = math.log2(math.e) / math.sqrt(HD)
 LOWEST = -1e30
 JOIN = 30000000000
+SPREAD = 10000000000
 
 IDS = np.arange(ZN * YN * XN * CN).reshape(ZN, YN, XN, CN)
 CROSS = [IDS[z, :, :, 0].ravel().tolist() for z in range(ZN)] + [IDS[:, y, :, 1].ravel().tolist() for y in range(YN)]
@@ -287,12 +288,12 @@
         scratch_shapes=[pltpu.SMEM((NEWT,), jnp.int32), pltpu.SemaphoreType.DMA((7,))],
     )(*(pltpu.with_memory_space_constraint(source, pltpu.HBM) for source in sources))
     q_received = lax.ppermute(q_sent, ALL, SWAP)
-    kv, q_received = lax.optimization_barrier((kv, q_received))
     lower = lax.ppermute(kv, ALL, along(3))
     upper = lax.ppermute(kv, ALL, along(-2))
     q = call(
         spread_kernel,
         bf16(BLOCKS, WIRE, HD),
+        flops=SPREAD,
         out_specs=HBM,
         scratch_shapes=[pltpu.VMEM((XN, WIRE, HD), jnp.bfloat16), pltpu.SemaphoreType.DMA((LINE,))],
     )(q_kept, q_received, tags)

time: 79.7 us -> 78 us (0.979)
  blocking collectives: 23.1 us -> 21 us
  waiting for transfers between devices: 13.8 us -> 12.4 us
  Pallas kernels: 10.4 us -> 11.5 us
    all_to_all x1, blocking collectives: 23.1 us -> 21 us  [body(): lax.all_to_all(parts, ALL, split_axis=0, concat_axis=0, axis_index_groups...]
    pallas_call x1, Pallas kernels: 6.92 us -> 8.03 us  [attend(): call(attend_kernel, bf16(BLOCKS, WIRE, HD), megabytes=20, flops=230000000...]
    ppermute x1, waiting for transfers between devices: 0.84 us -> 0.01 us  [body(): q_received = lax.ppermute(q_sent, ALL, SWAP)]
  transfers between devices with their start and end apart: 7 -> 7, of which waited for: 4 -> 3; matrix products, arithmetic and copies ran while one was open for 0% -> 0% of each run, Pallas kernels for 2% -> 2%
where the time goes in v10:
time: 78 us; the launch traced here: 77.6 us
  starting transfers between devices  32.5 us (42%)
  blocking collectives  21 us (27%)
  waiting for transfers between devices  12.4 us (16%)
  Pallas kernels  11.5 us (15%)
    all_to_all x1, blocking collectives, body(): lax.all_to_all(parts, ALL, split_axis=0, concat_axis=0, axis_index_groups...  21 us
    all_to_all x1, starting transfers between devices, body(): lax.all_to_all(q, ALL, split_axis=0, concat_axis=0, axis_index_groups=CRO...  12.1 us
    ppermute x1, waiting for transfers between devices, body(): below = lax.ppermute(two, ALL, along(1))  11.3 us
    ppermute x1, starting transfers between devices, body(): q_received = lax.ppermute(q_sent, ALL, SWAP)  8.79 us
    pallas_call x1, Pallas kernels, attend(): call(attend_kernel, bf16(BLOCKS, WIRE, HD), megabytes=20, flops=230000000...  8.03 us
    ppermute x1, starting transfers between devices, body(): below = lax.ppermute(two, ALL, along(1))  2.91 us
    ppermute x1, starting transfers between devices, body(): received = lax.ppermute(combined(1), ALL, SWAP)  2.5 us
    ppermute x1, starting transfers between devices, body(): above = lax.ppermute(three, ALL, along(-1))  2.38 us
  transfers between devices with their start and end apart: 7, of which 3 were waited for; matrix products, arithmetic and copies ran while one was open for 0% of the time, Pallas kernels for 2%

profile of v10, /device:TPU:1, one launch (start us, length us, event | category | flops | bytes accessed | tf_op | source)
XLA Modules:
  0.0 77.6 jit_solution(16131288201664134196)
XLA Ops:
  0.0 1.0 %shard_map.73 = (bf16[2,416,128]{2,1,0:T(8,128)(2,1)S(1)}, bf16[2,4,16,128]{3,2,1,0:T(8,128)(2,1)S(1)}, bf16[2,4,16,128]{3,2,1,0:T(8,128)(2,1)S(1)}, bf16[8,128]{1,0:T(8,128)(2,1)S(1)}) custom-call(s32[16]{0:T(128)} %positions.1, bf16[2,4,2,16,128]{4,3,2,1,0:T(8,128)(2,1)} %bitcast.7, bf16[384,128]{1,0:T(8,128)(2,1)} %bitcast.5, bf16[384,128]{1,0:T(8,128)(2,1)} %bitcast.6, ...), custom_call_target="tpu_custom_call" | custom-call | flops 1000000 | bytes 800000 | tf_op jit(solution)/shard_map/pallas_call | solution.py:284
  1.0 8.8 %collective-permute-start.4 = (bf16[2,4,16,128]{3,2,1,0:T(8,128)(2,1)S(1)}, bf16[2,4,16,128]{3,2,1,0:T(8,128)(2,1)S(1)}, u32[]{:S(2)}, u32[]{:S(2)}) collective-permute-start(bf16[2,4,16,128]{3,2,1,0:T(8,128)(2,1)S(1)} %get-tuple-element.15), channel_id=1, source_target_pairs={{0,1},{1,0},{2,3},{3,2},{4,5},{5,4},{6,7},{7,6},{8,9},{9,8},{10,11... | collective-permute-start | bytes 98312 | tf_op jit(solution)/shard_map/ppermute | solution.py:290
  9.8 1.9 %collective-permute-start = (bf16[2,416,128]{2,1,0:T(8,128)(2,1)S(1)}, bf16[2,416,128]{2,1,0:T(8,128)(2,1)S(1)}, u32[]{:S(2)}, u32[]{:S(2)}) collective-permute-start(bf16[2,416,128]{2,1,0:T(8,128)(2,1)S(1)} %get-tuple-element.11.own), channel_id=1, source_target_pairs={{0,192},{1,25},{2,194},{3,27},{4,196},{5,29},{6,198},{7,31},{8,200... | collective-permute-start | bytes 638984 | tf_op jit(solution)/shard_map/ppermute | solution.py:291
  11.7 1.9 %collective-permute-start.1 = (bf16[2,416,128]{2,1,0:T(8,128)(2,1)S(1)}, bf16[2,416,128]{2,1,0:T(8,128)(2,1)S(1)}, u32[]{:S(2)}, u32[]{:S(2)}) collective-permute-start(bf16[2,416,128]{2,1,0:T(8,128)(2,1)S(1)} %get-tuple-element.11.own), channel_id=1, source_target_pairs={{0,384},{1,49},{2,386},{3,51},{4,388},{5,53},{6,390},{7,55},{8,392... | collective-permute-start | bytes 638984 | tf_op jit(solution)/shard_map/ppermute | solution.py:292
  13.7 0.0 collective-permute-done.4.received
  13.7 0.9 %shard_map.75 = bf16[32,72,128]{2,1,0:T(8,128)(2,1)} custom-call(bf16[2,4,16,128]{3,2,1,0:T(8,128)(2,1)S(1)} %get-tuple-element.14.kept, bf16[2,4,16,128]{3,2,1,0:T(8,128)(2,1)S(1)} %collective-permute-done.4.received, bf16[8,128]{1,0:T(8,128)(2,1)S(1)} %get-tuple-element.16.tags), custom_call_target="tpu_custom_call" | custom-call | flops 10000000000 | bytes 800000 | tf_op jit(solution)/shard_map/pallas_call | solution.py:293
  14.6 12.1 %all-to-all-start = ((bf16[32,72,128]{2,1,0:T(8,128)(2,1)}), bf16[32,72,128]{2,1,0:T(8,128)(2,1)S(1)}, u32[]{:S(2)}, u32[]{:S(2)}) async-start(bf16[32,72,128]{2,1,0:T(8,128)(2,1)} %shard_map.75), calls=%async_computation | async-start | bytes 1179648 | tf_op jit(solution)/shard_map/all_to_all | solution.py:300
  26.7 0.0 collective-permute-done.lower
  26.7 0.0 collective-permute-done.1.upper
  26.7 0.1 shard_map.74
  26.8 0.0 copy-start
  26.8 2.4 %collective-permute-start.2 = (bf16[3,2,416,128]{3,2,1,0:T(8,128)(2,1)S(1)}, bf16[3,2,416,128]{3,2,1,0:T(8,128)(2,1)S(1)}, u32[]{:S(2)}, u32[]{:S(2)}) collective-permute-start(bf16[3,2,416,128]{3,2,1,0:T(8,128)(2,1)S(1)} %get-tuple-element.12), channel_id=1, source_target_pairs={{0,448},{1,57},{2,450},{3,59},{4,452},{5,61},{6,454},{7,63},{8,456... | collective-permute-start | bytes 1916936 | tf_op jit(solution)/shard_map/ppermute | solution.py:302
  29.2 2.9 %collective-permute-start.3 = (bf16[2,2,416,128]{3,2,1,0:T(8,128)(2,1)S(1)}, bf16[2,2,416,128]{3,2,1,0:T(8,128)(2,1)S(1)}, u32[]{:S(2)}, u32[]{:S(2)}) collective-permute-start(bf16[2,2,416,128]{3,2,1,0:T(8,128)(2,1)S(1)} %get-tuple-element.13), channel_id=1, source_target_pairs={{0,64},{1,9},{2,66},{3,11},{4,68},{5,13},{6,70},{7,15},{8,72},{9,1... | collective-permute-start | bytes 1277960 | tf_op jit(solution)/shard_map/ppermute | solution.py:303
  32.1 11.3 %collective-permute-done.3.below = bf16[2,2,416,128]{3,2,1,0:T(8,128)(2,1)S(1)} collective-permute-done((bf16[2,2,416,128]{3,2,1,0:T(8,128)(2,1)S(1)}, bf16[2,2,416,128]{3,2,1,0:T(8,128)(2,1)S(1)}, u32[]{:S(2)}, u32[]{:S(2)}) %collective-permute-start.3) | collective-permute-done | bytes 426016 | tf_op jit(solution)/shard_map/ppermute | solution.py:303
  43.4 0.7 collective-permute-done.2.above
  44.1 0.0 all-to-all-done.q
  44.1 0.0 copy-done
  44.1 8.0 %shard_map.76 = bf16[32,72,128]{2,1,0:T(8,128)(2,1)S(1)} custom-call(s32[128]{0:T(128)S(1)} %copy-done, bf16[2,416,128]{2,1,0:T(8,128)(2,1)S(1)} %get-tuple-element.11.own, bf16[2,416,128]{2,1,0:T(8,128)(2,1)S(1)} %collective-permute-done.lower, bf16[2,416,128]{2,1,0:T(8,128)(2,1)S(1)} %collective-permute-done.1.upper, ...), custom_call_target="tpu_custom_call" | custom-call | flops 2300000000 | bytes 5000000 | tf_op jit(solution)/shard_map/pallas_call | solution.py:229
  52.2 21.0 %all_to_all.10.parts = bf16[32,72,128]{2,1,0:T(8,128)(2,1)S(1)} all-to-all(bf16[32,72,128]{2,1,0:T(8,128)(2,1)S(1)} %shard_map.76), channel_id=1, replica_groups={{0,2,4,6,8,10,12,14,16,18,20,22,24,26,28,30,32,34,36,38,40,42,44,46,48,..., dimensions={0} | all-to-all | bytes 1179648 | tf_op jit(solution)/shard_map/all_to_all | solution.py:305
  73.2 0.4 shard_map.78
  73.6 2.5 %collective-permute-start.5 = (bf16[2,4,16,128]{3,2,1,0:T(8,128)(2,1)S(1)}, bf16[2,4,16,128]{3,2,1,0:T(8,128)(2,1)S(1)}, u32[]{:S(2)}, u32[]{:S(2)}) collective-permute-start(bf16[2,4,16,128]{3,2,1,0:T(8,128)(2,1)S(1)} %shard_map.78), channel_id=1, source_target_pairs={{0,1},{1,0},{2,3},{3,2},{4,5},{5,4},{6,7},{7,6},{8,9},{9,8},{10,11... | collective-permute-start | bytes 98312 | tf_op jit(solution)/shard_map/ppermute | solution.py:314
  76.1 0.4 shard_map.77.kept
  76.5 0.4 collective-permute-done.5.received
  76.9 0.6 shard_map.79
Async XLA Ops:
  1.0 12.7 %collective-permute-start.4 = (bf16[2,4,16,128]{3,2,1,0:T(8,128)(2,1)S(1)}, bf16[2,4,16,128]{3,2,1,0:T(8,128)(2,1)S(1)}, u32[]{:S(2)}, u32[]{:S(2)}) collective-permute-start(bf16[2,4,16,128]{3,2,1,0:T(8,128)(2,1)S(1)} %get-tuple-element.15), channel_id=1, source_target_pairs={{0,1},{1,0},{2,3},{3,2},{4,5},{5,4},{6,7},{7,6},{8,9},{9,8},{10,11... | collective-permute-start | bytes 98312 | tf_op jit(solution)/shard_map/ppermute | solution.py:290
  9.8 16.9 %collective-permute-start = (bf16[2,416,128]{2,1,0:T(8,128)(2,1)S(1)}, bf16[2,416,128]{2,1,0:T(8,128)(2,1)S(1)}, u32[]{:S(2)}, u32[]{:S(2)}) collective-permute-start(bf16[2,416,128]{2,1,0:T(8,128)(2,1)S(1)} %get-tuple-element.11.own), channel_id=1, source_target_pairs={{0,192},{1,25},{2,194},{3,27},{4,196},{5,29},{6,198},{7,31},{8,200... | collective-permute-start | bytes 638984 | tf_op jit(solution)/shard_map/ppermute | solution.py:291
  11.7 15.0 %collective-permute-start.1 = (bf16[2,416,128]{2,1,0:T(8,128)(2,1)S(1)}, bf16[2,416,128]{2,1,0:T(8,128)(2,1)S(1)}, u32[]{:S(2)}, u32[]{:S(2)}) collective-permute-start(bf16[2,416,128]{2,1,0:T(8,128)(2,1)S(1)} %get-tuple-element.11.own), channel_id=1, source_target_pairs={{0,384},{1,49},{2,386},{3,51},{4,388},{5,53},{6,390},{7,55},{8,392... | collective-permute-start | bytes 638984 | tf_op jit(solution)/shard_map/ppermute | solution.py:292
  14.6 29.5 %all-to-all-start = ((bf16[32,72,128]{2,1,0:T(8,128)(2,1)}), bf16[32,72,128]{2,1,0:T(8,128)(2,1)S(1)}, u32[]{:S(2)}, u32[]{:S(2)}) async-start(bf16[32,72,128]{2,1,0:T(8,128)(2,1)} %shard_map.75), calls=%async_computation | async-start | bytes 1179648 | tf_op jit(solution)/shard_map/all_to_all | solution.py:300
  26.8 17.3 %copy-start = (s32[128]{0:T(128)S(1)}, s32[128]{0:T(128)}, u32[]{:S(2)}) copy-start(s32[128]{0:T(128)} %page_slots.1) | copy-start | bytes 1540
  26.8 17.3 %collective-permute-start.2 = (bf16[3,2,416,128]{3,2,1,0:T(8,128)(2,1)S(1)}, bf16[3,2,416,128]{3,2,1,0:T(8,128)(2,1)S(1)}, u32[]{:S(2)}, u32[]{:S(2)}) collective-permute-start(bf16[3,2,416,128]{3,2,1,0:T(8,128)(2,1)S(1)} %get-tuple-element.12), channel_id=1, source_target_pairs={{0,448},{1,57},{2,450},{3,59},{4,452},{5,61},{6,454},{7,63},{8,456... | collective-permute-start | bytes 1916936 | tf_op jit(solution)/shard_map/ppermute | solution.py:302
  29.2 14.2 %collective-permute-start.3 = (bf16[2,2,416,128]{3,2,1,0:T(8,128)(2,1)S(1)}, bf16[2,2,416,128]{3,2,1,0:T(8,128)(2,1)S(1)}, u32[]{:S(2)}, u32[]{:S(2)}) collective-permute-start(bf16[2,2,416,128]{3,2,1,0:T(8,128)(2,1)S(1)} %get-tuple-element.13), channel_id=1, source_target_pairs={{0,64},{1,9},{2,66},{3,11},{4,68},{5,13},{6,70},{7,15},{8,72},{9,1... | collective-permute-start | bytes 1277960 | tf_op jit(solution)/shard_map/ppermute | solution.py:303
  73.6 3.3 %collective-permute-start.5 = (bf16[2,4,16,128]{3,2,1,0:T(8,128)(2,1)S(1)}, bf16[2,4,16,128]{3,2,1,0:T(8,128)(2,1)S(1)}, u32[]{:S(2)}, u32[]{:S(2)}) collective-permute-start(bf16[2,4,16,128]{3,2,1,0:T(8,128)(2,1)S(1)} %shard_map.78), channel_id=1, source_target_pairs={{0,1},{1,0},{2,3},{3,2},{4,5},{5,4},{6,7},{7,6},{8,9},{9,8},{10,11... | collective-permute-start | bytes 98312 | tf_op jit(solution)/shard_map/ppermute | solution.py:314

commit v11 on v10

--- a/solution.py
+++ b/solution.py
@@ -28,7 +28,7 @@
 PARTS = BLOCKS // STEP_BLOCKS
 CHUNK = 512
 SIZES = (16, 18, 20, 24)
-OFFSETS = (0, -3, 2, 1, -2, 3, -1, -4)
+OFFSETS = (0, 3, -2, 1, 4, -1, 2, -3)
 TO_BITS = math.log2(math.e) / math.sqrt(HD)
 LOWEST = -1e30
 JOIN = 30000000000
@@ -127,8 +127,8 @@
 def join_kernel(own, lower, upper, three, two):
     for i, block in enumerate((own, lower, upper)):
         three[i] = block[...]
-        if i < 2:
-            two[i] = block[...]
+        if i > 0:
+            two[i - 1] = block[...]
 
 
 def attend_kernel(page_slots, own, lower, upper, above, below, q, out, keys, values, scores):
@@ -288,8 +288,8 @@
         scratch_shapes=[pltpu.SMEM((NEWT,), jnp.int32), pltpu.SemaphoreType.DMA((7,))],
     )(*(pltpu.with_memory_space_constraint(source, pltpu.HBM) for source in sources))
     q_received = lax.ppermute(q_sent, ALL, SWAP)
-    lower = lax.ppermute(kv, ALL, along(3))
-    upper = lax.ppermute(kv, ALL, along(-2))
+    lower = lax.ppermute(kv, ALL, along(-3))
+    upper = lax.ppermute(kv, ALL, along(2))
     q = call(
         spread_kernel,
         bf16(BLOCKS, WIRE, HD),

time: 78 us -> 80.7 us (1.035)
  starting transfers between devices: 32.5 us -> 35.3 us
  Pallas kernels: 11.5 us -> 12.7 us
  blocking collectives: 21 us -> 19.8 us
    ppermute x1, starting transfers between devices: 2.38 us -> 4.19 us  [body(): above = lax.ppermute(three, ALL, along(-1))]
    ppermute x1, starting transfers between devices: 2.5 us -> 3.83 us  [body(): received = lax.ppermute(combined(1), ALL, SWAP)]
    all_to_all x1, blocking collectives: 21 us -> 19.8 us  [body(): lax.all_to_all(parts, ALL, split_axis=0, concat_axis=0, axis_index_groups...]
    pallas_call x1, Pallas kernels: 8.03 us -> 9.22 us  [attend(): call(attend_kernel, bf16(BLOCKS, WIRE, HD), megabytes=20, flops=230000000...]
    ppermute x1, starting transfers between devices: 2.91 us -> 1.92 us  [body(): below = lax.ppermute(two, ALL, along(1))]
  transfers between devices with their start and end apart: 7 -> 7, of which waited for: 3 -> 2; matrix products, arithmetic and copies ran while one was open for 0% -> 0% of each run, Pallas kernels for 2% -> 2%
where the time goes in v11:
time: 80.7 us; the launch traced here: 80.3 us
  starting transfers between devices  35.3 us (44%)
  blocking collectives  19.8 us (25%)
  Pallas kernels  12.7 us (16%)
  waiting for transfers between devices  12.4 us (15%)
    all_to_all x1, blocking collectives, body(): lax.all_to_all(parts, ALL, split_axis=0, concat_axis=0, axis_index_groups...  19.8 us
    all_to_all x1, starting transfers between devices, body(): lax.all_to_all(q, ALL, split_axis=0, concat_axis=0, axis_index_groups=CRO...  12.8 us
    ppermute x1, waiting for transfers between devices, body(): below = lax.ppermute(two, ALL, along(1))  11.9 us
    pallas_call x1, Pallas kernels, attend(): call(attend_kernel, bf16(BLOCKS, WIRE, HD), megabytes=20, flops=230000000...  9.22 us
    ppermute x1, starting transfers between devices, body(): q_received = lax.ppermute(q_sent, ALL, SWAP)  8.79 us
    ppermute x1, starting transfers between devices, body(): above = lax.ppermute(three, ALL, along(-1))  4.19 us
    ppermute x1, starting transfers between devices, body(): received = lax.ppermute(combined(1), ALL, SWAP)  3.83 us
    ppermute x1, starting transfers between devices, body(): lower = lax.ppermute(kv, ALL, along(-3))  1.92 us
  transfers between devices with their start and end apart: 7, of which 2 were waited for; matrix products, arithmetic and copies ran while one was open for 0% of the time, Pallas kernels for 2%

profile of v11, /device:TPU:1, one launch (start us, length us, event | category | flops | bytes accessed | tf_op | source)
XLA Modules:
  0.0 80.3 jit_solution(8902599447412083657)
XLA Ops:
  0.0 1.0 %shard_map.73 = (bf16[2,416,128]{2,1,0:T(8,128)(2,1)S(1)}, bf16[2,4,16,128]{3,2,1,0:T(8,128)(2,1)S(1)}, bf16[2,4,16,128]{3,2,1,0:T(8,128)(2,1)S(1)}, bf16[8,128]{1,0:T(8,128)(2,1)S(1)}) custom-call(s32[16]{0:T(128)} %positions.1, bf16[2,4,2,16,128]{4,3,2,1,0:T(8,128)(2,1)} %bitcast.7, bf16[384,128]{1,0:T(8,128)(2,1)} %bitcast.5, bf16[384,128]{1,0:T(8,128)(2,1)} %bitcast.6, ...), custom_call_target="tpu_custom_call" | custom-call | flops 1000000 | bytes 800000 | tf_op jit(solution)/shard_map/pallas_call | solution.py:284
  1.0 8.8 %collective-permute-start.4 = (bf16[2,4,16,128]{3,2,1,0:T(8,128)(2,1)S(1)}, bf16[2,4,16,128]{3,2,1,0:T(8,128)(2,1)S(1)}, u32[]{:S(2)}, u32[]{:S(2)}) collective-permute-start(bf16[2,4,16,128]{3,2,1,0:T(8,128)(2,1)S(1)} %get-tuple-element.15), channel_id=1, source_target_pairs={{0,1},{1,0},{2,3},{3,2},{4,5},{5,4},{6,7},{7,6},{8,9},{9,8},{10,11... | collective-permute-start | bytes 98312 | tf_op jit(solution)/shard_map/ppermute | solution.py:290
  9.8 1.9 %collective-permute-start = (bf16[2,416,128]{2,1,0:T(8,128)(2,1)S(1)}, bf16[2,416,128]{2,1,0:T(8,128)(2,1)S(1)}, u32[]{:S(2)}, u32[]{:S(2)}) collective-permute-start(bf16[2,416,128]{2,1,0:T(8,128)(2,1)S(1)} %get-tuple-element.11.own), channel_id=1, source_target_pairs={{0,320},{1,41},{2,322},{3,43},{4,324},{5,45},{6,326},{7,47},{8,328... | collective-permute-start | bytes 638984 | tf_op jit(solution)/shard_map/ppermute | solution.py:291
  11.7 1.9 %collective-permute-start.1 = (bf16[2,416,128]{2,1,0:T(8,128)(2,1)S(1)}, bf16[2,416,128]{2,1,0:T(8,128)(2,1)S(1)}, u32[]{:S(2)}, u32[]{:S(2)}) collective-permute-start(bf16[2,416,128]{2,1,0:T(8,128)(2,1)S(1)} %get-tuple-element.11.own), channel_id=1, source_target_pairs={{0,128},{1,17},{2,130},{3,19},{4,132},{5,21},{6,134},{7,23},{8,136... | collective-permute-start | bytes 638984 | tf_op jit(solution)/shard_map/ppermute | solution.py:292
  13.7 0.0 collective-permute-done.4.received
  13.7 0.9 %shard_map.75 = bf16[32,72,128]{2,1,0:T(8,128)(2,1)} custom-call(bf16[2,4,16,128]{3,2,1,0:T(8,128)(2,1)S(1)} %get-tuple-element.14.kept, bf16[2,4,16,128]{3,2,1,0:T(8,128)(2,1)S(1)} %collective-permute-done.4.received, bf16[8,128]{1,0:T(8,128)(2,1)S(1)} %get-tuple-element.16.tags), custom_call_target="tpu_custom_call" | custom-call | flops 10000000000 | bytes 800000 | tf_op jit(solution)/shard_map/pallas_call | solution.py:293
  14.6 12.8 %all-to-all-start = ((bf16[32,72,128]{2,1,0:T(8,128)(2,1)}), bf16[32,72,128]{2,1,0:T(8,128)(2,1)S(1)}, u32[]{:S(2)}, u32[]{:S(2)}) async-start(bf16[32,72,128]{2,1,0:T(8,128)(2,1)} %shard_map.75), calls=%async_computation | async-start | bytes 1179648 | tf_op jit(solution)/shard_map/all_to_all | solution.py:300
  27.4 0.0 collective-permute-done.lower
  27.4 0.0 collective-permute-done.1.upper
  27.4 0.1 shard_map.74
  27.5 0.0 copy-start
  27.5 4.2 %collective-permute-start.2 = (bf16[3,2,416,128]{3,2,1,0:T(8,128)(2,1)S(1)}, bf16[3,2,416,128]{3,2,1,0:T(8,128)(2,1)S(1)}, u32[]{:S(2)}, u32[]{:S(2)}) collective-permute-start(bf16[3,2,416,128]{3,2,1,0:T(8,128)(2,1)S(1)} %get-tuple-element.12), channel_id=1, source_target_pairs={{0,448},{1,57},{2,450},{3,59},{4,452},{5,61},{6,454},{7,63},{8,456... | collective-permute-start | bytes 1916936 | tf_op jit(solution)/shard_map/ppermute | solution.py:302
  31.7 1.9 %collective-permute-start.3 = (bf16[2,2,416,128]{3,2,1,0:T(8,128)(2,1)S(1)}, bf16[2,2,416,128]{3,2,1,0:T(8,128)(2,1)S(1)}, u32[]{:S(2)}, u32[]{:S(2)}) collective-permute-start(bf16[2,2,416,128]{3,2,1,0:T(8,128)(2,1)S(1)} %get-tuple-element.13), channel_id=1, source_target_pairs={{0,64},{1,9},{2,66},{3,11},{4,68},{5,13},{6,70},{7,15},{8,72},{9,1... | collective-permute-start | bytes 1277960 | tf_op jit(solution)/shard_map/ppermute | solution.py:303
  33.7 11.9 %collective-permute-done.3.below = bf16[2,2,416,128]{3,2,1,0:T(8,128)(2,1)S(1)} collective-permute-done((bf16[2,2,416,128]{3,2,1,0:T(8,128)(2,1)S(1)}, bf16[2,2,416,128]{3,2,1,0:T(8,128)(2,1)S(1)}, u32[]{:S(2)}, u32[]{:S(2)}) %collective-permute-start.3) | collective-permute-done | bytes 426016 | tf_op jit(solution)/shard_map/ppermute | solution.py:303
  45.6 0.0 collective-permute-done.2.above
  45.6 0.0 all-to-all-done.q
  45.6 0.0 copy-done
  45.6 9.2 %shard_map.76 = bf16[32,72,128]{2,1,0:T(8,128)(2,1)S(1)} custom-call(s32[128]{0:T(128)S(1)} %copy-done, bf16[2,416,128]{2,1,0:T(8,128)(2,1)S(1)} %get-tuple-element.11.own, bf16[2,416,128]{2,1,0:T(8,128)(2,1)S(1)} %collective-permute-done.lower, bf16[2,416,128]{2,1,0:T(8,128)(2,1)S(1)} %collective-permute-done.1.upper, ...), custom_call_target="tpu_custom_call" | custom-call | flops 2300000000 | bytes 5000000 | tf_op jit(solution)/shard_map/pallas_call | solution.py:229
  54.8 19.8 %all_to_all.10.parts = bf16[32,72,128]{2,1,0:T(8,128)(2,1)S(1)} all-to-all(bf16[32,72,128]{2,1,0:T(8,128)(2,1)S(1)} %shard_map.76), channel_id=1, replica_groups={{0,2,4,6,8,10,12,14,16,18,20,22,24,26,28,30,32,34,36,38,40,42,44,46,48,..., dimensions={0} | all-to-all | bytes 1179648 | tf_op jit(solution)/shard_map/all_to_all | solution.py:305
  74.6 0.4 shard_map.78
  75.0 3.8 %collective-permute-start.5 = (bf16[2,4,16,128]{3,2,1,0:T(8,128)(2,1)S(1)}, bf16[2,4,16,128]{3,2,1,0:T(8,128)(2,1)S(1)}, u32[]{:S(2)}, u32[]{:S(2)}) collective-permute-start(bf16[2,4,16,128]{3,2,1,0:T(8,128)(2,1)S(1)} %shard_map.78), channel_id=1, source_target_pairs={{0,1},{1,0},{2,3},{3,2},{4,5},{5,4},{6,7},{7,6},{8,9},{9,8},{10,11... | collective-permute-start | bytes 98312 | tf_op jit(solution)/shard_map/ppermute | solution.py:314
  78.8 0.4 shard_map.77.kept
  79.2 0.4 collective-permute-done.5.received
  79.6 0.6 shard_map.79
Async XLA Ops:
  1.0 12.7 %collective-permute-start.4 = (bf16[2,4,16,128]{3,2,1,0:T(8,128)(2,1)S(1)}, bf16[2,4,16,128]{3,2,1,0:T(8,128)(2,1)S(1)}, u32[]{:S(2)}, u32[]{:S(2)}) collective-permute-start(bf16[2,4,16,128]{3,2,1,0:T(8,128)(2,1)S(1)} %get-tuple-element.15), channel_id=1, source_target_pairs={{0,1},{1,0},{2,3},{3,2},{4,5},{5,4},{6,7},{7,6},{8,9},{9,8},{10,11... | collective-permute-start | bytes 98312 | tf_op jit(solution)/shard_map/ppermute | solution.py:290
  9.8 17.6 %collective-permute-start = (bf16[2,416,128]{2,1,0:T(8,128)(2,1)S(1)}, bf16[2,416,128]{2,1,0:T(8,128)(2,1)S(1)}, u32[]{:S(2)}, u32[]{:S(2)}) collective-permute-start(bf16[2,416,128]{2,1,0:T(8,128)(2,1)S(1)} %get-tuple-element.11.own), channel_id=1, source_target_pairs={{0,320},{1,41},{2,322},{3,43},{4,324},{5,45},{6,326},{7,47},{8,328... | collective-permute-start | bytes 638984 | tf_op jit(solution)/shard_map/ppermute | solution.py:291
  11.7 15.6 %collective-permute-start.1 = (bf16[2,416,128]{2,1,0:T(8,128)(2,1)S(1)}, bf16[2,416,128]{2,1,0:T(8,128)(2,1)S(1)}, u32[]{:S(2)}, u32[]{:S(2)}) collective-permute-start(bf16[2,416,128]{2,1,0:T(8,128)(2,1)S(1)} %get-tuple-element.11.own), channel_id=1, source_target_pairs={{0,128},{1,17},{2,130},{3,19},{4,132},{5,21},{6,134},{7,23},{8,136... | collective-permute-start | bytes 638984 | tf_op jit(solution)/shard_map/ppermute | solution.py:292
  14.6 31.0 %all-to-all-start = ((bf16[32,72,128]{2,1,0:T(8,128)(2,1)}), bf16[32,72,128]{2,1,0:T(8,128)(2,1)S(1)}, u32[]{:S(2)}, u32[]{:S(2)}) async-start(bf16[32,72,128]{2,1,0:T(8,128)(2,1)} %shard_map.75), calls=%async_computation | async-start | bytes 1179648 | tf_op jit(solution)/shard_map/all_to_all | solution.py:300
  27.5 18.1 %copy-start = (s32[128]{0:T(128)S(1)}, s32[128]{0:T(128)}, u32[]{:S(2)}) copy-start(s32[128]{0:T(128)} %page_slots.1) | copy-start | bytes 1540
  27.5 18.0 %collective-permute-start.2 = (bf16[3,2,416,128]{3,2,1,0:T(8,128)(2,1)S(1)}, bf16[3,2,416,128]{3,2,1,0:T(8,128)(2,1)S(1)}, u32[]{:S(2)}, u32[]{:S(2)}) collective-permute-start(bf16[3,2,416,128]{3,2,1,0:T(8,128)(2,1)S(1)} %get-tuple-element.12), channel_id=1, source_target_pairs={{0,448},{1,57},{2,450},{3,59},{4,452},{5,61},{6,454},{7,63},{8,456... | collective-permute-start | bytes 1916936 | tf_op jit(solution)/shard_map/ppermute | solution.py:302
  31.7 13.8 %collective-permute-start.3 = (bf16[2,2,416,128]{3,2,1,0:T(8,128)(2,1)S(1)}, bf16[2,2,416,128]{3,2,1,0:T(8,128)(2,1)S(1)}, u32[]{:S(2)}, u32[]{:S(2)}) collective-permute-start(bf16[2,2,416,128]{3,2,1,0:T(8,128)(2,1)S(1)} %get-tuple-element.13), channel_id=1, source_target_pairs={{0,64},{1,9},{2,66},{3,11},{4,68},{5,13},{6,70},{7,15},{8,72},{9,1... | collective-permute-start | bytes 1277960 | tf_op jit(solution)/shard_map/ppermute | solution.py:303
  75.0 4.7 %collective-permute-start.5 = (bf16[2,4,16,128]{3,2,1,0:T(8,128)(2,1)S(1)}, bf16[2,4,16,128]{3,2,1,0:T(8,128)(2,1)S(1)}, u32[]{:S(2)}, u32[]{:S(2)}) collective-permute-start(bf16[2,4,16,128]{3,2,1,0:T(8,128)(2,1)S(1)} %shard_map.78), channel_id=1, source_target_pairs={{0,1},{1,0},{2,3},{3,2},{4,5},{5,4},{6,7},{7,6},{8,9},{9,8},{10,11... | collective-permute-start | bytes 98312 | tf_op jit(solution)/shard_map/ppermute | solution.py:314
